TPU v7x, 256 devices: a whole 4x4x8 slice. The times are simulated.
256 devices in a mesh: block: 32 (over x_lo, z, core), lane: 8 (over x_hi, y).
Axes of the slice: x: 4 (x_hi: 2, x_lo: 2; x = x_hi * 2 + x_lo), y: 4, z: 8, core: 2. Of those that a mesh axis runs over, the one named last changes fastest.
Arguments:
- images: float32 [16384, 1152], P('block'), may hold values from -1.253025 to 1.253025
- texts: float32 [16384, 1152], P('block'), may hold values from -1.253025 to 1.253025
- labels: int32 [16384], P('block'), may hold values from 0 to 16383, each once
Outputs:
- image_grad: float32 [16384, 1152], P(('block', 'lane'))
- text_grad: float32 [16384, 1152], P(('block', 'lane'))
Inputs may be any that keep to these rules, and one draw needn't show every extreme that they name: `labels`: each text row is the partner of exactly one image row.
All inputs are finite; a program needn't handle non-finite values.
Results may differ from a plain program's by a relative error of at most 0.004.
Values may be sent and summed in bfloat16 or wider, within the bound.
No kernel may reach another device: no remote copies, remote signals or barrier semaphores. Data moves between devices by JAX's collectives and lax.ppermute only.
A program may use at most 64 MiB of HBM per device.

v0:
```python
import jax
import jax.numpy as jnp
from jax import lax
from jax.sharding import PartitionSpec as P

logit_bias = -6.0


def partner_2(value, axis, distance):
    return lax.ppermute(value, axis, [(i, i ^ 1 << distance) for i in range(lax.axis_size(axis))])


def next_text(travel, flip):
    return partner_2(travel, "block", flip)


def on_device(images, texts, labels):
    rows = images.shape[0]
    lanes = lax.axis_size("lane")
    blocks = lax.axis_size("block")
    block_id = lax.axis_index("block")
    lane_id = lax.axis_index("lane")
    image_low = images.astype(jnp.bfloat16)
    share = rows // lanes
    meet = blocks // lanes
    meet_bits = meet.bit_length() - 1
    lane_bits = lanes.bit_length() - 1
    offset = lane_id * meet
    travel = texts.astype(jnp.bfloat16)
    for bit_pos in range(lane_bits):
        swapped = partner_2(travel, "block", meet_bits + bit_pos)
        travel = jnp.where(lane_id >> bit_pos & 1 == 1, swapped, travel)
    columns = lax.broadcasted_iota(jnp.int32, (rows, rows), 1)

    def meeting(text_now, gray):
        partner = jnp.bitwise_xor(jnp.bitwise_xor(block_id, offset), gray)
        logits = (
            lax.dot_general(
                image_low, text_now, (((1,), (1,)), ((), ())), preferred_element_type=jnp.float32
            )
            + logit_bias
        )
        positive = (labels[:, None] == partner * rows + columns).astype(jnp.float32)
        weights = (jax.nn.sigmoid(logits) - positive).astype(jnp.bfloat16)
        image_term = jnp.dot(weights, text_now, preferred_element_type=jnp.float32)
        text_term = lax.dot_general(
            weights, image_low, (((0,), (0,)), ((), ())), preferred_element_type=jnp.float32
        )
        return (image_term, text_term)

    image_grad, own_term = meeting(travel, 0)
    text_grad = own_term
    for step in range(1, meet):
        flip = (step & -step).bit_length() - 1
        travel = next_text(travel, flip)
        gray = step ^ step >> 1
        image_term, text_term = meeting(travel, gray)
        image_grad = image_grad + image_term
        for bit_pos in range(meet_bits):
            if gray >> bit_pos & 1:
                text_term = partner_2(text_term, "block", bit_pos)
        text_grad = text_grad + text_term
    for bit_pos in range(lane_bits):
        swapped = partner_2(text_grad, "block", meet_bits + bit_pos)
        text_grad = jnp.where(lane_id >> bit_pos & 1 == 1, swapped, text_grad)
    image_total, text_total = lax.psum((image_grad, text_grad), "lane")
    start = lane_id * share
    image_out = lax.dynamic_slice_in_dim(image_total, start, share, 0)
    text_out = lax.dynamic_slice_in_dim(text_total, start, share, 0)
    return (image_out, text_out)


def solution(mesh):
    placed = (P("block", None), P("block", None), P("block"))
    return jax.shard_map(
        on_device,
        mesh=mesh,
        in_specs=placed,
        out_specs=(P(("block", "lane"), None), P(("block", "lane"), None)),
        check_vma=False,
    )
```

profile of v0, /device:TPU:1, one launch (start us, length us, event | category | flops | bytes accessed | tf_op | source)
XLA Modules:
  0.0 701.5 jit_solution(12617722248484060694)
XLA Ops:
  9.2 3.9 collective-permute-start
  13.1 50.4 %collective-permute-done = bf16[512,1152]{1,0:T(8,128)(2,1)} collective-permute-done((bf16[512,1152]{1,0:T(8,128)(2,1)S(1)}, bf16[512,1152]{1,0:T(8,128)(2,1)}, u32[]{:S(2)}, u32[]{:S(2)}) %collective-permute-start) | collective-permute-done | bytes 1179680 | tf_op jit(solution)/shard_map/ppermute | solution.py:10
  63.7 7.3 %collective-permute-start.1 = (bf16[512,1152]{1,0:T(8,128)(2,1)S(1)}, bf16[512,1152]{1,0:T(8,128)(2,1)S(1)}, u32[]{:S(2)}, u32[]{:S(2)}) collective-permute-start(bf16[512,1152]{1,0:T(8,128)(2,1)S(1)} %broadcast_select_fusion.1), channel_id=1, source_target_pairs={{0,64},{8,72},{16,80},{24,88},{32,96},{40,104},{48,112},{56,120},{... | collective-permute-start | bytes 3538952 | tf_op jit(solution)/shard_map/ppermute | solution.py:10
  71.0 51.0 %collective-permute-done.1 = bf16[512,1152]{1,0:T(8,128)(2,1)S(1)} collective-permute-done((bf16[512,1152]{1,0:T(8,128)(2,1)S(1)}, bf16[512,1152]{1,0:T(8,128)(2,1)S(1)}, u32[]{:S(2)}, u32[]{:S(2)}) %collective-permute-start.1) | collective-permute-done | bytes 1179680 | tf_op jit(solution)/shard_map/ppermute | solution.py:10
  123.4 24.6 %collective-permute-done.2 = bf16[512,1152]{1,0:T(8,128)(2,1)S(1)} collective-permute-done((bf16[512,1152]{1,0:T(8,128)(2,1)S(1)}, bf16[512,1152]{1,0:T(8,128)(2,1)S(1)}, u32[]{:S(2)}, u32[]{:S(2)}) %collective-permute-start.2) | collective-permute-done | bytes 1179680 | tf_op jit(solution)/shard_map/ppermute | solution.py:10
  148.2 2.6 collective-permute-start.3
  150.8 2.5 collective-permute-done.3
  154.3 26.3 %collective-permute-done.4 = bf16[512,1152]{1,0:T(8,128)(2,1)} collective-permute-done((bf16[512,1152]{1,0:T(8,128)(2,1)S(1)}, bf16[512,1152]{1,0:T(8,128)(2,1)}, u32[]{:S(2)}, u32[]{:S(2)}) %collective-permute-start.4) | collective-permute-done | bytes 1179680 | tf_op jit(solution)/shard_map/ppermute | solution.py:10
  180.6 2.3 fusion.27
  185.1 2.3 fusion.28
  187.4 2.3 fusion.31
  191.1 2.3 fusion.26
  193.4 2.2 fusion.33
  197.1 2.3 fusion.29
  199.4 49.2 %collective-permute-done.9 = f32[512,1152]{1,0:T(8,128)} collective-permute-done((f32[512,1152]{1,0:T(8,128)}, f32[512,1152]{1,0:T(8,128)}, u32[]{:S(2)}, u32[]{:S(2)}) %collective-permute-start.9) | collective-permute-done | bytes 2359328 | tf_op jit(solution)/shard_map/ppermute | solution.py:10
  248.7 50.5 %collective-permute-done.8 = f32[512,1152]{1,0:T(8,128)S(1)} collective-permute-done((f32[512,1152]{1,0:T(8,128)}, f32[512,1152]{1,0:T(8,128)S(1)}, u32[]{:S(2)}, u32[]{:S(2)}) %collective-permute-start.8) | collective-permute-done | bytes 2359328 | tf_op jit(solution)/shard_map/ppermute | solution.py:10
  299.1 3.3 fusion.1
  304.4 102.4 %collective-permute-done.10 = f32[512,1152]{1,0:T(8,128)S(1)} collective-permute-done((f32[512,1152]{1,0:T(8,128)S(1)}, f32[512,1152]{1,0:T(8,128)S(1)}, u32[]{:S(2)}, u32[]{:S(2)}) %collective-permute-start.10) | collective-permute-done | bytes 2359328 | tf_op jit(solution)/shard_map/ppermute | solution.py:10
  407.1 2.1 collective-permute-start.11
  409.2 104.5 %collective-permute-done.11 = f32[512,1152]{1,0:T(8,128)S(1)} collective-permute-done((f32[512,1152]{1,0:T(8,128)S(1)}, f32[512,1152]{1,0:T(8,128)S(1)}, u32[]{:S(2)}, u32[]{:S(2)}) %collective-permute-start.11) | collective-permute-done | bytes 2359328 | tf_op jit(solution)/shard_map/ppermute | solution.py:10
  517.2 2.2 convolution_add_fusion.2
  519.4 3.6 convolution_add_fusion.1
  523.0 43.3 %collective-permute-done.12 = f32[512,1152]{1,0:T(8,128)S(1)} collective-permute-done((f32[512,1152]{1,0:T(8,128)S(1)}, f32[512,1152]{1,0:T(8,128)S(1)}, u32[]{:S(2)}, u32[]{:S(2)}) %collective-permute-start.12) | collective-permute-done | bytes 2359328 | tf_op jit(solution)/shard_map/ppermute | solution.py:10
  568.1 124.6 %all-reduce.3.cloned.1.call-done = (f32[512,1152]{1,0:T(8,128)}, f32[512,1152]{1,0:T(8,128)}) async-done(((f32[512,1152]{1,0:T(8,128)}, f32[512,1152]{1,0:T(8,128)}), (f32[512,1152]{1,0:T(8,128)}, f32[512,1152]{1,0:T(8,128)})) %all-reduce.3.cloned.1.call-update) | async-done | bytes 4718608 | tf_op jit(solution)/shard_map/psum | solution.py:66
  (56 shorter events, 19.0 us)
Async XLA Ops:
  7.2 56.3 %copy-start = (f32[512,1152]{1,0:T(8,128)S(1)}, f32[512,1152]{1,0:T(8,128)}, u32[]{:S(2)}) copy-start(f32[512,1152]{1,0:T(8,128)} %param.4) | copy-start | bytes 7077892
  7.2 685.6 %all-reduce.3.cloned.1.call-start = ((), (), s32[]{:S(2)}) async-start(), calls=%async_computation | async-start | bytes 9437184 | tf_op jit(solution)/shard_map/psum | solution.py:66
  9.2 54.3 %collective-permute-start = (bf16[512,1152]{1,0:T(8,128)(2,1)S(1)}, bf16[512,1152]{1,0:T(8,128)(2,1)}, u32[]{:S(2)}, u32[]{:S(2)}) collective-permute-start(bf16[512,1152]{1,0:T(8,128)(2,1)S(1)} %convert_element_type.30), channel_id=1, source_target_pairs={{0,32},{8,40},{16,48},{24,56},{32,0},{40,8},{48,16},{56,24},{64,96... | collective-permute-start | bytes 3538952 | tf_op jit(solution)/shard_map/ppermute | solution.py:10
  63.7 58.3 %collective-permute-start.1 = (bf16[512,1152]{1,0:T(8,128)(2,1)S(1)}, bf16[512,1152]{1,0:T(8,128)(2,1)S(1)}, u32[]{:S(2)}, u32[]{:S(2)}) collective-permute-start(bf16[512,1152]{1,0:T(8,128)(2,1)S(1)} %broadcast_select_fusion.1), channel_id=1, source_target_pairs={{0,64},{8,72},{16,80},{24,88},{32,96},{40,104},{48,112},{56,120},{... | collective-permute-start | bytes 3538952 | tf_op jit(solution)/shard_map/ppermute | solution.py:10
  122.1 25.9 %collective-permute-start.2 = (bf16[512,1152]{1,0:T(8,128)(2,1)S(1)}, bf16[512,1152]{1,0:T(8,128)(2,1)S(1)}, u32[]{:S(2)}, u32[]{:S(2)}) collective-permute-start(bf16[512,1152]{1,0:T(8,128)(2,1)S(1)} %broadcast_select_fusion.3), channel_id=1, source_target_pairs={{0,128},{8,136},{16,144},{24,152},{32,160},{40,168},{48,176},{56,1... | collective-permute-start | bytes 3538952 | tf_op jit(solution)/shard_map/ppermute | solution.py:10
  123.4 29.9 %copy-start.9 = (f32[512,1152]{1,0:T(8,128)S(1)}, f32[512,1152]{1,0:T(8,128)}, u32[]{:S(2)}) copy-start(f32[512,1152]{1,0:T(8,128)} %param.3) | copy-start | bytes 7077892
  148.2 5.1 copy-start.1
  148.2 32.4 %copy-start.12 = (s32[512]{0:T(512)S(1)}, s32[512]{0:T(512)}, u32[]{:S(2)}) copy-start(s32[512]{0:T(512)} %param.5) | copy-start | bytes 6148
  148.2 5.1 collective-permute-start.3
  153.3 27.3 %collective-permute-start.4 = (bf16[512,1152]{1,0:T(8,128)(2,1)S(1)}, bf16[512,1152]{1,0:T(8,128)(2,1)}, u32[]{:S(2)}, u32[]{:S(2)}) collective-permute-start(bf16[512,1152]{1,0:T(8,128)(2,1)S(1)} %collective-permute-done.3), channel_id=1, source_target_pairs={{0,16},{8,24},{16,0},{24,8},{32,48},{40,56},{48,32},{56,40},{64,80... | collective-permute-start | bytes 3538952 | tf_op jit(solution)/shard_map/ppermute | solution.py:10
  183.7 11.9 %collective-permute-start.7 = (f32[512,1152]{1,0:T(8,128)S(1)}, f32[512,1152]{1,0:T(8,128)}, u32[]{:S(2)}, u32[]{:S(2)}) collective-permute-start(f32[512,1152]{1,0:T(8,128)S(1)} %fusion.32), channel_id=1, source_target_pairs={{0,8},{8,0},{16,24},{24,16},{32,40},{40,32},{48,56},{56,48},{64,72... | collective-permute-start | bytes 7077896 | tf_op jit(solution)/shard_map/ppermute | solution.py:10
  185.0 6.1 collective-permute-start.5
  187.4 2.4 copy-start.3
  189.8 9.6 %collective-permute-start.6 = (f32[512,1152]{1,0:T(8,128)}, f32[512,1152]{1,0:T(8,128)}, u32[]{:S(2)}, u32[]{:S(2)}) collective-permute-start(f32[512,1152]{1,0:T(8,128)} %fusion.31), channel_id=1, source_target_pairs={{0,8},{8,0},{16,24},{24,16},{32,40},{40,32},{48,56},{56,48},{64,72... | collective-permute-start | bytes 7077896 | tf_op jit(solution)/shard_map/ppermute | solution.py:10
  193.4 2.3 copy-start.7
  195.7 53.0 %collective-permute-start.9 = (f32[512,1152]{1,0:T(8,128)}, f32[512,1152]{1,0:T(8,128)}, u32[]{:S(2)}, u32[]{:S(2)}) collective-permute-start(f32[512,1152]{1,0:T(8,128)} %fusion.33), channel_id=1, source_target_pairs={{0,16},{8,24},{16,0},{24,8},{32,48},{40,56},{48,32},{56,40},{64,80... | collective-permute-start | bytes 7077896 | tf_op jit(solution)/shard_map/ppermute | solution.py:10
  195.7 103.5 %collective-permute-start.8 = (f32[512,1152]{1,0:T(8,128)}, f32[512,1152]{1,0:T(8,128)S(1)}, u32[]{:S(2)}, u32[]{:S(2)}) collective-permute-start(f32[512,1152]{1,0:T(8,128)} %collective-permute-done.7), channel_id=1, source_target_pairs={{0,16},{8,24},{16,0},{24,8},{32,48},{40,56},{48,32},{56,40},{64,80... | collective-permute-start | bytes 7077896 | tf_op jit(solution)/shard_map/ppermute | solution.py:10
  302.5 104.4 %collective-permute-start.10 = (f32[512,1152]{1,0:T(8,128)S(1)}, f32[512,1152]{1,0:T(8,128)S(1)}, u32[]{:S(2)}, u32[]{:S(2)}) collective-permute-start(f32[512,1152]{1,0:T(8,128)S(1)} %fusion.1), channel_id=1, source_target_pairs={{0,32},{8,40},{16,48},{24,56},{32,0},{40,8},{48,16},{56,24},{64,96... | collective-permute-start | bytes 7077896 | tf_op jit(solution)/shard_map/ppermute | solution.py:10
  407.1 108.2 %copy-start.4 = (bf16[512,512]{0,1:T(8,128)(2,1)S(1)}, bf16[512,512]{0,1:T(8,128)(2,1)}, u32[]{:S(2)}) copy-start(bf16[512,512]{0,1:T(8,128)(2,1)} %copy-done.3) | copy-start | bytes 1572868
  407.1 108.2 %copy-start.11 = (bf16[512,1152]{1,0:T(8,128)(2,1)S(1)}, bf16[512,1152]{1,0:T(8,128)(2,1)}, u32[]{:S(2)}) copy-start(bf16[512,1152]{1,0:T(8,128)(2,1)} %copy-done.10) | copy-start | bytes 3538948
  407.1 106.6 %collective-permute-start.11 = (f32[512,1152]{1,0:T(8,128)S(1)}, f32[512,1152]{1,0:T(8,128)S(1)}, u32[]{:S(2)}, u32[]{:S(2)}) collective-permute-start(f32[512,1152]{1,0:T(8,128)S(1)} %broadcast_select_fusion), channel_id=1, source_target_pairs={{0,64},{8,72},{16,80},{24,88},{32,96},{40,104},{48,112},{56,120},{... | collective-permute-start | bytes 7077896 | tf_op jit(solution)/shard_map/ppermute | solution.py:10
  514.0 2.2 copy-start.2
  514.0 52.4 %collective-permute-start.12 = (f32[512,1152]{1,0:T(8,128)S(1)}, f32[512,1152]{1,0:T(8,128)S(1)}, u32[]{:S(2)}, u32[]{:S(2)}) collective-permute-start(f32[512,1152]{1,0:T(8,128)S(1)} %broadcast_select_fusion.2), channel_id=1, source_target_pairs={{0,128},{8,136},{16,144},{24,152},{32,160},{40,168},{48,176},{56,1... | collective-permute-start | bytes 7077896 | tf_op jit(solution)/shard_map/ppermute | solution.py:10
  517.2 2.2 copy-start.8
  (3 other events, 2.9 us)
Sparse Core Ops, SparseCore 0:
  568.3 124.4 all-reduce.2
where the time goes:
time: 702 us
  waiting for transfers between devices  630 us (90%)
  matrix products  25.5 us (4%)
  starting transfers between devices  23.7 us (3%)
  between operations  14.3 us (2%)
    ppermute x13, waiting for transfers between devices, partner_2(): lax.ppermute(value, axis, [(i, i ^ 1 << distance) for i in range(lax.axis...  506 us
    psum x1, waiting for transfers between devices, on_device(): image_total, text_total = lax.psum((image_grad, text_grad), 'lane')  125 us
    ppermute x13, starting transfers between devices, partner_2(): lax.ppermute(value, axis, [(i, i ^ 1 << distance) for i in range(lax.axis...  23.7 us
  transfers between devices with their start and end apart: 14, of which 12 were waited for; matrix products, arithmetic and copies ran while one was open for 3% of the time, Pallas kernels for 0%

commit v1 on v0

v1 whole, which is shorter than its diff:
```python
import functools

import jax
import jax.numpy as jnp
from jax import lax
from jax.experimental import pallas as pl
from jax.experimental.pallas import tpu as pltpu
from jax.sharding import PartitionSpec as P

logit_bias = -6.0
Z, C, X, Y = 8, 2, 4, 4
AXES = ("block", "lane")
ROWS = 512
SHARE = 64
low = jnp.bfloat16
f32 = jnp.float32
MIB = 1 << 20
VMEM = pl.BlockSpec(memory_space=pltpu.VMEM)
ANY = pl.BlockSpec(memory_space=pl.ANY)


def flat(x, y, z, c):
    return (((x % 2) * Z + z) * C + c) * (X // 2 * Y) + (x // 2) * Y + y


def send(value, step):
    pairs = []
    for x in range(X):
        for y in range(Y):
            for z in range(Z):
                for c in range(C):
                    dx, dy, dz, dc = step(c)
                    to = flat((x + dx) % X, (y + dy) % Y, (z + dz) % Z, (c + dc) % C)
                    pairs.append((flat(x, y, z, c), to))
    return lax.ppermute(value, AXES, pairs)


def to_core(value):
    return send(value, lambda c: (0, 0, 0, 1))


def to_x(value, d):
    return send(value, lambda c: (d, 0, 0, 0))


def to_z(value, d):
    return send(value, lambda c: (0, 0, -d if c else d, 0))


def first_stage(value, d):
    return send(value, lambda c: (0, d, 0, 0) if c else (d, 0, 0, 0))


def second_stage(value, d):
    return send(value, lambda c: (d, 0, 0, 0) if c else (0, d, 0, 0))


def place():
    block = lax.axis_index("block")
    lane = lax.axis_index("lane")
    return block // 16, block // 2 % 8, block % 2, lane // 4, lane % 4


def prep_kernel(far, where_ref, images_ref, texts_ref, labels_ref, *refs):
    refs = list(refs)
    text_out = None if far else refs.pop(0)
    image_out, held, text_held, sems = refs
    xh, y = where_ref[3], where_ref[4]
    if not far:
        start = pl.multiple_of((xh * Y + y) * SHARE, SHARE)
        text_copy = pltpu.make_async_copy(texts_ref.at[pl.ds(start, SHARE)], text_held, sems.at[4])
        text_copy.start()
    half = 1 - xh if far else xh
    copies = []
    for i in range(Y):
        row = pl.multiple_of((half * Y + lax.rem(y + i, Y)) * SHARE, SHARE)
        copy = pltpu.make_async_copy(images_ref.at[pl.ds(row, SHARE)], held.at[i], sems.at[i])
        copy.start()
        copies.append(copy)
    labels = jnp.concatenate([labels_ref[pl.ds(2 * half, 1), :], labels_ref[pl.ds(2 * half + 1, 1), :]], axis=1)
    labels = jnp.broadcast_to(labels, (16, 256))
    labels = pltpu.roll(labels, lax.rem(Y - y, Y) * SHARE, 1)
    row = lax.broadcasted_iota(jnp.int32, (16, 256), 0)
    digits = jnp.where(row == 0, labels >> 7, jnp.where(row == 1, labels & 127, 0))
    image_out[256:272, :256] = digits.astype(f32).astype(low)
    image_out[256:272, 256:] = jnp.zeros((16, image_out.shape[1] - 256), low)
    if not far:
        text_copy.wait()
        text_out[...] = text_held[...].astype(low)
    for i in range(Y):
        copies[i].wait()
        image_out[i * SHARE : (i + 1) * SHARE, :] = held[i].astype(low)


def prep(where, images, texts, labels, far):
    width = images.shape[1]
    outs = [] if far else [jax.ShapeDtypeStruct((SHARE, width), low)]
    outs.append(jax.ShapeDtypeStruct((272, width), low))
    return pl.pallas_call(
        functools.partial(prep_kernel, far),
        out_shape=tuple(outs),
        in_specs=[pl.BlockSpec(memory_space=pltpu.SMEM), ANY, ANY, VMEM],
        out_specs=(VMEM,) * len(outs),
        scratch_shapes=[
            pltpu.VMEM((Y, SHARE, width), f32),
            pltpu.VMEM((SHARE, width), f32),
            pltpu.SemaphoreType.DMA((5,)),
        ],
        compiler_params=pltpu.CompilerParams(vmem_limit_bytes=58 * MIB),
        cost_estimate=pl.CostEstimate(flops=0, bytes_accessed=3 << 20, transcendentals=0),
    )(where, images, texts, labels)


def tile_kernel(group, first, last, where_ref, *refs):
    refs = list(refs)
    if first:
        parts = [refs.pop(0) for _ in range(4)]
    else:
        images_ref = refs.pop(0)
        labels_ref = refs.pop(0)
        held = refs.pop(0)
    texts = [(refs.pop(0), refs.pop(0)) for _ in group]
    if first:
        images_ref = refs.pop(0)
        labels_ref = refs.pop(0)
    if last:
        image_outs = [refs.pop(0) for _ in range(4)]
    else:
        sums_ref = refs.pop(0)
    keep_ref = refs.pop(0)
    give_ref = refs.pop(0)
    text_ref, weight_ref = refs
    n = text_ref.shape[0]
    half = n // 2
    xl, z, c, xh, y = (where_ref[i] for i in range(5))
    if first:
        for a in range(4):
            images_ref[a * 256 : (a + 1) * 256, :] = parts[a][:256, :]
            digits = parts[a][256:272, :256].astype(f32)
            both = digits[0:1] * 128.0 + digits[1:2]
            labels_ref[:, a * 256 : (a + 1) * 256] = jnp.broadcast_to(both, (8, 256))
    numbers = [[], []]
    at = 0
    sign = 1 - 2 * c
    for d, pair in zip(group, texts):
        rows = pair[0].shape[0]
        for side in range(2):
            offset = at + side * half
            text_ref[offset : offset + rows, :] = pair[side][...]
            if d in (0, 4):
                cores = (c,) if side == 0 else (1 - c,)
                chip = lax.rem(z + d, Z)
            else:
                cores = (c, 1 - c) if side == 0 else (1 - c, c)
                chip = lax.rem(z + Z + sign * (d if side == 0 else -d), Z)
            for core in cores:
                start = ((xl * Z + chip) * C + core) * ROWS + (xh * Y + y) * SHARE
                numbers[side].append(lax.broadcasted_iota(jnp.int32, (SHARE, 1), 0) + start)
        at += rows
    numbers = jnp.concatenate(numbers[0] + numbers[1], axis=0).astype(f32)
    text = text_ref[...]
    for a in range(4):
        cut = slice(a * 256, (a + 1) * 256)
        logits = (
            lax.dot_general(text, images_ref[cut, :], (((1,), (1,)), ((), ())), preferred_element_type=f32)
            + logit_bias
        )
        positive = (labels_ref[0:1, cut] == numbers).astype(f32)
        weight_ref[:, cut] = (jax.nn.sigmoid(logits) - positive).astype(low)
    text_term = jnp.dot(weight_ref[...], images_ref[...], preferred_element_type=f32)
    keep_ref[...] = text_term[:half]
    give_ref[...] = text_term[half:].astype(low)
    total = lax.dot_general(weight_ref[...], text, (((0,), (0,)), ((), ())), preferred_element_type=f32)
    if not first:
        total = total + held[...]
    if last:
        total = total.astype(low)

        @pl.when(c == 0)
        def _():
            for a in range(4):
                image_outs[a][...] = total[a * 256 : (a + 1) * 256]

        @pl.when(c == 1)
        def _():
            for a in range(4):
                for b in range(4):
                    start = a * 256 + b * SHARE
                    image_outs[b][a * SHARE : (a + 1) * SHARE, :] = total[start : start + SHARE]
    else:
        sums_ref[...] = total


def tile(where, state, group, texts, last):
    first = len(state) == 4
    width = state[0].shape[1]
    half = sum(pair[0].shape[0] for pair in texts)
    n = 2 * half
    outs = []
    if first:
        outs.append(jax.ShapeDtypeStruct((1024, width), low))
        outs.append(jax.ShapeDtypeStruct((8, 1024), f32))
    if last:
        outs += [jax.ShapeDtypeStruct((256, width), low)] * 4
    else:
        outs.append(jax.ShapeDtypeStruct((1024, width), f32))
    outs += [jax.ShapeDtypeStruct((half, width), f32), jax.ShapeDtypeStruct((half, width), low)]
    args = [where, *state]
    for pair in texts:
        args += pair
    results = pl.pallas_call(
        functools.partial(tile_kernel, group, first, last),
        out_shape=tuple(outs),
        in_specs=[pl.BlockSpec(memory_space=pltpu.SMEM)] + [VMEM] * (len(args) - 1),
        out_specs=(VMEM,) * len(outs),
        scratch_shapes=[pltpu.VMEM((n, width), low), pltpu.VMEM((n, 1024), low)],
        compiler_params=pltpu.CompilerParams(vmem_limit_bytes=28 * MIB),
        cost_estimate=pl.CostEstimate(
            flops=6 * 1024 * n * width, bytes_accessed=4 << 20, transcendentals=1024 * n
        ),
    )(*args)
    keep, give = results[-2:]
    if first:
        state = results[:3]
    elif last:
        state = results[:4]
    else:
        state = (state[0], state[1], results[0])
    return state, keep, give


def on_device(images, texts, labels):
    where = jnp.stack(place()).astype(jnp.int32)
    label_rows = labels.reshape(4, 128)
    text_own, image_near = prep(where, images, texts, label_rows, False)
    text_other = to_core(text_own)
    image_right = to_x(image_near, -1)
    image_left = to_x(image_near, 1)
    chunk = jnp.concatenate([text_own, text_other], axis=0)
    arrived = {}
    for d in (3, 2, 1):
        arrived[d] = to_z(chunk, -d)
    arrived[4] = to_z(text_own, 4)
    (image_far,) = prep(where, images, texts, label_rows, True)
    state = (image_near, image_right, image_far, image_left)

    groups = ((0, 1), (2,), (3, 4))
    parts = {}
    for i, group in enumerate(groups):
        pairs = [(text_own, text_other) if d == 0 else (arrived[d], to_core(arrived[d])) for d in group]
        state, keep, give = tile(where, state, group, pairs, i == len(groups) - 1)
        at = 0
        if group[0] == 0:
            own_keep, own_give = keep[:SHARE], give[:SHARE]
            keep, give = keep[SHARE:], give[SHARE:]
            group = group[1:]
        both = (keep + to_core(give).astype(f32)).astype(low)
        for d in group:
            rows = SHARE if d == 4 else 2 * SHARE
            parts[d] = to_z(both[at : at + rows], d).astype(f32)
            at += rows

    image_sum = state[0].astype(f32)
    for d in (2, 1, 3):
        image_sum = image_sum + first_stage(state[d], d).astype(f32)
    image_out = image_sum[:SHARE]
    for d in (2, 1, 3):
        piece = image_sum[d * SHARE : (d + 1) * SHARE].astype(low)
        image_out = image_out + second_stage(piece, d).astype(f32)

    text_sum = parts[1] + parts[2] + parts[3]
    give = (text_sum[SHARE:] + own_give.astype(f32)).astype(low)
    text_out = text_sum[:SHARE] + own_keep + parts[4] + to_core(give).astype(f32)
    return image_out, text_out


def solution(mesh):
    placed = (P("block", None), P("block", None), P("block"))
    return jax.shard_map(
        on_device,
        mesh=mesh,
        in_specs=placed,
        out_specs=(P(("block", "lane"), None), P(("block", "lane"), None)),
        check_vma=False,
    )
```

time: 702 us -> 94.9 us (0.14)
  the two profiles are of different devices: /device:TPU:1 before, /device:TPU:103 now
where the time goes in v1:
time: 94.9 us; the launch traced here: 94.6 us
  waiting for transfers between devices  38.5 us (41%)
  starting transfers between devices  33.1 us (35%)
  Pallas kernels  17.2 us (18%)
  local copies, waits for them, and re-layouts  2.8 us (3%)
  other arithmetic  2.16 us (2%)
    ppermute x25, waiting for transfers between devices, send(): return lax.ppermute(value, AXES, pairs)  38.5 us
    ppermute x25, starting transfers between devices, send(): return lax.ppermute(value, AXES, pairs)  33.1 us
    pallas_call x3, Pallas kernels, tile(): pl.pallas_call(functools.partial(tile_kernel, group, first, last), out_sh...  11.4 us
    pallas_call x2, Pallas kernels, prep(): pl.pallas_call(functools.partial(prep_kernel, far), out_shape=tuple(outs)...  5.81 us
    unnamed x9, local copies, waits for them, and re-layouts  2.01 us
  transfers between devices with their start and end apart: 25, of which 8 were waited for; matrix products, arithmetic and copies ran while one was open for 3% of the time, Pallas kernels for 15%

profile of v1, /device:TPU:103, one launch (start us, length us, event | category | flops | bytes accessed | tf_op | source)
XLA Modules:
  0.0 94.6 jit_solution(4090107447696097229)
XLA Ops:
  1.4 2.9 %shard_map.50 = (bf16[64,1152]{1,0:T(8,128)(2,1)}, bf16[272,1152]{1,0:T(8,128)(2,1)}) custom-call(s32[5]{0:T(128)} %stack.23.where_ref, f32[512,1152]{1,0:T(8,128)} %images_ref.3, f32[512,1152]{1,0:T(8,128)} %texts_ref.3, s32[4,128]{1,0:T(4,128)} %bitcast.6), custom_call_target="tpu_custom_call" | custom-call | bytes 3145728 | tf_op jit(solution)/shard_map/pallas_call | solution.py:99
  4.9 2.1 %collective-permute-start.1 = (bf16[272,1152]{1,0:T(8,128)(2,1)}, bf16[272,1152]{1,0:T(8,128)(2,1)S(1)}, u32[]{:S(2)}, u32[]{:S(2)}) collective-permute-start(bf16[272,1152]{1,0:T(8,128)(2,1)} %get-tuple-element.18.refs_0_), channel_id=1, source_target_pairs={{0,128},{8,136},{16,144},{24,152},{32,160},{40,168},{48,176},{56,1... | collective-permute-start | bytes 1880072 | tf_op jit(solution)/shard_map/ppermute | solution.py:35
  7.1 1.2 %collective-permute-start.2 = (bf16[64,1152]{1,0:T(8,128)(2,1)}, bf16[64,1152]{1,0:T(8,128)(2,1)S(1)}, u32[]{:S(2)}, u32[]{:S(2)}) collective-permute-start(bf16[64,1152]{1,0:T(8,128)(2,1)} %get-tuple-element.19.refs_4_), channel_id=1, source_target_pairs={{0,8},{8,0},{16,24},{24,16},{32,40},{40,32},{48,56},{56,48},{64,72... | collective-permute-start | bytes 442376 | tf_op jit(solution)/shard_map/ppermute | solution.py:35
  8.3 0.9 constant_dynamic-update-slice_fusion.1
  9.6 2.9 %collective-permute-start.3 = (bf16[128,1152]{1,0:T(8,128)(2,1)S(1)}, bf16[128,1152]{1,0:T(8,128)(2,1)S(1)}, u32[]{:S(2)}, u32[]{:S(2)}) collective-permute-start(bf16[128,1152]{1,0:T(8,128)(2,1)S(1)} %constant_dynamic-update-slice_fusion), channel_id=1, source_target_pairs={{0,112},{8,24},{16,0},{24,40},{32,16},{40,56},{48,32},{56,72},{64,... | collective-permute-start | bytes 884744 | tf_op jit(solution)/shard_map/ppermute | solution.py:35
  12.5 1.5 %collective-permute-start.9 = (bf16[64,1152]{1,0:T(8,128)(2,1)}, bf16[64,1152]{1,0:T(8,128)(2,1)S(1)}, u32[]{:S(2)}, u32[]{:S(2)}) collective-permute-start(bf16[64,1152]{1,0:T(8,128)(2,1)} %get-tuple-element.19.refs_4_), channel_id=1, source_target_pairs={{0,64},{8,72},{16,80},{24,88},{32,96},{40,104},{48,112},{56,120},{... | collective-permute-start | bytes 442376 | tf_op jit(solution)/shard_map/ppermute | solution.py:35
  14.0 10.2 %collective-permute-done.9.refs_5_ = bf16[64,1152]{1,0:T(8,128)(2,1)S(1)} collective-permute-done((bf16[64,1152]{1,0:T(8,128)(2,1)}, bf16[64,1152]{1,0:T(8,128)(2,1)S(1)}, u32[]{:S(2)}, u32[]{:S(2)}) %collective-permute-start.9) | collective-permute-done | bytes 147488 | tf_op jit(solution)/shard_map/ppermute | solution.py:35
  24.7 4.2 %collective-permute-start.4 = (bf16[128,1152]{1,0:T(8,128)(2,1)S(1)}, bf16[128,1152]{1,0:T(8,128)(2,1)S(1)}, u32[]{:S(2)}, u32[]{:S(2)}) collective-permute-start(bf16[128,1152]{1,0:T(8,128)(2,1)S(1)} %collective-permute-done.3.refs_6_), channel_id=1, source_target_pairs={{0,8},{8,0},{16,24},{24,16},{32,40},{40,32},{48,56},{56,48},{64,72... | collective-permute-start | bytes 884744 | tf_op jit(solution)/shard_map/ppermute | solution.py:35
  28.9 1.9 %collective-permute-done.5.refs_3_ = bf16[128,1152]{1,0:T(8,128)(2,1)S(1)} collective-permute-done((bf16[128,1152]{1,0:T(8,128)(2,1)S(1)}, bf16[128,1152]{1,0:T(8,128)(2,1)S(1)}, u32[]{:S(2)}, u32[]{:S(2)}) %collective-permute-start.5) | collective-permute-done | bytes 294944 | tf_op jit(solution)/shard_map/ppermute | solution.py:35
  30.8 2.9 %shard_map.51.refs_2_ = bf16[272,1152]{1,0:T(8,128)(2,1)} custom-call(s32[5]{0:T(128)} %stack.23.where_ref, f32[512,1152]{1,0:T(8,128)} %images_ref.3, f32[512,1152]{1,0:T(8,128)} %texts_ref.3, s32[4,128]{1,0:T(4,128)} %bitcast.7), custom_call_target="tpu_custom_call" | custom-call | bytes 3145728 | tf_op jit(solution)/shard_map/pallas_call | solution.py:99
  33.7 5.5 %collective-permute-done.7.refs_3_ = bf16[128,1152]{1,0:T(8,128)(2,1)S(1)} collective-permute-done((bf16[128,1152]{1,0:T(8,128)(2,1)S(1)}, bf16[128,1152]{1,0:T(8,128)(2,1)S(1)}, u32[]{:S(2)}, u32[]{:S(2)}) %collective-permute-start.7) | collective-permute-done | bytes 294944 | tf_op jit(solution)/shard_map/ppermute | solution.py:35
  39.7 1.1 %copy-done = bf16[272,1152]{1,0:T(8,128)(2,1)S(1)} copy-done((bf16[272,1152]{1,0:T(8,128)(2,1)S(1)}, bf16[272,1152]{1,0:T(8,128)(2,1)}, u32[]{:S(2)}) %copy-start) | copy-done | bytes 626712
  40.7 4.2 %shard_map.52 = (bf16[1024,1152]{1,0:T(8,128)(2,1)S(1)}, f32[8,1024]{1,0:T(8,128)S(1)}, f32[1024,1152]{1,0:T(8,128)S(1)}, f32[192,1152]{1,0:T(8,128)S(1)}, bf16[192,1152]{1,0:T(8,128)(2,1)S(1)}) custom-call(s32[5]{0:T(128)S(1)} %copy-done.2, bf16[272,1152]{1,0:T(8,128)(2,1)S(1)} %copy-done.3, bf16[272,1152]{1,0:T(8,128)(2,1)S(1)} %collective-permute-done.refs_1_, ...), custom_call_target="tpu_custom_call" | custom-call | flops 2717908992 | bytes 4194304 | tf_op jit(solution)/shard_map/pallas_call | solution.py:211
  44.9 2.9 %shard_map.53 = (f32[1024,1152]{1,0:T(8,128)S(1)}, f32[128,1152]{1,0:T(8,128)S(1)}, bf16[128,1152]{1,0:T(8,128)(2,1)S(1)}) custom-call(s32[5]{0:T(128)S(1)} %copy-done.2, bf16[1024,1152]{1,0:T(8,128)(2,1)S(1)} %get-tuple-element.20.refs_0_, f32[8,1024]{1,0:T(8,128)S(1)} %get-tuple-element.21.refs_1_, f32[1024,1152]{1,0:T(8,128)S(1)} %get-tuple-element.22.refs_2_, ...), custom_call_target="tpu_custom_call" | custom-call | flops 1811939328 | bytes 4194304 | tf_op jit(solution)/shard_map/pallas_call | solution.py:211
  48.0 4.4 %shard_map.54 = (bf16[256,1152]{1,0:T(8,128)(2,1)S(1)}, bf16[256,1152]{1,0:T(8,128)(2,1)S(1)}, bf16[256,1152]{1,0:T(8,128)(2,1)S(1)}, bf16[256,1152]{1,0:T(8,128...) custom-call(s32[5]{0:T(128)S(1)} %copy-done.2, bf16[1024,1152]{1,0:T(8,128)(2,1)S(1)} %get-tuple-element.20.refs_0_, ...), custom_call_target="tpu_custom_call" | custom-call | flops 2717908992 | bytes 4194304 | tf_op jit(solution)/shard_map/pallas_call | solution.py:211
  53.1 2.9 %collective-permute-start.11 = (bf16[256,1152]{1,0:T(8,128)(2,1)S(1)}, bf16[256,1152]{1,0:T(8,128)(2,1)S(1)}, u32[]{:S(2)}, u32[]{:S(2)}) collective-permute-start(bf16[256,1152]{1,0:T(8,128)(2,1)S(1)} %get-tuple-element.25), channel_id=1, source_target_pairs={{0,4},{8,10},{16,20},{24,26},{32,36},{40,42},{48,52},{56,58},{64,6... | collective-permute-start | bytes 1769480 | tf_op jit(solution)/shard_map/ppermute | solution.py:35
  56.4 2.3 %collective-permute-start.13 = (bf16[256,1152]{1,0:T(8,128)(2,1)S(1)}, bf16[256,1152]{1,0:T(8,128)(2,1)S(1)}, u32[]{:S(2)}, u32[]{:S(2)}) collective-permute-start(bf16[256,1152]{1,0:T(8,128)(2,1)S(1)} %get-tuple-element.27), channel_id=1, source_target_pairs={{0,132},{8,11},{16,148},{24,27},{32,164},{40,43},{48,180},{56,59},... | collective-permute-start | bytes 1769480 | tf_op jit(solution)/shard_map/ppermute | solution.py:35
  58.8 2.6 %collective-permute-start.20 = (bf16[128,1152]{1,0:T(8,128)(2,1)S(1)}, bf16[128,1152]{1,0:T(8,128)(2,1)S(1)}, u32[]{:S(2)}, u32[]{:S(2)}) collective-permute-start(bf16[128,1152]{1,0:T(8,128)(2,1)S(1)} %add_convert_fusion.1), channel_id=1, source_target_pairs={{0,32},{8,104},{16,48},{24,120},{32,64},{40,8},{48,80},{56,24},{64... | collective-permute-start | bytes 884744 | tf_op jit(solution)/shard_map/ppermute | solution.py:35
  61.4 1.7 %collective-permute-start.18 = (bf16[128,1152]{1,0:T(8,128)(2,1)S(1)}, bf16[128,1152]{1,0:T(8,128)(2,1)S(1)}, u32[]{:S(2)}, u32[]{:S(2)}) collective-permute-start(bf16[128,1152]{1,0:T(8,128)(2,1)S(1)} %add_convert_fusion.2), channel_id=1, source_target_pairs={{0,16},{8,120},{16,32},{24,8},{32,48},{40,24},{48,64},{56,40},{64,... | collective-permute-start | bytes 884744 | tf_op jit(solution)/shard_map/ppermute | solution.py:35
  63.7 3.0 %collective-permute-start.22 = (bf16[128,1152]{1,0:T(8,128)(2,1)S(1)}, bf16[128,1152]{1,0:T(8,128)(2,1)S(1)}, u32[]{:S(2)}, u32[]{:S(2)}) collective-permute-start(bf16[128,1152]{1,0:T(8,128)(2,1)S(1)} %slice.55), channel_id=1, source_target_pairs={{0,48},{8,88},{16,64},{24,104},{32,80},{40,120},{48,96},{56,8},{64... | collective-permute-start | bytes 884744 | tf_op jit(solution)/shard_map/ppermute | solution.py:35
  66.6 3.3 %collective-permute-done.12 = bf16[256,1152]{1,0:T(8,128)(2,1)S(1)} collective-permute-done((bf16[256,1152]{1,0:T(8,128)(2,1)S(1)}, bf16[256,1152]{1,0:T(8,128)(2,1)S(1)}, u32[]{:S(2)}, u32[]{:S(2)}) %collective-permute-start.12) | collective-permute-done | bytes 589856 | tf_op jit(solution)/shard_map/ppermute | solution.py:35
  69.9 4.0 %collective-permute-start.23 = (bf16[64,1152]{1,0:T(8,128)(2,1)S(1)}, bf16[64,1152]{1,0:T(8,128)(2,1)S(1)}, u32[]{:S(2)}, u32[]{:S(2)}) collective-permute-start(bf16[64,1152]{1,0:T(8,128)(2,1)S(1)} %slice.57), channel_id=1, source_target_pairs={{0,64},{8,72},{16,80},{24,88},{32,96},{40,104},{48,112},{56,120},{... | collective-permute-start | bytes 442376 | tf_op jit(solution)/shard_map/ppermute | solution.py:35
  74.4 1.4 %collective-permute-start.15 = (bf16[64,1152]{1,0:T(8,128)(2,1)S(1)}, bf16[64,1152]{1,0:T(8,128)(2,1)S(1)}, u32[]{:S(2)}, u32[]{:S(2)}) collective-permute-start(bf16[64,1152]{1,0:T(8,128)(2,1)S(1)} %get-tuple-element.38), channel_id=1, source_target_pairs={{0,1},{8,136},{16,17},{24,152},{32,33},{40,168},{48,49},{56,184},{... | collective-permute-start | bytes 442376 | tf_op jit(solution)/shard_map/ppermute | solution.py:35
  76.0 16.3 %collective-permute-done.22 = bf16[128,1152]{1,0:T(8,128)(2,1)S(1)} collective-permute-done((bf16[128,1152]{1,0:T(8,128)(2,1)S(1)}, bf16[128,1152]{1,0:T(8,128)(2,1)S(1)}, u32[]{:S(2)}, u32[]{:S(2)}) %collective-permute-start.22) | collective-permute-done | bytes 294944 | tf_op jit(solution)/shard_map/ppermute | solution.py:35
  (54 shorter events, 7.5 us)
Async XLA Ops:
  4.3 34.9 %collective-permute-start = (bf16[272,1152]{1,0:T(8,128)(2,1)}, bf16[272,1152]{1,0:T(8,128)(2,1)S(1)}, u32[]{:S(2)}, u32[]{:S(2)}) collective-permute-start(bf16[272,1152]{1,0:T(8,128)(2,1)} %get-tuple-element.18.refs_0_), channel_id=1, source_target_pairs={{0,132},{8,140},{16,148},{24,156},{32,164},{40,172},{48,180},{56,1... | collective-permute-start | bytes 1880072 | tf_op jit(solution)/shard_map/ppermute | solution.py:35
  4.9 34.7 %collective-permute-start.1 = (bf16[272,1152]{1,0:T(8,128)(2,1)}, bf16[272,1152]{1,0:T(8,128)(2,1)S(1)}, u32[]{:S(2)}, u32[]{:S(2)}) collective-permute-start(bf16[272,1152]{1,0:T(8,128)(2,1)} %get-tuple-element.18.refs_0_), channel_id=1, source_target_pairs={{0,128},{8,136},{16,144},{24,152},{32,160},{40,168},{48,176},{56,1... | collective-permute-start | bytes 1880072 | tf_op jit(solution)/shard_map/ppermute | solution.py:35
  7.1 2.5 %collective-permute-start.2 = (bf16[64,1152]{1,0:T(8,128)(2,1)}, bf16[64,1152]{1,0:T(8,128)(2,1)S(1)}, u32[]{:S(2)}, u32[]{:S(2)}) collective-permute-start(bf16[64,1152]{1,0:T(8,128)(2,1)} %get-tuple-element.19.refs_4_), channel_id=1, source_target_pairs={{0,8},{8,0},{16,24},{24,16},{32,40},{40,32},{48,56},{56,48},{64,72... | collective-permute-start | bytes 442376 | tf_op jit(solution)/shard_map/ppermute | solution.py:35
  9.6 15.1 %collective-permute-start.3 = (bf16[128,1152]{1,0:T(8,128)(2,1)S(1)}, bf16[128,1152]{1,0:T(8,128)(2,1)S(1)}, u32[]{:S(2)}, u32[]{:S(2)}) collective-permute-start(bf16[128,1152]{1,0:T(8,128)(2,1)S(1)} %constant_dynamic-update-slice_fusion), channel_id=1, source_target_pairs={{0,112},{8,24},{16,0},{24,40},{32,16},{40,56},{48,32},{56,72},{64,... | collective-permute-start | bytes 884744 | tf_op jit(solution)/shard_map/ppermute | solution.py:35
  12.5 11.7 %collective-permute-start.9 = (bf16[64,1152]{1,0:T(8,128)(2,1)}, bf16[64,1152]{1,0:T(8,128)(2,1)S(1)}, u32[]{:S(2)}, u32[]{:S(2)}) collective-permute-start(bf16[64,1152]{1,0:T(8,128)(2,1)} %get-tuple-element.19.refs_4_), channel_id=1, source_target_pairs={{0,64},{8,72},{16,80},{24,88},{32,96},{40,104},{48,112},{56,120},{... | collective-permute-start | bytes 442376 | tf_op jit(solution)/shard_map/ppermute | solution.py:35
  14.0 16.8 %collective-permute-start.5 = (bf16[128,1152]{1,0:T(8,128)(2,1)S(1)}, bf16[128,1152]{1,0:T(8,128)(2,1)S(1)}, u32[]{:S(2)}, u32[]{:S(2)}) collective-permute-start(bf16[128,1152]{1,0:T(8,128)(2,1)S(1)} %constant_dynamic-update-slice_fusion), channel_id=1, source_target_pairs={{0,96},{8,40},{16,112},{24,56},{32,0},{40,72},{48,16},{56,88},{64,... | collective-permute-start | bytes 884744 | tf_op jit(solution)/shard_map/ppermute | solution.py:35
  24.2 14.9 %collective-permute-start.7 = (bf16[128,1152]{1,0:T(8,128)(2,1)S(1)}, bf16[128,1152]{1,0:T(8,128)(2,1)S(1)}, u32[]{:S(2)}, u32[]{:S(2)}) collective-permute-start(bf16[128,1152]{1,0:T(8,128)(2,1)S(1)} %constant_dynamic-update-slice_fusion), channel_id=1, source_target_pairs={{0,80},{8,56},{16,96},{24,72},{32,112},{40,88},{48,0},{56,104},{64... | collective-permute-start | bytes 884744 | tf_op jit(solution)/shard_map/ppermute | solution.py:35
  24.7 15.0 %collective-permute-start.4 = (bf16[128,1152]{1,0:T(8,128)(2,1)S(1)}, bf16[128,1152]{1,0:T(8,128)(2,1)S(1)}, u32[]{:S(2)}, u32[]{:S(2)}) collective-permute-start(bf16[128,1152]{1,0:T(8,128)(2,1)S(1)} %collective-permute-done.3.refs_6_), channel_id=1, source_target_pairs={{0,8},{8,0},{16,24},{24,16},{32,40},{40,32},{48,56},{56,48},{64,72... | collective-permute-start | bytes 884744 | tf_op jit(solution)/shard_map/ppermute | solution.py:35
  30.8 14.2 %collective-permute-start.6 = (bf16[128,1152]{1,0:T(8,128)(2,1)S(1)}, bf16[128,1152]{1,0:T(8,128)(2,1)S(1)}, u32[]{:S(2)}, u32[]{:S(2)}) collective-permute-start(bf16[128,1152]{1,0:T(8,128)(2,1)S(1)} %collective-permute-done.5.refs_3_), channel_id=1, source_target_pairs={{0,8},{8,0},{16,24},{24,16},{32,40},{40,32},{48,56},{56,48},{64,72... | collective-permute-start | bytes 884744 | tf_op jit(solution)/shard_map/ppermute | solution.py:35
  39.1 8.9 %collective-permute-start.10 = (bf16[64,1152]{1,0:T(8,128)(2,1)S(1)}, bf16[64,1152]{1,0:T(8,128)(2,1)S(1)}, u32[]{:S(2)}, u32[]{:S(2)}) collective-permute-start(bf16[64,1152]{1,0:T(8,128)(2,1)S(1)} %collective-permute-done.9.refs_5_), channel_id=1, source_target_pairs={{0,8},{8,0},{16,24},{24,16},{32,40},{40,32},{48,56},{56,48},{64,72... | collective-permute-start | bytes 442376 | tf_op jit(solution)/shard_map/ppermute | solution.py:35
  39.2 8.8 %collective-permute-start.8 = (bf16[128,1152]{1,0:T(8,128)(2,1)S(1)}, bf16[128,1152]{1,0:T(8,128)(2,1)S(1)}, u32[]{:S(2)}, u32[]{:S(2)}) collective-permute-start(bf16[128,1152]{1,0:T(8,128)(2,1)S(1)} %collective-permute-done.7.refs_3_), channel_id=1, source_target_pairs={{0,8},{8,0},{16,24},{24,16},{32,40},{40,32},{48,56},{56,48},{64,72... | collective-permute-start | bytes 884744 | tf_op jit(solution)/shard_map/ppermute | solution.py:35
  47.8 8.6 %collective-permute-start.19 = (bf16[128,1152]{1,0:T(8,128)(2,1)S(1)}, bf16[128,1152]{1,0:T(8,128)(2,1)S(1)}, u32[]{:S(2)}, u32[]{:S(2)}) collective-permute-start(bf16[128,1152]{1,0:T(8,128)(2,1)S(1)} %get-tuple-element.31), channel_id=1, source_target_pairs={{0,8},{8,0},{16,24},{24,16},{32,40},{40,32},{48,56},{56,48},{64,72... | collective-permute-start | bytes 884744 | tf_op jit(solution)/shard_map/ppermute | solution.py:35
  52.4 9.0 %collective-permute-start.21 = (bf16[192,1152]{1,0:T(8,128)(2,1)S(1)}, bf16[192,1152]{1,0:T(8,128)(2,1)S(1)}, u32[]{:S(2)}, u32[]{:S(2)}) collective-permute-start(bf16[192,1152]{1,0:T(8,128)(2,1)S(1)} %get-tuple-element.33), channel_id=1, source_target_pairs={{0,8},{8,0},{16,24},{24,16},{32,40},{40,32},{48,56},{56,48},{64,72... | collective-permute-start | bytes 1327112 | tf_op jit(solution)/shard_map/ppermute | solution.py:35
  52.9 5.9 %collective-permute-start.17 = (bf16[128,1152]{1,0:T(8,128)(2,1)S(1)}, bf16[128,1152]{1,0:T(8,128)(2,1)S(1)}, u32[]{:S(2)}, u32[]{:S(2)}) collective-permute-start(bf16[128,1152]{1,0:T(8,128)(2,1)S(1)} %slice.44), channel_id=1, source_target_pairs={{0,8},{8,0},{16,24},{24,16},{32,40},{40,32},{48,56},{56,48},{64,72... | collective-permute-start | bytes 884744 | tf_op jit(solution)/shard_map/ppermute | solution.py:35
  53.1 10.6 %collective-permute-start.11 = (bf16[256,1152]{1,0:T(8,128)(2,1)S(1)}, bf16[256,1152]{1,0:T(8,128)(2,1)S(1)}, u32[]{:S(2)}, u32[]{:S(2)}) collective-permute-start(bf16[256,1152]{1,0:T(8,128)(2,1)S(1)} %get-tuple-element.25), channel_id=1, source_target_pairs={{0,4},{8,10},{16,20},{24,26},{32,36},{40,42},{48,52},{56,58},{64,6... | collective-permute-start | bytes 1769480 | tf_op jit(solution)/shard_map/ppermute | solution.py:35
  56.0 13.9 %collective-permute-start.12 = (bf16[256,1152]{1,0:T(8,128)(2,1)S(1)}, bf16[256,1152]{1,0:T(8,128)(2,1)S(1)}, u32[]{:S(2)}, u32[]{:S(2)}) collective-permute-start(bf16[256,1152]{1,0:T(8,128)(2,1)S(1)} %get-tuple-element.26), channel_id=1, source_target_pairs={{0,128},{8,9},{16,144},{24,25},{32,160},{40,41},{48,176},{56,57},{... | collective-permute-start | bytes 1769480 | tf_op jit(solution)/shard_map/ppermute | solution.py:35
  56.4 17.6 %collective-permute-start.13 = (bf16[256,1152]{1,0:T(8,128)(2,1)S(1)}, bf16[256,1152]{1,0:T(8,128)(2,1)S(1)}, u32[]{:S(2)}, u32[]{:S(2)}) collective-permute-start(bf16[256,1152]{1,0:T(8,128)(2,1)S(1)} %get-tuple-element.27), channel_id=1, source_target_pairs={{0,132},{8,11},{16,148},{24,27},{32,164},{40,43},{48,180},{56,59},... | collective-permute-start | bytes 1769480 | tf_op jit(solution)/shard_map/ppermute | solution.py:35
  58.8 15.7 %collective-permute-start.20 = (bf16[128,1152]{1,0:T(8,128)(2,1)S(1)}, bf16[128,1152]{1,0:T(8,128)(2,1)S(1)}, u32[]{:S(2)}, u32[]{:S(2)}) collective-permute-start(bf16[128,1152]{1,0:T(8,128)(2,1)S(1)} %add_convert_fusion.1), channel_id=1, source_target_pairs={{0,32},{8,104},{16,48},{24,120},{32,64},{40,8},{48,80},{56,24},{64... | collective-permute-start | bytes 884744 | tf_op jit(solution)/shard_map/ppermute | solution.py:35
  61.4 14.5 %collective-permute-start.18 = (bf16[128,1152]{1,0:T(8,128)(2,1)S(1)}, bf16[128,1152]{1,0:T(8,128)(2,1)S(1)}, u32[]{:S(2)}, u32[]{:S(2)}) collective-permute-start(bf16[128,1152]{1,0:T(8,128)(2,1)S(1)} %add_convert_fusion.2), channel_id=1, source_target_pairs={{0,16},{8,120},{16,32},{24,8},{32,48},{40,24},{48,64},{56,40},{64,... | collective-permute-start | bytes 884744 | tf_op jit(solution)/shard_map/ppermute | solution.py:35
  63.7 28.6 %collective-permute-start.22 = (bf16[128,1152]{1,0:T(8,128)(2,1)S(1)}, bf16[128,1152]{1,0:T(8,128)(2,1)S(1)}, u32[]{:S(2)}, u32[]{:S(2)}) collective-permute-start(bf16[128,1152]{1,0:T(8,128)(2,1)S(1)} %slice.55), channel_id=1, source_target_pairs={{0,48},{8,88},{16,64},{24,104},{32,80},{40,120},{48,96},{56,8},{64... | collective-permute-start | bytes 884744 | tf_op jit(solution)/shard_map/ppermute | solution.py:35
  69.9 23.4 %collective-permute-start.23 = (bf16[64,1152]{1,0:T(8,128)(2,1)S(1)}, bf16[64,1152]{1,0:T(8,128)(2,1)S(1)}, u32[]{:S(2)}, u32[]{:S(2)}) collective-permute-start(bf16[64,1152]{1,0:T(8,128)(2,1)S(1)} %slice.57), channel_id=1, source_target_pairs={{0,64},{8,72},{16,80},{24,88},{32,96},{40,104},{48,112},{56,120},{... | collective-permute-start | bytes 442376 | tf_op jit(solution)/shard_map/ppermute | solution.py:35
  74.3 18.2 %collective-permute-start.14 = (bf16[64,1152]{1,0:T(8,128)(2,1)S(1)}, bf16[64,1152]{1,0:T(8,128)(2,1)S(1)}, u32[]{:S(2)}, u32[]{:S(2)}) collective-permute-start(bf16[64,1152]{1,0:T(8,128)(2,1)S(1)} %get-tuple-element.36), channel_id=1, source_target_pairs={{0,2},{8,12},{16,18},{24,28},{32,34},{40,44},{48,50},{56,60},{64,6... | collective-permute-start | bytes 442376 | tf_op jit(solution)/shard_map/ppermute | solution.py:35
  74.4 18.1 %collective-permute-start.15 = (bf16[64,1152]{1,0:T(8,128)(2,1)S(1)}, bf16[64,1152]{1,0:T(8,128)(2,1)S(1)}, u32[]{:S(2)}, u32[]{:S(2)}) collective-permute-start(bf16[64,1152]{1,0:T(8,128)(2,1)S(1)} %get-tuple-element.38), channel_id=1, source_target_pairs={{0,1},{8,136},{16,17},{24,152},{32,33},{40,168},{48,49},{56,184},{... | collective-permute-start | bytes 442376 | tf_op jit(solution)/shard_map/ppermute | solution.py:35
  75.9 16.7 %collective-permute-start.16 = (bf16[64,1152]{1,0:T(8,128)(2,1)S(1)}, bf16[64,1152]{1,0:T(8,128)(2,1)S(1)}, u32[]{:S(2)}, u32[]{:S(2)}) collective-permute-start(bf16[64,1152]{1,0:T(8,128)(2,1)S(1)} %get-tuple-element.37), channel_id=1, source_target_pairs={{0,3},{8,140},{16,19},{24,156},{32,35},{40,172},{48,51},{56,188},{... | collective-permute-start | bytes 442376 | tf_op jit(solution)/shard_map/ppermute | solution.py:35
  (5 other events, 92.8 us)

commit v2 on v1

--- a/solution.py
+++ b/solution.py
@@ -16,7 +16,7 @@
 f32 = jnp.float32
 MIB = 1 << 20
 VMEM = pl.BlockSpec(memory_space=pltpu.VMEM)
-ANY = pl.BlockSpec(memory_space=pl.ANY)
+HBM = pl.BlockSpec(memory_space=pltpu.HBM)
 
 
 def flat(x, y, z, c):
@@ -99,19 +99,19 @@
     return pl.pallas_call(
         functools.partial(prep_kernel, far),
         out_shape=tuple(outs),
-        in_specs=[pl.BlockSpec(memory_space=pltpu.SMEM), ANY, ANY, VMEM],
+        in_specs=[pl.BlockSpec(memory_space=pltpu.SMEM), HBM, HBM, VMEM],
         out_specs=(VMEM,) * len(outs),
         scratch_shapes=[
             pltpu.VMEM((Y, SHARE, width), f32),
             pltpu.VMEM((SHARE, width), f32),
             pltpu.SemaphoreType.DMA((5,)),
         ],
-        compiler_params=pltpu.CompilerParams(vmem_limit_bytes=58 * MIB),
+        compiler_params=pltpu.CompilerParams(vmem_limit_bytes=52 * MIB),
         cost_estimate=pl.CostEstimate(flops=0, bytes_accessed=3 << 20, transcendentals=0),
     )(where, images, texts, labels)
 
 
-def tile_kernel(group, first, last, where_ref, *refs):
+def tile_kernel(group, gives, first, last, where_ref, *refs):
     refs = list(refs)
     if first:
         parts = [refs.pop(0) for _ in range(4)]
@@ -127,8 +127,8 @@
         image_outs = [refs.pop(0) for _ in range(4)]
     else:
         sums_ref = refs.pop(0)
-    keep_ref = refs.pop(0)
-    give_ref = refs.pop(0)
+    keep_refs = [refs.pop(0) for _ in group]
+    give_refs = [refs.pop(0) for _ in range(gives)]
     text_ref, weight_ref = refs
     n = text_ref.shape[0]
     half = n // 2
@@ -168,8 +168,13 @@
         positive = (labels_ref[0:1, cut] == numbers).astype(f32)
         weight_ref[:, cut] = (jax.nn.sigmoid(logits) - positive).astype(low)
     text_term = jnp.dot(weight_ref[...], images_ref[...], preferred_element_type=f32)
-    keep_ref[...] = text_term[:half]
-    give_ref[...] = text_term[half:].astype(low)
+    at = 0
+    for ref in keep_refs:
+        ref[...] = text_term[at : at + ref.shape[0]]
+        at += ref.shape[0]
+    for ref in give_refs:
+        ref[...] = text_term[at : at + ref.shape[0]].astype(low)
+        at += ref.shape[0]
     total = lax.dot_general(weight_ref[...], text, (((0,), (0,)), ((), ())), preferred_element_type=f32)
     if not first:
         total = total + held[...]
@@ -204,12 +209,15 @@
         outs += [jax.ShapeDtypeStruct((256, width), low)] * 4
     else:
         outs.append(jax.ShapeDtypeStruct((1024, width), f32))
-    outs += [jax.ShapeDtypeStruct((half, width), f32), jax.ShapeDtypeStruct((half, width), low)]
+    sizes = [pair[0].shape[0] for pair in texts]
+    give_sizes = sizes if first else [half]
+    outs += [jax.ShapeDtypeStruct((size, width), f32) for size in sizes]
+    outs += [jax.ShapeDtypeStruct((size, width), low) for size in give_sizes]
     args = [where, *state]
     for pair in texts:
         args += pair
     results = pl.pallas_call(
-        functools.partial(tile_kernel, group, first, last),
+        functools.partial(tile_kernel, group, len(give_sizes), first, last),
         out_shape=tuple(outs),
         in_specs=[pl.BlockSpec(memory_space=pltpu.SMEM)] + [VMEM] * (len(args) - 1),
         out_specs=(VMEM,) * len(outs),
@@ -219,7 +227,8 @@
             flops=6 * 1024 * n * width, bytes_accessed=4 << 20, transcendentals=1024 * n
         ),
     )(*args)
-    keep, give = results[-2:]
+    cut = len(results) - len(give_sizes)
+    keep, give = results[cut - len(sizes) : cut], results[cut:]
     if first:
         state = results[:3]
     elif last:
@@ -237,28 +246,34 @@
     image_right = to_x(image_near, -1)
     image_left = to_x(image_near, 1)
     chunk = jnp.concatenate([text_own, text_other], axis=0)
-    arrived = {}
-    for d in (3, 2, 1):
-        arrived[d] = to_z(chunk, -d)
-    arrived[4] = to_z(text_own, 4)
+    arrived = {2: to_z(chunk, -2), 1: to_z(chunk, -1)}
+    swapped_1 = to_core(arrived[1])
+    arrived[2], swapped_1 = lax.optimization_barrier((arrived[2], swapped_1))
+    arrived[3] = to_z(arrived[2], -1)
+    arrived[4] = to_z(arrived[2][:SHARE], -2)
     (image_far,) = prep(where, images, texts, label_rows, True)
+    image_right, _ = lax.optimization_barrier((image_right, arrived[2]))
     state = (image_near, image_right, image_far, image_left)
 
-    groups = ((0, 1), (2,), (3, 4))
-    parts = {}
-    for i, group in enumerate(groups):
-        pairs = [(text_own, text_other) if d == 0 else (arrived[d], to_core(arrived[d])) for d in group]
-        state, keep, give = tile(where, state, group, pairs, i == len(groups) - 1)
-        at = 0
-        if group[0] == 0:
-            own_keep, own_give = keep[:SHARE], give[:SHARE]
-            keep, give = keep[SHARE:], give[SHARE:]
-            group = group[1:]
-        both = (keep + to_core(give).astype(f32)).astype(low)
-        for d in group:
-            rows = SHARE if d == 4 else 2 * SHARE
-            parts[d] = to_z(both[at : at + rows], d).astype(f32)
-            at += rows
+    pairs = [(text_own, text_other), (arrived[1], swapped_1)]
+    state, keep, give = tile(where, state, (0, 1), pairs, False)
+    own_keep, own_give = keep[0], give[0]
+    term_1 = (keep[1] + to_core(give[1]).astype(f32)).astype(low)
+
+    pairs = [(arrived[2], to_core(arrived[2]))]
+    state, keep, give = tile(where, state, (2,), pairs, False)
+    term_2 = keep[0] + to_core(give[0]).astype(f32)
+
+    pairs = [(arrived[d], to_core(arrived[d])) for d in (3, 4)]
+    held, term_1 = lax.optimization_barrier((state[2], term_1))
+    state, keep, give = tile(where, (state[0], state[1], held), (3, 4), pairs, True)
+    swapped = to_core(give[0]).astype(f32)
+    from_3 = to_z((keep[0] + swapped[: 2 * SHARE]).astype(low), 1).astype(f32)
+    from_4 = to_z((keep[1] + swapped[2 * SHARE :]).astype(low), 2).astype(f32)
+    upper = term_2[:SHARE] + from_3[:SHARE] + from_4
+    lower = term_2[SHARE:] + from_3[SHARE:]
+    term_2 = jnp.concatenate([upper, lower], axis=0).astype(low)
+    parts = to_z(term_1, 1).astype(f32) + to_z(term_2, 2).astype(f32)
 
     image_sum = state[0].astype(f32)
     for d in (2, 1, 3):
@@ -268,9 +283,8 @@
         piece = image_sum[d * SHARE : (d + 1) * SHARE].astype(low)
         image_out = image_out + second_stage(piece, d).astype(f32)
 
-    text_sum = parts[1] + parts[2] + parts[3]
-    give = (text_sum[SHARE:] + own_give.astype(f32)).astype(low)
-    text_out = text_sum[:SHARE] + own_keep + parts[4] + to_core(give).astype(f32)
+    give = (parts[SHARE:] + own_give.astype(f32)).astype(low)
+    text_out = parts[:SHARE] + own_keep + to_core(give).astype(f32)
     return image_out, text_out
 
 

time: 94.9 us -> 80.3 us (0.85)
  the two profiles are of different devices: /device:TPU:103 before, /device:TPU:1 now
where the time goes in v2:
time: 80.3 us; the launch traced here: 80.1 us
  starting transfers between devices  43.3 us (54%)
  waiting for transfers between devices  17.6 us (22%)
  Pallas kernels  15.2 us (19%)
  other arithmetic  2.33 us (3%)
  between operations  0.88 us (1%)
  local copies, waits for them, and re-layouts  0.85 us (1%)
    ppermute x25, starting transfers between devices, send(): return lax.ppermute(value, AXES, pairs)  43.3 us
    ppermute x25, waiting for transfers between devices, send(): return lax.ppermute(value, AXES, pairs)  17.6 us
    pallas_call x3, Pallas kernels, tile(): pl.pallas_call(functools.partial(tile_kernel, group, len(give_sizes), fir...  11.4 us
    pallas_call x2, Pallas kernels, prep(): pl.pallas_call(functools.partial(prep_kernel, far), out_shape=tuple(outs)...  3.77 us
  transfers between devices with their start and end apart: 25, of which 8 were waited for; matrix products, arithmetic and copies ran while one was open for 2% of the time, Pallas kernels for 17%

profile of v2, /device:TPU:1, one launch (start us, length us, event | category | flops | bytes accessed | tf_op | source)
XLA Modules:
  0.0 80.1 jit_solution(8608654849874531006)
XLA Ops:
  1.5 1.9 %shard_map.50 = (bf16[64,1152]{1,0:T(8,128)(2,1)S(1)}, bf16[272,1152]{1,0:T(8,128)(2,1)S(1)}) custom-call(s32[5]{0:T(128)S(1)} %stack.23.where_ref, f32[512,1152]{1,0:T(8,128)} %images_ref.3, f32[512,1152]{1,0:T(8,128)} %texts_ref.3, s32[4,128]{1,0:T(4,128)S(1)} %bitcast.6), custom_call_target="tpu_custom_call" | custom-call | bytes 3145728 | tf_op jit(solution)/shard_map/pallas_call | solution.py:99
  3.4 3.4 %collective-permute-start = (bf16[272,1152]{1,0:T(8,128)(2,1)S(1)}, bf16[272,1152]{1,0:T(8,128)(2,1)S(1)}, u32[]{:S(2)}, u32[]{:S(2)}) collective-permute-start(bf16[272,1152]{1,0:T(8,128)(2,1)S(1)} %get-tuple-element.26.refs_0_), channel_id=1, source_target_pairs={{0,132},{8,140},{16,148},{24,156},{32,164},{40,172},{48,180},{56,1... | collective-permute-start | bytes 1880072 | tf_op jit(solution)/shard_map/ppermute | solution.py:35
  6.8 2.0 %collective-permute-start.1 = (bf16[64,1152]{1,0:T(8,128)(2,1)S(1)}, bf16[64,1152]{1,0:T(8,128)(2,1)S(1)}, u32[]{:S(2)}, u32[]{:S(2)}) collective-permute-start(bf16[64,1152]{1,0:T(8,128)(2,1)S(1)} %get-tuple-element.27.refs_4_), channel_id=1, source_target_pairs={{0,8},{8,0},{16,24},{24,16},{32,40},{40,32},{48,56},{56,48},{64,72... | collective-permute-start | bytes 442376 | tf_op jit(solution)/shard_map/ppermute | solution.py:35
  10.5 3.0 %collective-permute-start.2 = (bf16[128,1152]{1,0:T(8,128)(2,1)S(1)}, bf16[128,1152]{1,0:T(8,128)(2,1)S(1)}, u32[]{:S(2)}, u32[]{:S(2)}) collective-permute-start(bf16[128,1152]{1,0:T(8,128)(2,1)S(1)} %constant_dynamic-update-slice_fusion), channel_id=1, source_target_pairs={{0,96},{8,40},{16,112},{24,56},{32,0},{40,72},{48,16},{56,88},{64,... | collective-permute-start | bytes 884744 | tf_op jit(solution)/shard_map/ppermute | solution.py:35
  13.5 5.4 %collective-permute-done.3.refs_6_ = bf16[128,1152]{1,0:T(8,128)(2,1)S(1)} collective-permute-done((bf16[128,1152]{1,0:T(8,128)(2,1)S(1)}, bf16[128,1152]{1,0:T(8,128)(2,1)S(1)}, u32[]{:S(2)}, u32[]{:S(2)}) %collective-permute-start.3) | collective-permute-done | bytes 294944 | tf_op jit(solution)/shard_map/ppermute | solution.py:35
  18.8 2.8 %collective-permute-start.4 = (bf16[128,1152]{1,0:T(8,128)(2,1)S(1)}, bf16[128,1152]{1,0:T(8,128)(2,1)S(1)}, u32[]{:S(2)}, u32[]{:S(2)}) collective-permute-start(bf16[128,1152]{1,0:T(8,128)(2,1)S(1)} %collective-permute-done.3.refs_6_), channel_id=1, source_target_pairs={{0,8},{8,0},{16,24},{24,16},{32,40},{40,32},{48,56},{56,48},{64,72... | collective-permute-start | bytes 884744 | tf_op jit(solution)/shard_map/ppermute | solution.py:35
  21.6 1.8 %shard_map.51.refs_2_ = bf16[272,1152]{1,0:T(8,128)(2,1)S(1)} custom-call(s32[5]{0:T(128)S(1)} %stack.23.where_ref, f32[512,1152]{1,0:T(8,128)} %images_ref.3, f32[512,1152]{1,0:T(8,128)} %texts_ref.3, s32[4,128]{1,0:T(4,128)S(1)} %bitcast.7), custom_call_target="tpu_custom_call" | custom-call | bytes 3145728 | tf_op jit(solution)/shard_map/pallas_call | solution.py:99
  23.5 2.1 %collective-permute-start.6 = (bf16[128,1152]{1,0:T(8,128)(2,1)S(1)}, bf16[128,1152]{1,0:T(8,128)(2,1)S(1)}, u32[]{:S(2)}, u32[]{:S(2)}) collective-permute-start(bf16[128,1152]{1,0:T(8,128)(2,1)S(1)} %collective-permute-done.2.refs_3_), channel_id=1, source_target_pairs={{0,8},{8,0},{16,24},{24,16},{32,40},{40,32},{48,56},{56,48},{64,72... | collective-permute-start | bytes 884744 | tf_op jit(solution)/shard_map/ppermute | solution.py:35
  26.1 1.8 %collective-permute-start.10 = (bf16[64,1152]{1,0:T(8,128)(2,1)S(1)}, bf16[64,1152]{1,0:T(8,128)(2,1)S(1)}, u32[]{:S(2)}, u32[]{:S(2)}) collective-permute-start(bf16[64,1152]{1,0:T(8,128)(2,1)S(1)} %slice.42), channel_id=1, source_target_pairs={{0,96},{8,40},{16,112},{24,56},{32,0},{40,72},{48,16},{56,88},{64,... | collective-permute-start | bytes 442376 | tf_op jit(solution)/shard_map/ppermute | solution.py:35
  27.9 4.2 %shard_map.52 = (bf16[1024,1152]{1,0:T(8,128)(2,1)S(1)}, f32[8,1024]{1,0:T(8,128)S(1)}, f32[1024,1152]{1,0:T(8,128)S(1)}, f32[64,1152]{1,0:T(8,128)S(1)}, f32[12...) custom-call(s32[5]{0:T(128)S(1)} %stack.23.where_ref, ...), custom_call_target="tpu_custom_call" | custom-call | flops 2717908992 | bytes 4194304 | tf_op jit(solution)/shard_map/pallas_call | solution.py:219
  32.1 2.5 %collective-permute-start.7 = (bf16[128,1152]{1,0:T(8,128)(2,1)S(1)}, bf16[128,1152]{1,0:T(8,128)(2,1)S(1)}, u32[]{:S(2)}, u32[]{:S(2)}) collective-permute-start(bf16[128,1152]{1,0:T(8,128)(2,1)S(1)} %get-tuple-element.36), channel_id=1, source_target_pairs={{0,8},{8,0},{16,24},{24,16},{32,40},{40,32},{48,56},{56,48},{64,72... | collective-permute-start | bytes 884744 | tf_op jit(solution)/shard_map/ppermute | solution.py:35
  35.6 2.8 %shard_map.53 = (f32[1024,1152]{1,0:T(8,128)S(1)}, f32[128,1152]{1,0:T(8,128)S(1)}, bf16[128,1152]{1,0:T(8,128)(2,1)S(1)}) custom-call(s32[5]{0:T(128)S(1)} %stack.23.where_ref, bf16[1024,1152]{1,0:T(8,128)(2,1)S(1)} %get-tuple-element.31.refs_0_, f32[8,1024]{1,0:T(8,128)S(1)} %get-tuple-element.32.refs_1_, f32[1024,1152]{1,0:T(8,128)S(1)} %get-tuple-element.33.refs_2_, ...), custom_call_target="tpu_custom_call" | custom-call | flops 1811939328 | bytes 4194304 | tf_op jit(solution)/shard_map/pallas_call | solution.py:219
  39.3 3.1 %collective-permute-start.18 = (bf16[128,1152]{1,0:T(8,128)(2,1)S(1)}, bf16[128,1152]{1,0:T(8,128)(2,1)S(1)}, u32[]{:S(2)}, u32[]{:S(2)}) collective-permute-start(bf16[128,1152]{1,0:T(8,128)(2,1)S(1)} %add_convert_fusion), channel_id=1, source_target_pairs={{0,16},{8,120},{16,32},{24,8},{32,48},{40,24},{48,64},{56,40},{64,... | collective-permute-start | bytes 884744 | tf_op jit(solution)/shard_map/ppermute | solution.py:35
  42.4 4.4 %shard_map.54 = (bf16[256,1152]{1,0:T(8,128)(2,1)S(1)}, bf16[256,1152]{1,0:T(8,128)(2,1)S(1)}, bf16[256,1152]{1,0:T(8,128)(2,1)S(1)}, bf16[256,1152]{1,0:T(8,128...) custom-call(s32[5]{0:T(128)S(1)} %stack.23.where_ref, ...), custom_call_target="tpu_custom_call" | custom-call | flops 2717908992 | bytes 4194304 | tf_op jit(solution)/shard_map/pallas_call | solution.py:219
  46.9 3.0 %collective-permute-start.12 = (bf16[256,1152]{1,0:T(8,128)(2,1)S(1)}, bf16[256,1152]{1,0:T(8,128)(2,1)S(1)}, u32[]{:S(2)}, u32[]{:S(2)}) collective-permute-start(bf16[256,1152]{1,0:T(8,128)(2,1)S(1)} %get-tuple-element.39), channel_id=1, source_target_pairs={{0,4},{8,10},{16,20},{24,26},{32,36},{40,42},{48,52},{56,58},{64,6... | collective-permute-start | bytes 1769480 | tf_op jit(solution)/shard_map/ppermute | solution.py:35
  50.3 2.3 %collective-permute-start.14 = (bf16[256,1152]{1,0:T(8,128)(2,1)S(1)}, bf16[256,1152]{1,0:T(8,128)(2,1)S(1)}, u32[]{:S(2)}, u32[]{:S(2)}) collective-permute-start(bf16[256,1152]{1,0:T(8,128)(2,1)S(1)} %get-tuple-element.41), channel_id=1, source_target_pairs={{0,132},{8,11},{16,148},{24,27},{32,164},{40,43},{48,180},{56,59},... | collective-permute-start | bytes 1769480 | tf_op jit(solution)/shard_map/ppermute | solution.py:35
  52.7 2.5 %collective-permute-start.22 = (bf16[64,1152]{1,0:T(8,128)(2,1)S(1)}, bf16[64,1152]{1,0:T(8,128)(2,1)S(1)}, u32[]{:S(2)}, u32[]{:S(2)}) collective-permute-start(bf16[64,1152]{1,0:T(8,128)(2,1)S(1)} %fusion.4), channel_id=1, source_target_pairs={{0,32},{8,104},{16,48},{24,120},{32,64},{40,8},{48,80},{56,24},{64... | collective-permute-start | bytes 442376 | tf_op jit(solution)/shard_map/ppermute | solution.py:35
  55.3 2.2 %collective-permute-done.12 = bf16[256,1152]{1,0:T(8,128)(2,1)S(1)} collective-permute-done((bf16[256,1152]{1,0:T(8,128)(2,1)S(1)}, bf16[256,1152]{1,0:T(8,128)(2,1)S(1)}, u32[]{:S(2)}, u32[]{:S(2)}) %collective-permute-start.12) | collective-permute-done | bytes 589856 | tf_op jit(solution)/shard_map/ppermute | solution.py:35
  57.5 1.6 %collective-permute-start.21 = (bf16[128,1152]{1,0:T(8,128)(2,1)S(1)}, bf16[128,1152]{1,0:T(8,128)(2,1)S(1)}, u32[]{:S(2)}, u32[]{:S(2)}) collective-permute-start(bf16[128,1152]{1,0:T(8,128)(2,1)S(1)} %fusion), channel_id=1, source_target_pairs={{0,16},{8,120},{16,32},{24,8},{32,48},{40,24},{48,64},{56,40},{64,... | collective-permute-start | bytes 884744 | tf_op jit(solution)/shard_map/ppermute | solution.py:35
  59.2 4.6 %collective-permute-done.13 = bf16[256,1152]{1,0:T(8,128)(2,1)S(1)} collective-permute-done((bf16[256,1152]{1,0:T(8,128)(2,1)S(1)}, bf16[256,1152]{1,0:T(8,128)(2,1)S(1)}, u32[]{:S(2)}, u32[]{:S(2)}) %collective-permute-start.13) | collective-permute-done | bytes 589856 | tf_op jit(solution)/shard_map/ppermute | solution.py:35
  64.7 2.5 %collective-permute-start.23 = (bf16[128,1152]{1,0:T(8,128)(2,1)S(1)}, bf16[128,1152]{1,0:T(8,128)(2,1)S(1)}, u32[]{:S(2)}, u32[]{:S(2)}) collective-permute-start(bf16[128,1152]{1,0:T(8,128)(2,1)S(1)} %pad_maximum_fusion), channel_id=1, source_target_pairs={{0,32},{8,104},{16,48},{24,120},{32,64},{40,8},{48,80},{56,24},{64... | collective-permute-start | bytes 884744 | tf_op jit(solution)/shard_map/ppermute | solution.py:35
  67.3 2.1 %collective-permute-start.15 = (bf16[64,1152]{1,0:T(8,128)(2,1)S(1)}, bf16[64,1152]{1,0:T(8,128)(2,1)S(1)}, u32[]{:S(2)}, u32[]{:S(2)}) collective-permute-start(bf16[64,1152]{1,0:T(8,128)(2,1)S(1)} %get-tuple-element.54), channel_id=1, source_target_pairs={{0,2},{8,12},{16,18},{24,28},{32,34},{40,44},{48,50},{56,60},{64,6... | collective-permute-start | bytes 442376 | tf_op jit(solution)/shard_map/ppermute | solution.py:35
  72.1 2.7 %collective-permute-done.23 = bf16[128,1152]{1,0:T(8,128)(2,1)S(1)} collective-permute-done((bf16[128,1152]{1,0:T(8,128)(2,1)S(1)}, bf16[128,1152]{1,0:T(8,128)(2,1)S(1)}, u32[]{:S(2)}, u32[]{:S(2)}) %collective-permute-start.23) | collective-permute-done | bytes 294944 | tf_op jit(solution)/shard_map/ppermute | solution.py:35
  74.9 3.5 %collective-permute-start.24 = (bf16[64,1152]{1,0:T(8,128)(2,1)S(1)}, bf16[64,1152]{1,0:T(8,128)(2,1)S(1)}, u32[]{:S(2)}, u32[]{:S(2)}) collective-permute-start(bf16[64,1152]{1,0:T(8,128)(2,1)S(1)} %fusion.1), channel_id=1, source_target_pairs={{0,8},{8,0},{16,24},{24,16},{32,40},{40,32},{48,56},{56,48},{64,72... | collective-permute-start | bytes 442376 | tf_op jit(solution)/shard_map/ppermute | solution.py:35
  (53 shorter events, 10.8 us)
Async XLA Ops:
  3.4 22.7 %collective-permute-start = (bf16[272,1152]{1,0:T(8,128)(2,1)S(1)}, bf16[272,1152]{1,0:T(8,128)(2,1)S(1)}, u32[]{:S(2)}, u32[]{:S(2)}) collective-permute-start(bf16[272,1152]{1,0:T(8,128)(2,1)S(1)} %get-tuple-element.26.refs_0_), channel_id=1, source_target_pairs={{0,132},{8,140},{16,148},{24,156},{32,164},{40,172},{48,180},{56,1... | collective-permute-start | bytes 1880072 | tf_op jit(solution)/shard_map/ppermute | solution.py:35
  6.8 21.1 %collective-permute-start.5 = (bf16[272,1152]{1,0:T(8,128)(2,1)S(1)}, bf16[272,1152]{1,0:T(8,128)(2,1)S(1)}, u32[]{:S(2)}, u32[]{:S(2)}) collective-permute-start(bf16[272,1152]{1,0:T(8,128)(2,1)S(1)} %get-tuple-element.26.refs_0_), channel_id=1, source_target_pairs={{0,128},{8,136},{16,144},{24,152},{32,160},{40,168},{48,176},{56,1... | collective-permute-start | bytes 1880072 | tf_op jit(solution)/shard_map/ppermute | solution.py:35
  9.8 9.1 %collective-permute-start.3 = (bf16[128,1152]{1,0:T(8,128)(2,1)S(1)}, bf16[128,1152]{1,0:T(8,128)(2,1)S(1)}, u32[]{:S(2)}, u32[]{:S(2)}) collective-permute-start(bf16[128,1152]{1,0:T(8,128)(2,1)S(1)} %constant_dynamic-update-slice_fusion), channel_id=1, source_target_pairs={{0,112},{8,24},{16,0},{24,40},{32,16},{40,56},{48,32},{56,72},{64,... | collective-permute-start | bytes 884744 | tf_op jit(solution)/shard_map/ppermute | solution.py:35
  10.5 13.0 %collective-permute-start.2 = (bf16[128,1152]{1,0:T(8,128)(2,1)S(1)}, bf16[128,1152]{1,0:T(8,128)(2,1)S(1)}, u32[]{:S(2)}, u32[]{:S(2)}) collective-permute-start(bf16[128,1152]{1,0:T(8,128)(2,1)S(1)} %constant_dynamic-update-slice_fusion), channel_id=1, source_target_pairs={{0,96},{8,40},{16,112},{24,56},{32,0},{40,72},{48,16},{56,88},{64,... | collective-permute-start | bytes 884744 | tf_op jit(solution)/shard_map/ppermute | solution.py:35
  18.8 4.7 %collective-permute-start.4 = (bf16[128,1152]{1,0:T(8,128)(2,1)S(1)}, bf16[128,1152]{1,0:T(8,128)(2,1)S(1)}, u32[]{:S(2)}, u32[]{:S(2)}) collective-permute-start(bf16[128,1152]{1,0:T(8,128)(2,1)S(1)} %collective-permute-done.3.refs_6_), channel_id=1, source_target_pairs={{0,8},{8,0},{16,24},{24,16},{32,40},{40,32},{48,56},{56,48},{64,72... | collective-permute-start | bytes 884744 | tf_op jit(solution)/shard_map/ppermute | solution.py:35
  23.5 12.1 %collective-permute-start.6 = (bf16[128,1152]{1,0:T(8,128)(2,1)S(1)}, bf16[128,1152]{1,0:T(8,128)(2,1)S(1)}, u32[]{:S(2)}, u32[]{:S(2)}) collective-permute-start(bf16[128,1152]{1,0:T(8,128)(2,1)S(1)} %collective-permute-done.2.refs_3_), channel_id=1, source_target_pairs={{0,8},{8,0},{16,24},{24,16},{32,40},{40,32},{48,56},{56,48},{64,72... | collective-permute-start | bytes 884744 | tf_op jit(solution)/shard_map/ppermute | solution.py:35
  25.7 13.4 %collective-permute-start.8 = (bf16[128,1152]{1,0:T(8,128)(2,1)S(1)}, bf16[128,1152]{1,0:T(8,128)(2,1)S(1)}, u32[]{:S(2)}, u32[]{:S(2)}) collective-permute-start(bf16[128,1152]{1,0:T(8,128)(2,1)S(1)} %collective-permute-done.2.refs_3_), channel_id=1, source_target_pairs={{0,112},{8,24},{16,0},{24,40},{32,16},{40,56},{48,32},{56,72},{64,... | collective-permute-start | bytes 884744 | tf_op jit(solution)/shard_map/ppermute | solution.py:35
  26.1 9.6 %collective-permute-start.10 = (bf16[64,1152]{1,0:T(8,128)(2,1)S(1)}, bf16[64,1152]{1,0:T(8,128)(2,1)S(1)}, u32[]{:S(2)}, u32[]{:S(2)}) collective-permute-start(bf16[64,1152]{1,0:T(8,128)(2,1)S(1)} %slice.42), channel_id=1, source_target_pairs={{0,96},{8,40},{16,112},{24,56},{32,0},{40,72},{48,16},{56,88},{64,... | collective-permute-start | bytes 442376 | tf_op jit(solution)/shard_map/ppermute | solution.py:35
  32.1 7.1 %collective-permute-start.7 = (bf16[128,1152]{1,0:T(8,128)(2,1)S(1)}, bf16[128,1152]{1,0:T(8,128)(2,1)S(1)}, u32[]{:S(2)}, u32[]{:S(2)}) collective-permute-start(bf16[128,1152]{1,0:T(8,128)(2,1)S(1)} %get-tuple-element.36), channel_id=1, source_target_pairs={{0,8},{8,0},{16,24},{24,16},{32,40},{40,32},{48,56},{56,48},{64,72... | collective-permute-start | bytes 884744 | tf_op jit(solution)/shard_map/ppermute | solution.py:35
  35.6 6.8 %collective-permute-start.11 = (bf16[64,1152]{1,0:T(8,128)(2,1)S(1)}, bf16[64,1152]{1,0:T(8,128)(2,1)S(1)}, u32[]{:S(2)}, u32[]{:S(2)}) collective-permute-start(bf16[64,1152]{1,0:T(8,128)(2,1)S(1)} %collective-permute-done.10.refs_5_), channel_id=1, source_target_pairs={{0,8},{8,0},{16,24},{24,16},{32,40},{40,32},{48,56},{56,48},{64,72... | collective-permute-start | bytes 442376 | tf_op jit(solution)/shard_map/ppermute | solution.py:35
  38.5 11.8 %collective-permute-start.19 = (bf16[128,1152]{1,0:T(8,128)(2,1)S(1)}, bf16[128,1152]{1,0:T(8,128)(2,1)S(1)}, u32[]{:S(2)}, u32[]{:S(2)}) collective-permute-start(bf16[128,1152]{1,0:T(8,128)(2,1)S(1)} %get-tuple-element.44), channel_id=1, source_target_pairs={{0,8},{8,0},{16,24},{24,16},{32,40},{40,32},{48,56},{56,48},{64,72... | collective-permute-start | bytes 884744 | tf_op jit(solution)/shard_map/ppermute | solution.py:35
  39.1 3.3 %collective-permute-start.9 = (bf16[128,1152]{1,0:T(8,128)(2,1)S(1)}, bf16[128,1152]{1,0:T(8,128)(2,1)S(1)}, u32[]{:S(2)}, u32[]{:S(2)}) collective-permute-start(bf16[128,1152]{1,0:T(8,128)(2,1)S(1)} %collective-permute-done.8.refs_3_), channel_id=1, source_target_pairs={{0,8},{8,0},{16,24},{24,16},{32,40},{40,32},{48,56},{56,48},{64,72... | collective-permute-start | bytes 884744 | tf_op jit(solution)/shard_map/ppermute | solution.py:35
  39.3 32.8 %collective-permute-start.18 = (bf16[128,1152]{1,0:T(8,128)(2,1)S(1)}, bf16[128,1152]{1,0:T(8,128)(2,1)S(1)}, u32[]{:S(2)}, u32[]{:S(2)}) collective-permute-start(bf16[128,1152]{1,0:T(8,128)(2,1)S(1)} %add_convert_fusion), channel_id=1, source_target_pairs={{0,16},{8,120},{16,32},{24,8},{32,48},{40,24},{48,64},{56,40},{64,... | collective-permute-start | bytes 884744 | tf_op jit(solution)/shard_map/ppermute | solution.py:35
  46.8 5.8 %collective-permute-start.20 = (bf16[192,1152]{1,0:T(8,128)(2,1)S(1)}, bf16[192,1152]{1,0:T(8,128)(2,1)S(1)}, u32[]{:S(2)}, u32[]{:S(2)}) collective-permute-start(bf16[192,1152]{1,0:T(8,128)(2,1)S(1)} %get-tuple-element.46), channel_id=1, source_target_pairs={{0,8},{8,0},{16,24},{24,16},{32,40},{40,32},{48,56},{56,48},{64,72... | collective-permute-start | bytes 1327112 | tf_op jit(solution)/shard_map/ppermute | solution.py:35
  46.9 10.7 %collective-permute-start.12 = (bf16[256,1152]{1,0:T(8,128)(2,1)S(1)}, bf16[256,1152]{1,0:T(8,128)(2,1)S(1)}, u32[]{:S(2)}, u32[]{:S(2)}) collective-permute-start(bf16[256,1152]{1,0:T(8,128)(2,1)S(1)} %get-tuple-element.39), channel_id=1, source_target_pairs={{0,4},{8,10},{16,20},{24,26},{32,36},{40,42},{48,52},{56,58},{64,6... | collective-permute-start | bytes 1769480 | tf_op jit(solution)/shard_map/ppermute | solution.py:35
  49.9 13.9 %collective-permute-start.13 = (bf16[256,1152]{1,0:T(8,128)(2,1)S(1)}, bf16[256,1152]{1,0:T(8,128)(2,1)S(1)}, u32[]{:S(2)}, u32[]{:S(2)}) collective-permute-start(bf16[256,1152]{1,0:T(8,128)(2,1)S(1)} %get-tuple-element.40), channel_id=1, source_target_pairs={{0,128},{8,9},{16,144},{24,25},{32,160},{40,41},{48,176},{56,57},{... | collective-permute-start | bytes 1769480 | tf_op jit(solution)/shard_map/ppermute | solution.py:35
  50.3 13.9 %collective-permute-start.14 = (bf16[256,1152]{1,0:T(8,128)(2,1)S(1)}, bf16[256,1152]{1,0:T(8,128)(2,1)S(1)}, u32[]{:S(2)}, u32[]{:S(2)}) collective-permute-start(bf16[256,1152]{1,0:T(8,128)(2,1)S(1)} %get-tuple-element.41), channel_id=1, source_target_pairs={{0,132},{8,11},{16,148},{24,27},{32,164},{40,43},{48,180},{56,59},... | collective-permute-start | bytes 1769480 | tf_op jit(solution)/shard_map/ppermute | solution.py:35
  52.7 11.8 %collective-permute-start.22 = (bf16[64,1152]{1,0:T(8,128)(2,1)S(1)}, bf16[64,1152]{1,0:T(8,128)(2,1)S(1)}, u32[]{:S(2)}, u32[]{:S(2)}) collective-permute-start(bf16[64,1152]{1,0:T(8,128)(2,1)S(1)} %fusion.4), channel_id=1, source_target_pairs={{0,32},{8,104},{16,48},{24,120},{32,64},{40,8},{48,80},{56,24},{64... | collective-permute-start | bytes 442376 | tf_op jit(solution)/shard_map/ppermute | solution.py:35
  57.5 7.0 %collective-permute-start.21 = (bf16[128,1152]{1,0:T(8,128)(2,1)S(1)}, bf16[128,1152]{1,0:T(8,128)(2,1)S(1)}, u32[]{:S(2)}, u32[]{:S(2)}) collective-permute-start(bf16[128,1152]{1,0:T(8,128)(2,1)S(1)} %fusion), channel_id=1, source_target_pairs={{0,16},{8,120},{16,32},{24,8},{32,48},{40,24},{48,64},{56,40},{64,... | collective-permute-start | bytes 884744 | tf_op jit(solution)/shard_map/ppermute | solution.py:35
  64.7 10.1 %collective-permute-start.23 = (bf16[128,1152]{1,0:T(8,128)(2,1)S(1)}, bf16[128,1152]{1,0:T(8,128)(2,1)S(1)}, u32[]{:S(2)}, u32[]{:S(2)}) collective-permute-start(bf16[128,1152]{1,0:T(8,128)(2,1)S(1)} %pad_maximum_fusion), channel_id=1, source_target_pairs={{0,32},{8,104},{16,48},{24,120},{32,64},{40,8},{48,80},{56,24},{64... | collective-permute-start | bytes 884744 | tf_op jit(solution)/shard_map/ppermute | solution.py:35
  67.3 11.1 %collective-permute-start.15 = (bf16[64,1152]{1,0:T(8,128)(2,1)S(1)}, bf16[64,1152]{1,0:T(8,128)(2,1)S(1)}, u32[]{:S(2)}, u32[]{:S(2)}) collective-permute-start(bf16[64,1152]{1,0:T(8,128)(2,1)S(1)} %get-tuple-element.54), channel_id=1, source_target_pairs={{0,2},{8,12},{16,18},{24,28},{32,34},{40,44},{48,50},{56,60},{64,6... | collective-permute-start | bytes 442376 | tf_op jit(solution)/shard_map/ppermute | solution.py:35
  69.4 9.0 %collective-permute-start.16 = (bf16[64,1152]{1,0:T(8,128)(2,1)S(1)}, bf16[64,1152]{1,0:T(8,128)(2,1)S(1)}, u32[]{:S(2)}, u32[]{:S(2)}) collective-permute-start(bf16[64,1152]{1,0:T(8,128)(2,1)S(1)} %get-tuple-element.56), channel_id=1, source_target_pairs={{0,1},{8,136},{16,17},{24,152},{32,33},{40,168},{48,49},{56,184},{... | collective-permute-start | bytes 442376 | tf_op jit(solution)/shard_map/ppermute | solution.py:35
  70.9 7.5 %collective-permute-start.17 = (bf16[64,1152]{1,0:T(8,128)(2,1)S(1)}, bf16[64,1152]{1,0:T(8,128)(2,1)S(1)}, u32[]{:S(2)}, u32[]{:S(2)}) collective-permute-start(bf16[64,1152]{1,0:T(8,128)(2,1)S(1)} %get-tuple-element.55), channel_id=1, source_target_pairs={{0,3},{8,140},{16,19},{24,156},{32,35},{40,172},{48,51},{56,188},{... | collective-permute-start | bytes 442376 | tf_op jit(solution)/shard_map/ppermute | solution.py:35
  74.9 4.5 %collective-permute-start.24 = (bf16[64,1152]{1,0:T(8,128)(2,1)S(1)}, bf16[64,1152]{1,0:T(8,128)(2,1)S(1)}, u32[]{:S(2)}, u32[]{:S(2)}) collective-permute-start(bf16[64,1152]{1,0:T(8,128)(2,1)S(1)} %fusion.1), channel_id=1, source_target_pairs={{0,8},{8,0},{16,24},{24,16},{32,40},{40,32},{48,56},{56,48},{64,72... | collective-permute-start | bytes 442376 | tf_op jit(solution)/shard_map/ppermute | solution.py:35
  (3 other events, 23.8 us)

commit v3 on v2

v3 whole, which is shorter than its diff:
```python
import functools

import jax
import jax.numpy as jnp
from jax import lax
from jax.experimental import pallas as pl
from jax.experimental.pallas import tpu as pltpu
from jax.sharding import PartitionSpec as P

logit_bias = -6.0
Z, C, X, Y = 8, 2, 4, 4
AXES = ("block", "lane")
ROWS = 512
SHARE = 64
low = jnp.bfloat16
f32 = jnp.float32
MIB = 1 << 20
ORDER = (2, 1, 3, 0)
VMEM = pl.BlockSpec(memory_space=pltpu.VMEM)
HBM = pl.BlockSpec(memory_space=pltpu.HBM)


def flat(x, y, z, c):
    return (((x % 2) * Z + z) * C + c) * (X // 2 * Y) + (x // 2) * Y + y


def send(value, step):
    pairs = []
    for x in range(X):
        for y in range(Y):
            for z in range(Z):
                for c in range(C):
                    dx, dy, dz, dc = step(c)
                    to = flat((x + dx) % X, (y + dy) % Y, (z + dz) % Z, (c + dc) % C)
                    pairs.append((flat(x, y, z, c), to))
    return lax.ppermute(value, AXES, pairs)


def to_core(value):
    return send(value, lambda c: (0, 0, 0, 1))


def to_x(value, d):
    return send(value, lambda c: (d, 0, 0, 0))


def to_z(value, d):
    return send(value, lambda c: (0, 0, -d if c else d, 0))


def first_stage(value, d):
    return send(value, lambda c: (0, d, 0, 0) if c else (d, 0, 0, 0))


def second_stage(value, d):
    return send(value, lambda c: (d, 0, 0, 0) if c else (0, d, 0, 0))


def place():
    block = lax.axis_index("block")
    lane = lax.axis_index("lane")
    return block // 16, block // 2 % 8, block % 2, lane // 4, lane % 4


def prep_kernel(far, where_ref, images_ref, labels_ref, image_out, held, sems):
    xh, y = where_ref[3], where_ref[4]
    half = 1 - xh if far else xh
    copies = []
    for i in range(Y):
        row = pl.multiple_of((half * Y + lax.rem(y + i, Y)) * SHARE, SHARE)
        copy = pltpu.make_async_copy(images_ref.at[pl.ds(row, SHARE)], held.at[i], sems.at[i])
        copy.start()
        copies.append(copy)
    labels = jnp.concatenate([labels_ref[pl.ds(2 * half, 1), :], labels_ref[pl.ds(2 * half + 1, 1), :]], axis=1)
    labels = jnp.broadcast_to(labels, (16, 256))
    labels = pltpu.roll(labels, lax.rem(Y - y, Y) * SHARE, 1)
    row = lax.broadcasted_iota(jnp.int32, (16, 256), 0)
    digits = jnp.where(row == 0, labels >> 7, jnp.where(row == 1, labels & 127, 0))
    image_out[256:272, :256] = digits.astype(f32).astype(low)
    image_out[256:272, 256:] = jnp.zeros((16, image_out.shape[1] - 256), low)
    for i in range(Y):
        copies[i].wait()
        image_out[i * SHARE : (i + 1) * SHARE, :] = held[i].astype(low)


def prep(where, images, labels, far):
    width = images.shape[1]
    return pl.pallas_call(
        functools.partial(prep_kernel, far),
        out_shape=jax.ShapeDtypeStruct((272, width), low),
        in_specs=[pl.BlockSpec(memory_space=pltpu.SMEM), HBM, VMEM],
        out_specs=VMEM,
        scratch_shapes=[pltpu.VMEM((Y, SHARE, width), f32), pltpu.SemaphoreType.DMA((Y,))],
        compiler_params=pltpu.CompilerParams(vmem_limit_bytes=52 * MIB),
        cost_estimate=pl.CostEstimate(flops=0, bytes_accessed=3 << 20, transcendentals=0),
    )(where, images, labels)


def text_kernel(where_ref, texts_ref, text_out, held, sem):
    row = pl.multiple_of((where_ref[3] * Y + where_ref[4]) * SHARE, SHARE)
    copy = pltpu.make_async_copy(texts_ref.at[pl.ds(row, SHARE)], held, sem)
    copy.start()
    copy.wait()
    text_out[...] = held[...].astype(low)


def own_text(where, texts):
    width = texts.shape[1]
    return pl.pallas_call(
        text_kernel,
        out_shape=jax.ShapeDtypeStruct((SHARE, width), low),
        in_specs=[pl.BlockSpec(memory_space=pltpu.SMEM), HBM],
        out_specs=VMEM,
        scratch_shapes=[pltpu.VMEM((SHARE, width), f32), pltpu.SemaphoreType.DMA],
        compiler_params=pltpu.CompilerParams(vmem_limit_bytes=52 * MIB),
        cost_estimate=pl.CostEstimate(flops=0, bytes_accessed=1 << 19, transcendentals=0),
    )(where, texts)


def arrange(where_ref, parts, images_ref, labels_ref):
    labels = []
    for part in parts:
        digits = part[256:272, :256].astype(f32)
        labels.append(digits[0:1] * 128.0 + digits[1:2])
    core = where_ref[2]

    @pl.when(core == 0)
    def _():
        for k, d in enumerate(ORDER):
            images_ref[k * 256 : (k + 1) * 256, :] = parts[d][:256, :]
            labels_ref[:, k * 256 : (k + 1) * 256] = jnp.broadcast_to(labels[d], (8, 256))

    @pl.when(core == 1)
    def _():
        for k, d in enumerate(ORDER):
            cut = slice(d * SHARE, (d + 1) * SHARE)
            for a in range(4):
                start = k * 256 + a * SHARE
                images_ref[start : start + SHARE, :] = parts[a][cut, :]
            row = jnp.concatenate([labels[a][:, cut] for a in range(4)], axis=1)
            labels_ref[:, k * 256 : (k + 1) * 256] = jnp.broadcast_to(row, (8, 256))


def text_numbers(where_ref, group):
    xl, z, c, xh, y = (where_ref[i] for i in range(5))
    sign = 1 - 2 * c
    numbers = [[], []]
    for d in group:
        for side in range(2):
            if d in (0, 4):
                cores = (c,) if side == 0 else (1 - c,)
                chip = lax.rem(z + d, Z)
            else:
                cores = (c, 1 - c) if side == 0 else (1 - c, c)
                chip = lax.rem(z + Z + sign * (d if side == 0 else -d), Z)
            for core in cores:
                start = ((xl * Z + chip) * C + core) * ROWS + (xh * Y + y) * SHARE
                numbers[side].append(lax.broadcasted_iota(jnp.int32, (SHARE, 1), 0) + start)
    return jnp.concatenate(numbers[0] + numbers[1], axis=0).astype(f32)


def tile_kernel(group, kind, gives, where_ref, *refs):
    refs = list(refs)
    take = lambda count: [refs.pop(0) for _ in range(count)]
    if kind == "first":
        parts = take(4)
    else:
        images_ref, labels_ref, held = take(3)
    texts = take(2 * len(group))
    if kind == "first":
        images_ref, labels_ref = take(2)
        arrange(where_ref, parts, images_ref, labels_ref)
    image_outs = take(4 if kind == "last" else 1)
    term_refs = take(len(group) + gives)
    text_ref, weight_ref = refs
    at = 0
    for side in range(2):
        for i in range(len(group)):
            piece = texts[2 * i + side]
            text_ref[at : at + piece.shape[0], :] = piece[...]
            at += piece.shape[0]
    numbers = text_numbers(where_ref, group)
    text = text_ref[...]
    for a in range(0, 1024, 256):
        cut = slice(a, a + 256)
        logits = (
            lax.dot_general(text, images_ref[cut, :], (((1,), (1,)), ((), ())), preferred_element_type=f32)
            + logit_bias
        )
        positive = (labels_ref[0:1, cut] == numbers).astype(f32)
        weight_ref[:, cut] = (jax.nn.sigmoid(logits) - positive).astype(low)
    total = lax.dot_general(weight_ref[...], text, (((0,), (0,)), ((), ())), preferred_element_type=f32)
    if kind != "first":
        total = total + held[...]
    if kind == "last":
        for k, ref in enumerate(image_outs):
            ref[...] = total[k * 256 : (k + 1) * 256].astype(low)
    else:
        image_outs[0][...] = total
    term = jnp.dot(weight_ref[...], images_ref[...], preferred_element_type=f32)
    at = 0
    for ref in term_refs:
        ref[...] = term[at : at + ref.shape[0]].astype(ref.dtype)
        at += ref.shape[0]


def tile(where, args, group, kind, sizes, give_sizes):
    width = args[0].shape[1]
    n = 2 * sum(sizes)
    shape = jax.ShapeDtypeStruct
    outs = []
    if kind == "first":
        outs += [shape((1024, width), low), shape((8, 1024), f32)]
    if kind == "last":
        outs += [shape((256, width), low)] * 4
    else:
        outs += [shape((1024, width), f32)]
    outs += [shape((size, width), f32) for size in sizes]
    outs += [shape((size, width), low) for size in give_sizes]
    return pl.pallas_call(
        functools.partial(tile_kernel, group, kind, len(give_sizes)),
        out_shape=tuple(outs),
        in_specs=[pl.BlockSpec(memory_space=pltpu.SMEM)] + [VMEM] * len(args),
        out_specs=(VMEM,) * len(outs),
        scratch_shapes=[pltpu.VMEM((n, width), low), pltpu.VMEM((n, 1024), low)],
        compiler_params=pltpu.CompilerParams(vmem_limit_bytes=28 * MIB),
        cost_estimate=pl.CostEstimate(
            flops=18 * 1024 * n * width, bytes_accessed=4 << 20, transcendentals=1024 * n
        ),
    )(where, *args)


def after(value, *others):
    return lax.optimization_barrier((value, *others))[0]


def on_device(images, texts, labels):
    where = jnp.stack(place()).astype(jnp.int32)
    label_rows = labels.reshape(4, 128)
    text_own = own_text(where, texts)
    text_other = to_core(text_own)
    image_near = prep(where, images, label_rows, False)
    chunk = jnp.concatenate([text_own, text_other], axis=0)
    arrived_2 = to_z(chunk, -2)
    image_near = after(image_near, chunk)
    image_right = to_x(image_near, -1)
    image_left = to_x(image_near, 1)
    arrived_1 = to_z(chunk, -1)
    swapped_1 = to_core(arrived_1)
    image_far = prep(where, images, label_rows, True)
    arrived_2 = after(arrived_2, swapped_1, image_far)
    arrived_3 = to_z(arrived_2, -1)
    arrived_4 = to_z(arrived_2[:SHARE], -2)
    swapped_2 = to_core(after(arrived_2, image_right, image_left))

    args = (image_near, after(image_right, arrived_2), image_far, image_left)
    args += (text_own, text_other, arrived_1, swapped_1)
    image_rows, label_row, held, own_keep, keep_1, own_give, give_1 = tile(
        where, args, (0, 1), "first", (SHARE, 2 * SHARE), (SHARE, 2 * SHARE)
    )
    args = (image_rows, label_row, held, arrived_2, swapped_2)
    held, keep_2, give_2 = tile(where, args, (2,), "middle", (2 * SHARE,), (2 * SHARE,))
    arrived_3 = after(arrived_3, held)
    arrived_4 = after(arrived_4, held)
    swapped_4 = to_core(arrived_4)
    swapped_3 = to_core(arrived_3)
    term_1 = (keep_1 + to_core(give_1).astype(f32)).astype(low)

    term_2 = keep_2 + to_core(give_2).astype(f32)
    held, term_1 = lax.optimization_barrier((held, term_1))
    args = (image_rows, label_row, held, arrived_3, swapped_3, arrived_4, swapped_4)
    sizes = (2 * SHARE, SHARE)
    image_2, image_1, image_3, image_0, keep_3, keep_4, give_3, give_4 = tile(
        where, args, (3, 4), "last", sizes, sizes
    )
    from_1 = to_z(term_1, 1)
    back_3, back_4 = to_core(give_3), to_core(give_4)
    back_3, back_4 = after(back_3, from_1), after(back_4, from_1)
    from_3 = to_z((keep_3 + back_3.astype(f32)).astype(low), 1).astype(f32)
    from_4 = to_z((keep_4 + back_4.astype(f32)).astype(low), 2).astype(f32)
    upper = term_2[:SHARE] + from_3[:SHARE] + from_4
    lower = term_2[SHARE:] + from_3[SHARE:]
    term_2 = jnp.concatenate([upper, lower], axis=0).astype(low)
    parts = from_1.astype(f32) + to_z(term_2, 2).astype(f32)

    state = (image_0, image_1, image_2, image_3)
    arrived = [first_stage(state[d], d) for d in (2, 1, 3)]
    arrived = list(lax.optimization_barrier((*arrived, term_2))[:3])
    image_sum = state[0].astype(f32)
    for value in arrived:
        image_sum = image_sum + value.astype(f32)
    image_out = image_sum[:SHARE]
    for d in (2, 1, 3):
        piece = image_sum[d * SHARE : (d + 1) * SHARE].astype(low)
        image_out = image_out + second_stage(piece, d).astype(f32)

    give = (parts[SHARE:] + own_give.astype(f32)).astype(low)
    text_out = parts[:SHARE] + own_keep + to_core(give).astype(f32)
    return image_out, text_out


def solution(mesh):
    placed = (P("block", None), P("block", None), P("block"))
    return jax.shard_map(
        on_device,
        mesh=mesh,
        in_specs=placed,
        out_specs=(P(("block", "lane"), None), P(("block", "lane"), None)),
        check_vma=False,
    )
```

time: 80.3 us -> 77 us (0.959)
  starting transfers between devices: 43.3 us -> 40.2 us
  Pallas kernels: 15.2 us -> 16.9 us
  waiting for transfers between devices: 17.6 us -> 16.5 us
    ppermute x25 -> x26, starting transfers between devices: 43.3 us -> 40.2 us  [send(): return lax.ppermute(value, AXES, pairs)]
    pallas_call x5 -> x6, Pallas kernels: 15.2 us -> 16.9 us  [the longest x3 11.7 us: tile(): pl.pallas_call(functools.partial(tile_kernel, group, kind, len(give_sizes...]
    ppermute x25 -> x26, waiting for transfers between devices: 17.6 us -> 16.5 us  [send(): return lax.ppermute(value, AXES, pairs)]
  transfers between devices with their start and end apart: 25 -> 26, of which waited for: 8 -> 5; matrix products, arithmetic and copies ran while one was open for 2% -> 2% of each run, Pallas kernels for 17% -> 20%
where the time goes in v3:
time: 77 us; the launch traced here: 76.9 us
  starting transfers between devices  40.2 us (52%)
  Pallas kernels  16.9 us (22%)
  waiting for transfers between devices  16.5 us (21%)
  other arithmetic  2.27 us (3%)
  between operations  0.88 us (1%)
    ppermute x26, starting transfers between devices, send(): return lax.ppermute(value, AXES, pairs)  40.2 us
    ppermute x26, waiting for transfers between devices, send(): return lax.ppermute(value, AXES, pairs)  16.5 us
    pallas_call x3, Pallas kernels, tile(): pl.pallas_call(functools.partial(tile_kernel, group, kind, len(give_sizes...  11.7 us
    pallas_call x2, Pallas kernels, prep(): pl.pallas_call(functools.partial(prep_kernel, far), out_shape=jax.ShapeDt...  3.66 us
  transfers between devices with their start and end apart: 26, of which 5 were waited for; matrix products, arithmetic and copies ran while one was open for 2% of the time, Pallas kernels for 20%

profile of v3, /device:TPU:1, one launch (start us, length us, event | category | flops | bytes accessed | tf_op | source)
XLA Modules:
  0.0 76.9 jit_solution(10384703080214886906)
XLA Ops:
  0.8 1.5 %shard_map.51.refs_4_ = bf16[64,1152]{1,0:T(8,128)(2,1)S(1)} custom-call(s32[5]{0:T(128)S(1)} %stack.23.where_ref, f32[512,1152]{1,0:T(8,128)} %texts_ref.1), custom_call_target="tpu_custom_call" | custom-call | bytes 524288 | tf_op jit(solution)/shard_map/pallas_call | solution.py:109
  2.3 3.3 %collective-permute-start = (bf16[64,1152]{1,0:T(8,128)(2,1)S(1)}, bf16[64,1152]{1,0:T(8,128)(2,1)S(1)}, u32[]{:S(2)}, u32[]{:S(2)}) collective-permute-start(bf16[64,1152]{1,0:T(8,128)(2,1)S(1)} %shard_map.51.refs_4_), channel_id=1, source_target_pairs={{0,8},{8,0},{16,24},{24,16},{32,40},{40,32},{48,56},{56,48},{64,72... | collective-permute-start | bytes 442376 | tf_op jit(solution)/shard_map/ppermute | solution.py:36
  5.6 1.8 %shard_map.50.refs_0_ = bf16[272,1152]{1,0:T(8,128)(2,1)S(1)} custom-call(s32[5]{0:T(128)S(1)} %stack.23.where_ref, f32[512,1152]{1,0:T(8,128)} %images_ref.3, s32[4,128]{1,0:T(4,128)S(1)} %bitcast.6), custom_call_target="tpu_custom_call" | custom-call | bytes 3145728 | tf_op jit(solution)/shard_map/pallas_call | solution.py:88
  10.0 3.0 %collective-permute-start.2 = (bf16[128,1152]{1,0:T(8,128)(2,1)S(1)}, bf16[128,1152]{1,0:T(8,128)(2,1)S(1)}, u32[]{:S(2)}, u32[]{:S(2)}) collective-permute-start(bf16[128,1152]{1,0:T(8,128)(2,1)S(1)} %pad_maximum_fusion), channel_id=1, source_target_pairs={{0,96},{8,40},{16,112},{24,56},{32,0},{40,72},{48,16},{56,88},{64,... | collective-permute-start | bytes 884744 | tf_op jit(solution)/shard_map/ppermute | solution.py:36
  13.0 5.4 %collective-permute-done.3.refs_6_ = bf16[128,1152]{1,0:T(8,128)(2,1)S(1)} collective-permute-done((bf16[128,1152]{1,0:T(8,128)(2,1)S(1)}, bf16[128,1152]{1,0:T(8,128)(2,1)S(1)}, u32[]{:S(2)}, u32[]{:S(2)}) %collective-permute-start.3) | collective-permute-done | bytes 294944 | tf_op jit(solution)/shard_map/ppermute | solution.py:36
  18.3 2.8 %collective-permute-start.4 = (bf16[128,1152]{1,0:T(8,128)(2,1)S(1)}, bf16[128,1152]{1,0:T(8,128)(2,1)S(1)}, u32[]{:S(2)}, u32[]{:S(2)}) collective-permute-start(bf16[128,1152]{1,0:T(8,128)(2,1)S(1)} %collective-permute-done.3.refs_6_), channel_id=1, source_target_pairs={{0,8},{8,0},{16,24},{24,16},{32,40},{40,32},{48,56},{56,48},{64,72... | collective-permute-start | bytes 884744 | tf_op jit(solution)/shard_map/ppermute | solution.py:36
  21.1 1.8 %shard_map.52.refs_2_ = bf16[272,1152]{1,0:T(8,128)(2,1)S(1)} custom-call(s32[5]{0:T(128)S(1)} %stack.23.where_ref, f32[512,1152]{1,0:T(8,128)} %images_ref.3, s32[4,128]{1,0:T(4,128)S(1)} %bitcast.7), custom_call_target="tpu_custom_call" | custom-call | bytes 3145728 | tf_op jit(solution)/shard_map/pallas_call | solution.py:88
  23.0 2.7 %collective-permute-start.8 = (bf16[128,1152]{1,0:T(8,128)(2,1)S(1)}, bf16[128,1152]{1,0:T(8,128)(2,1)S(1)}, u32[]{:S(2)}, u32[]{:S(2)}) collective-permute-start(bf16[128,1152]{1,0:T(8,128)(2,1)S(1)} %collective-permute-done.2.refs_3_), channel_id=1, source_target_pairs={{0,112},{8,24},{16,0},{24,40},{32,16},{40,56},{48,32},{56,72},{64,... | collective-permute-start | bytes 884744 | tf_op jit(solution)/shard_map/ppermute | solution.py:36
  25.9 3.9 %collective-permute-start.6 = (bf16[128,1152]{1,0:T(8,128)(2,1)S(1)}, bf16[128,1152]{1,0:T(8,128)(2,1)S(1)}, u32[]{:S(2)}, u32[]{:S(2)}) collective-permute-start(bf16[128,1152]{1,0:T(8,128)(2,1)S(1)} %collective-permute-done.2.refs_3_), channel_id=1, source_target_pairs={{0,8},{8,0},{16,24},{24,16},{32,40},{40,32},{48,56},{56,48},{64,72... | collective-permute-start | bytes 884744 | tf_op jit(solution)/shard_map/ppermute | solution.py:36
  29.9 4.4 %shard_map.53 = (bf16[1024,1152]{1,0:T(8,128)(2,1)S(1)}, f32[8,1024]{1,0:T(8,128)S(1)}, f32[1024,1152]{1,0:T(8,128)S(1)}, f32[64,1152]{1,0:T(8,128)S(1)}, f32[12...) custom-call(s32[5]{0:T(128)S(1)} %stack.23.where_ref, ...), custom_call_target="tpu_custom_call" | custom-call | flops 8153726976 | bytes 4194304 | tf_op jit(solution)/shard_map/pallas_call | solution.py:220
  34.6 2.9 %shard_map.54 = (f32[1024,1152]{1,0:T(8,128)S(1)}, f32[128,1152]{1,0:T(8,128)S(1)}, bf16[128,1152]{1,0:T(8,128)(2,1)S(1)}) custom-call(s32[5]{0:T(128)S(1)} %stack.23.where_ref, bf16[1024,1152]{1,0:T(8,128)(2,1)S(1)} %get-tuple-element.36.refs_0_, f32[8,1024]{1,0:T(8,128)S(1)} %get-tuple-element.37.refs_1_, f32[1024,1152]{1,0:T(8,128)S(1)} %get-tuple-element.38.refs_2_, ...), custom_call_target="tpu_custom_call" | custom-call | flops 5435817984 | bytes 4194304 | tf_op jit(solution)/shard_map/pallas_call | solution.py:220
  38.3 1.9 %collective-permute-start.17 = (bf16[128,1152]{1,0:T(8,128)(2,1)S(1)}, bf16[128,1152]{1,0:T(8,128)(2,1)S(1)}, u32[]{:S(2)}, u32[]{:S(2)}) collective-permute-start(bf16[128,1152]{1,0:T(8,128)(2,1)S(1)} %add_convert_fusion.1), channel_id=1, source_target_pairs={{0,16},{8,120},{16,32},{24,8},{32,48},{40,24},{48,64},{56,40},{64,... | collective-permute-start | bytes 884744 | tf_op jit(solution)/shard_map/ppermute | solution.py:36
  40.2 4.3 %shard_map.55 = (bf16[256,1152]{1,0:T(8,128)(2,1)S(1)}, bf16[256,1152]{1,0:T(8,128)(2,1)S(1)}, bf16[256,1152]{1,0:T(8,128)(2,1)S(1)}, bf16[256,1152]{1,0:T(8,128...) custom-call(s32[5]{0:T(128)S(1)} %stack.23.where_ref, ...), custom_call_target="tpu_custom_call" | custom-call | flops 8153726976 | bytes 4194304 | tf_op jit(solution)/shard_map/pallas_call | solution.py:220
  45.6 2.9 %collective-permute-start.12 = (bf16[256,1152]{1,0:T(8,128)(2,1)S(1)}, bf16[256,1152]{1,0:T(8,128)(2,1)S(1)}, u32[]{:S(2)}, u32[]{:S(2)}) collective-permute-start(bf16[256,1152]{1,0:T(8,128)(2,1)S(1)} %get-tuple-element.47), channel_id=1, source_target_pairs={{0,4},{8,10},{16,20},{24,26},{32,36},{40,42},{48,52},{56,58},{64,6... | collective-permute-start | bytes 1769480 | tf_op jit(solution)/shard_map/ppermute | solution.py:36
  48.9 2.3 %collective-permute-start.14 = (bf16[256,1152]{1,0:T(8,128)(2,1)S(1)}, bf16[256,1152]{1,0:T(8,128)(2,1)S(1)}, u32[]{:S(2)}, u32[]{:S(2)}) collective-permute-start(bf16[256,1152]{1,0:T(8,128)(2,1)S(1)} %get-tuple-element.49), channel_id=1, source_target_pairs={{0,132},{8,11},{16,148},{24,27},{32,164},{40,43},{48,180},{56,59},... | collective-permute-start | bytes 1769480 | tf_op jit(solution)/shard_map/ppermute | solution.py:36
  51.3 1.5 %collective-permute-start.20 = (bf16[64,1152]{1,0:T(8,128)(2,1)S(1)}, bf16[64,1152]{1,0:T(8,128)(2,1)S(1)}, u32[]{:S(2)}, u32[]{:S(2)}) collective-permute-start(bf16[64,1152]{1,0:T(8,128)(2,1)S(1)} %add_convert_fusion.2), channel_id=1, source_target_pairs={{0,32},{8,104},{16,48},{24,120},{32,64},{40,8},{48,80},{56,24},{64... | collective-permute-start | bytes 442376 | tf_op jit(solution)/shard_map/ppermute | solution.py:36
  52.9 1.0 %collective-permute-start.18 = (bf16[128,1152]{1,0:T(8,128)(2,1)S(1)}, bf16[128,1152]{1,0:T(8,128)(2,1)S(1)}, u32[]{:S(2)}, u32[]{:S(2)}) collective-permute-start(bf16[128,1152]{1,0:T(8,128)(2,1)S(1)} %add_convert_fusion), channel_id=1, source_target_pairs={{0,16},{8,120},{16,32},{24,8},{32,48},{40,24},{48,64},{56,40},{64,... | collective-permute-start | bytes 884744 | tf_op jit(solution)/shard_map/ppermute | solution.py:36
  53.9 7.2 %collective-permute-done.18 = bf16[128,1152]{1,0:T(8,128)(2,1)S(1)} collective-permute-done((bf16[128,1152]{1,0:T(8,128)(2,1)S(1)}, bf16[128,1152]{1,0:T(8,128)(2,1)S(1)}, u32[]{:S(2)}, u32[]{:S(2)}) %collective-permute-start.18) | collective-permute-done | bytes 294944 | tf_op jit(solution)/shard_map/ppermute | solution.py:36
  61.3 1.3 %collective-permute-start.24 = (bf16[128,1152]{1,0:T(8,128)(2,1)S(1)}, bf16[128,1152]{1,0:T(8,128)(2,1)S(1)}, u32[]{:S(2)}, u32[]{:S(2)}) collective-permute-start(bf16[128,1152]{1,0:T(8,128)(2,1)S(1)} %pad_maximum_fusion.1), channel_id=1, source_target_pairs={{0,32},{8,104},{16,48},{24,120},{32,64},{40,8},{48,80},{56,24},{64... | collective-permute-start | bytes 884744 | tf_op jit(solution)/shard_map/ppermute | solution.py:36
  63.2 2.1 %collective-permute-start.21 = (bf16[64,1152]{1,0:T(8,128)(2,1)S(1)}, bf16[64,1152]{1,0:T(8,128)(2,1)S(1)}, u32[]{:S(2)}, u32[]{:S(2)}) collective-permute-start(bf16[64,1152]{1,0:T(8,128)(2,1)S(1)} %get-tuple-element.68), channel_id=1, source_target_pairs={{0,2},{8,12},{16,18},{24,28},{32,34},{40,44},{48,50},{56,60},{64,6... | collective-permute-start | bytes 442376 | tf_op jit(solution)/shard_map/ppermute | solution.py:36
  65.3 1.5 %collective-permute-start.22 = (bf16[64,1152]{1,0:T(8,128)(2,1)S(1)}, bf16[64,1152]{1,0:T(8,128)(2,1)S(1)}, u32[]{:S(2)}, u32[]{:S(2)}) collective-permute-start(bf16[64,1152]{1,0:T(8,128)(2,1)S(1)} %get-tuple-element.70), channel_id=1, source_target_pairs={{0,1},{8,136},{16,17},{24,152},{32,33},{40,168},{48,49},{56,184},{... | collective-permute-start | bytes 442376 | tf_op jit(solution)/shard_map/ppermute | solution.py:36
  66.8 1.2 %collective-permute-start.23 = (bf16[64,1152]{1,0:T(8,128)(2,1)S(1)}, bf16[64,1152]{1,0:T(8,128)(2,1)S(1)}, u32[]{:S(2)}, u32[]{:S(2)}) collective-permute-start(bf16[64,1152]{1,0:T(8,128)(2,1)S(1)} %get-tuple-element.69), channel_id=1, source_target_pairs={{0,3},{8,140},{16,19},{24,156},{32,35},{40,172},{48,51},{56,188},{... | collective-permute-start | bytes 442376 | tf_op jit(solution)/shard_map/ppermute | solution.py:36
  68.0 3.4 %collective-permute-done.24 = bf16[128,1152]{1,0:T(8,128)(2,1)S(1)} collective-permute-done((bf16[128,1152]{1,0:T(8,128)(2,1)S(1)}, bf16[128,1152]{1,0:T(8,128)(2,1)S(1)}, u32[]{:S(2)}, u32[]{:S(2)}) %collective-permute-start.24) | collective-permute-done | bytes 294944 | tf_op jit(solution)/shard_map/ppermute | solution.py:36
  71.5 3.6 %collective-permute-start.25 = (bf16[64,1152]{1,0:T(8,128)(2,1)S(1)}, bf16[64,1152]{1,0:T(8,128)(2,1)S(1)}, u32[]{:S(2)}, u32[]{:S(2)}) collective-permute-start(bf16[64,1152]{1,0:T(8,128)(2,1)S(1)} %fusion), channel_id=1, source_target_pairs={{0,8},{8,0},{16,24},{24,16},{32,40},{40,32},{48,56},{56,48},{64,72... | collective-permute-start | bytes 442376 | tf_op jit(solution)/shard_map/ppermute | solution.py:36
  (52 shorter events, 8.2 us)
Async XLA Ops:
  2.3 5.2 %collective-permute-start = (bf16[64,1152]{1,0:T(8,128)(2,1)S(1)}, bf16[64,1152]{1,0:T(8,128)(2,1)S(1)}, u32[]{:S(2)}, u32[]{:S(2)}) collective-permute-start(bf16[64,1152]{1,0:T(8,128)(2,1)S(1)} %shard_map.51.refs_4_), channel_id=1, source_target_pairs={{0,8},{8,0},{16,24},{24,16},{32,40},{40,32},{48,56},{56,48},{64,72... | collective-permute-start | bytes 442376 | tf_op jit(solution)/shard_map/ppermute | solution.py:36
  7.5 18.4 %collective-permute-start.1 = (bf16[272,1152]{1,0:T(8,128)(2,1)S(1)}, bf16[272,1152]{1,0:T(8,128)(2,1)S(1)}, u32[]{:S(2)}, u32[]{:S(2)}) collective-permute-start(bf16[272,1152]{1,0:T(8,128)(2,1)S(1)} %shard_map.50.refs_0_), channel_id=1, source_target_pairs={{0,132},{8,140},{16,148},{24,156},{32,164},{40,172},{48,180},{56,1... | collective-permute-start | bytes 1880072 | tf_op jit(solution)/shard_map/ppermute | solution.py:36
  8.3 17.6 %collective-permute-start.5 = (bf16[272,1152]{1,0:T(8,128)(2,1)S(1)}, bf16[272,1152]{1,0:T(8,128)(2,1)S(1)}, u32[]{:S(2)}, u32[]{:S(2)}) collective-permute-start(bf16[272,1152]{1,0:T(8,128)(2,1)S(1)} %shard_map.50.refs_0_), channel_id=1, source_target_pairs={{0,128},{8,136},{16,144},{24,152},{32,160},{40,168},{48,176},{56,1... | collective-permute-start | bytes 1880072 | tf_op jit(solution)/shard_map/ppermute | solution.py:36
  9.1 9.3 %collective-permute-start.3 = (bf16[128,1152]{1,0:T(8,128)(2,1)S(1)}, bf16[128,1152]{1,0:T(8,128)(2,1)S(1)}, u32[]{:S(2)}, u32[]{:S(2)}) collective-permute-start(bf16[128,1152]{1,0:T(8,128)(2,1)S(1)} %pad_maximum_fusion), channel_id=1, source_target_pairs={{0,112},{8,24},{16,0},{24,40},{32,16},{40,56},{48,32},{56,72},{64,... | collective-permute-start | bytes 884744 | tf_op jit(solution)/shard_map/ppermute | solution.py:36
  10.0 12.9 %collective-permute-start.2 = (bf16[128,1152]{1,0:T(8,128)(2,1)S(1)}, bf16[128,1152]{1,0:T(8,128)(2,1)S(1)}, u32[]{:S(2)}, u32[]{:S(2)}) collective-permute-start(bf16[128,1152]{1,0:T(8,128)(2,1)S(1)} %pad_maximum_fusion), channel_id=1, source_target_pairs={{0,96},{8,40},{16,112},{24,56},{32,0},{40,72},{48,16},{56,88},{64,... | collective-permute-start | bytes 884744 | tf_op jit(solution)/shard_map/ppermute | solution.py:36
  18.3 4.6 %collective-permute-start.4 = (bf16[128,1152]{1,0:T(8,128)(2,1)S(1)}, bf16[128,1152]{1,0:T(8,128)(2,1)S(1)}, u32[]{:S(2)}, u32[]{:S(2)}) collective-permute-start(bf16[128,1152]{1,0:T(8,128)(2,1)S(1)} %collective-permute-done.3.refs_6_), channel_id=1, source_target_pairs={{0,8},{8,0},{16,24},{24,16},{32,40},{40,32},{48,56},{56,48},{64,72... | collective-permute-start | bytes 884744 | tf_op jit(solution)/shard_map/ppermute | solution.py:36
  23.0 15.1 %collective-permute-start.8 = (bf16[128,1152]{1,0:T(8,128)(2,1)S(1)}, bf16[128,1152]{1,0:T(8,128)(2,1)S(1)}, u32[]{:S(2)}, u32[]{:S(2)}) collective-permute-start(bf16[128,1152]{1,0:T(8,128)(2,1)S(1)} %collective-permute-done.2.refs_3_), channel_id=1, source_target_pairs={{0,112},{8,24},{16,0},{24,40},{32,16},{40,56},{48,32},{56,72},{64,... | collective-permute-start | bytes 884744 | tf_op jit(solution)/shard_map/ppermute | solution.py:36
  25.6 11.9 %collective-permute-start.10 = (bf16[64,1152]{1,0:T(8,128)(2,1)S(1)}, bf16[64,1152]{1,0:T(8,128)(2,1)S(1)}, u32[]{:S(2)}, u32[]{:S(2)}) collective-permute-start(bf16[64,1152]{1,0:T(8,128)(2,1)S(1)} %slice.36), channel_id=1, source_target_pairs={{0,96},{8,40},{16,112},{24,56},{32,0},{40,72},{48,16},{56,88},{64,... | collective-permute-start | bytes 442376 | tf_op jit(solution)/shard_map/ppermute | solution.py:36
  25.9 8.7 %collective-permute-start.6 = (bf16[128,1152]{1,0:T(8,128)(2,1)S(1)}, bf16[128,1152]{1,0:T(8,128)(2,1)S(1)}, u32[]{:S(2)}, u32[]{:S(2)}) collective-permute-start(bf16[128,1152]{1,0:T(8,128)(2,1)S(1)} %collective-permute-done.2.refs_3_), channel_id=1, source_target_pairs={{0,8},{8,0},{16,24},{24,16},{32,40},{40,32},{48,56},{56,48},{64,72... | collective-permute-start | bytes 884744 | tf_op jit(solution)/shard_map/ppermute | solution.py:36
  34.3 3.9 %collective-permute-start.7 = (bf16[128,1152]{1,0:T(8,128)(2,1)S(1)}, bf16[128,1152]{1,0:T(8,128)(2,1)S(1)}, u32[]{:S(2)}, u32[]{:S(2)}) collective-permute-start(bf16[128,1152]{1,0:T(8,128)(2,1)S(1)} %get-tuple-element.42), channel_id=1, source_target_pairs={{0,8},{8,0},{16,24},{24,16},{32,40},{40,32},{48,56},{56,48},{64,72... | collective-permute-start | bytes 884744 | tf_op jit(solution)/shard_map/ppermute | solution.py:36
  38.3 10.2 %collective-permute-start.17 = (bf16[128,1152]{1,0:T(8,128)(2,1)S(1)}, bf16[128,1152]{1,0:T(8,128)(2,1)S(1)}, u32[]{:S(2)}, u32[]{:S(2)}) collective-permute-start(bf16[128,1152]{1,0:T(8,128)(2,1)S(1)} %add_convert_fusion.1), channel_id=1, source_target_pairs={{0,16},{8,120},{16,32},{24,8},{32,48},{40,24},{48,64},{56,40},{64,... | collective-permute-start | bytes 884744 | tf_op jit(solution)/shard_map/ppermute | solution.py:36
  44.5 4.5 %collective-permute-start.19 = (bf16[64,1152]{1,0:T(8,128)(2,1)S(1)}, bf16[64,1152]{1,0:T(8,128)(2,1)S(1)}, u32[]{:S(2)}, u32[]{:S(2)}) collective-permute-start(bf16[64,1152]{1,0:T(8,128)(2,1)S(1)} %get-tuple-element.57), channel_id=1, source_target_pairs={{0,8},{8,0},{16,24},{24,16},{32,40},{40,32},{48,56},{56,48},{64,72... | collective-permute-start | bytes 442376 | tf_op jit(solution)/shard_map/ppermute | solution.py:36
  45.1 7.7 %collective-permute-start.15 = (bf16[128,1152]{1,0:T(8,128)(2,1)S(1)}, bf16[128,1152]{1,0:T(8,128)(2,1)S(1)}, u32[]{:S(2)}, u32[]{:S(2)}) collective-permute-start(bf16[128,1152]{1,0:T(8,128)(2,1)S(1)} %get-tuple-element.51), channel_id=1, source_target_pairs={{0,8},{8,0},{16,24},{24,16},{32,40},{40,32},{48,56},{56,48},{64,72... | collective-permute-start | bytes 884744 | tf_op jit(solution)/shard_map/ppermute | solution.py:36
  45.2 6.0 %collective-permute-start.16 = (bf16[128,1152]{1,0:T(8,128)(2,1)S(1)}, bf16[128,1152]{1,0:T(8,128)(2,1)S(1)}, u32[]{:S(2)}, u32[]{:S(2)}) collective-permute-start(bf16[128,1152]{1,0:T(8,128)(2,1)S(1)} %get-tuple-element.53), channel_id=1, source_target_pairs={{0,8},{8,0},{16,24},{24,16},{32,40},{40,32},{48,56},{56,48},{64,72... | collective-permute-start | bytes 884744 | tf_op jit(solution)/shard_map/ppermute | solution.py:36
  45.6 16.9 %collective-permute-start.12 = (bf16[256,1152]{1,0:T(8,128)(2,1)S(1)}, bf16[256,1152]{1,0:T(8,128)(2,1)S(1)}, u32[]{:S(2)}, u32[]{:S(2)}) collective-permute-start(bf16[256,1152]{1,0:T(8,128)(2,1)S(1)} %get-tuple-element.47), channel_id=1, source_target_pairs={{0,4},{8,10},{16,20},{24,26},{32,36},{40,42},{48,52},{56,58},{64,6... | collective-permute-start | bytes 1769480 | tf_op jit(solution)/shard_map/ppermute | solution.py:36
  48.5 14.0 %collective-permute-start.13 = (bf16[256,1152]{1,0:T(8,128)(2,1)S(1)}, bf16[256,1152]{1,0:T(8,128)(2,1)S(1)}, u32[]{:S(2)}, u32[]{:S(2)}) collective-permute-start(bf16[256,1152]{1,0:T(8,128)(2,1)S(1)} %get-tuple-element.48), channel_id=1, source_target_pairs={{0,128},{8,9},{16,144},{24,25},{32,160},{40,41},{48,176},{56,57},{... | collective-permute-start | bytes 1769480 | tf_op jit(solution)/shard_map/ppermute | solution.py:36
  48.9 13.9 %collective-permute-start.14 = (bf16[256,1152]{1,0:T(8,128)(2,1)S(1)}, bf16[256,1152]{1,0:T(8,128)(2,1)S(1)}, u32[]{:S(2)}, u32[]{:S(2)}) collective-permute-start(bf16[256,1152]{1,0:T(8,128)(2,1)S(1)} %get-tuple-element.49), channel_id=1, source_target_pairs={{0,132},{8,11},{16,148},{24,27},{32,164},{40,43},{48,180},{56,59},... | collective-permute-start | bytes 1769480 | tf_op jit(solution)/shard_map/ppermute | solution.py:36
  51.3 9.9 %collective-permute-start.20 = (bf16[64,1152]{1,0:T(8,128)(2,1)S(1)}, bf16[64,1152]{1,0:T(8,128)(2,1)S(1)}, u32[]{:S(2)}, u32[]{:S(2)}) collective-permute-start(bf16[64,1152]{1,0:T(8,128)(2,1)S(1)} %add_convert_fusion.2), channel_id=1, source_target_pairs={{0,32},{8,104},{16,48},{24,120},{32,64},{40,8},{48,80},{56,24},{64... | collective-permute-start | bytes 442376 | tf_op jit(solution)/shard_map/ppermute | solution.py:36
  52.9 8.2 %collective-permute-start.18 = (bf16[128,1152]{1,0:T(8,128)(2,1)S(1)}, bf16[128,1152]{1,0:T(8,128)(2,1)S(1)}, u32[]{:S(2)}, u32[]{:S(2)}) collective-permute-start(bf16[128,1152]{1,0:T(8,128)(2,1)S(1)} %add_convert_fusion), channel_id=1, source_target_pairs={{0,16},{8,120},{16,32},{24,8},{32,48},{40,24},{48,64},{56,40},{64,... | collective-permute-start | bytes 884744 | tf_op jit(solution)/shard_map/ppermute | solution.py:36
  61.3 10.1 %collective-permute-start.24 = (bf16[128,1152]{1,0:T(8,128)(2,1)S(1)}, bf16[128,1152]{1,0:T(8,128)(2,1)S(1)}, u32[]{:S(2)}, u32[]{:S(2)}) collective-permute-start(bf16[128,1152]{1,0:T(8,128)(2,1)S(1)} %pad_maximum_fusion.1), channel_id=1, source_target_pairs={{0,32},{8,104},{16,48},{24,120},{32,64},{40,8},{48,80},{56,24},{64... | collective-permute-start | bytes 884744 | tf_op jit(solution)/shard_map/ppermute | solution.py:36
  63.2 11.9 %collective-permute-start.21 = (bf16[64,1152]{1,0:T(8,128)(2,1)S(1)}, bf16[64,1152]{1,0:T(8,128)(2,1)S(1)}, u32[]{:S(2)}, u32[]{:S(2)}) collective-permute-start(bf16[64,1152]{1,0:T(8,128)(2,1)S(1)} %get-tuple-element.68), channel_id=1, source_target_pairs={{0,2},{8,12},{16,18},{24,28},{32,34},{40,44},{48,50},{56,60},{64,6... | collective-permute-start | bytes 442376 | tf_op jit(solution)/shard_map/ppermute | solution.py:36
  65.3 9.8 %collective-permute-start.22 = (bf16[64,1152]{1,0:T(8,128)(2,1)S(1)}, bf16[64,1152]{1,0:T(8,128)(2,1)S(1)}, u32[]{:S(2)}, u32[]{:S(2)}) collective-permute-start(bf16[64,1152]{1,0:T(8,128)(2,1)S(1)} %get-tuple-element.70), channel_id=1, source_target_pairs={{0,1},{8,136},{16,17},{24,152},{32,33},{40,168},{48,49},{56,184},{... | collective-permute-start | bytes 442376 | tf_op jit(solution)/shard_map/ppermute | solution.py:36
  66.8 8.3 %collective-permute-start.23 = (bf16[64,1152]{1,0:T(8,128)(2,1)S(1)}, bf16[64,1152]{1,0:T(8,128)(2,1)S(1)}, u32[]{:S(2)}, u32[]{:S(2)}) collective-permute-start(bf16[64,1152]{1,0:T(8,128)(2,1)S(1)} %get-tuple-element.69), channel_id=1, source_target_pairs={{0,3},{8,140},{16,19},{24,156},{32,35},{40,172},{48,51},{56,188},{... | collective-permute-start | bytes 442376 | tf_op jit(solution)/shard_map/ppermute | solution.py:36
  71.5 4.6 %collective-permute-start.25 = (bf16[64,1152]{1,0:T(8,128)(2,1)S(1)}, bf16[64,1152]{1,0:T(8,128)(2,1)S(1)}, u32[]{:S(2)}, u32[]{:S(2)}) collective-permute-start(bf16[64,1152]{1,0:T(8,128)(2,1)S(1)} %fusion), channel_id=1, source_target_pairs={{0,8},{8,0},{16,24},{24,16},{32,40},{40,32},{48,56},{56,48},{64,72... | collective-permute-start | bytes 442376 | tf_op jit(solution)/shard_map/ppermute | solution.py:36
  (3 other events, 9.6 us)

commit v4 on v3

--- a/solution.py
+++ b/solution.py
@@ -62,8 +62,8 @@
     return block // 16, block // 2 % 8, block % 2, lane // 4, lane % 4
 
 
-def prep_kernel(far, where_ref, images_ref, labels_ref, image_out, held, sems):
-    xh, y = where_ref[3], where_ref[4]
+def prep_kernel(far, images_ref, labels_ref, image_out, held, sems):
+    xh, y = place()[3:]
     half = 1 - xh if far else xh
     copies = []
     for i in range(Y):
@@ -83,46 +83,46 @@
         image_out[i * SHARE : (i + 1) * SHARE, :] = held[i].astype(low)
 
 
-def prep(where, images, labels, far):
+def prep(images, labels, far):
     width = images.shape[1]
     return pl.pallas_call(
         functools.partial(prep_kernel, far),
         out_shape=jax.ShapeDtypeStruct((272, width), low),
-        in_specs=[pl.BlockSpec(memory_space=pltpu.SMEM), HBM, VMEM],
+        in_specs=[HBM, VMEM],
         out_specs=VMEM,
         scratch_shapes=[pltpu.VMEM((Y, SHARE, width), f32), pltpu.SemaphoreType.DMA((Y,))],
         compiler_params=pltpu.CompilerParams(vmem_limit_bytes=52 * MIB),
         cost_estimate=pl.CostEstimate(flops=0, bytes_accessed=3 << 20, transcendentals=0),
-    )(where, images, labels)
-
-
-def text_kernel(where_ref, texts_ref, text_out, held, sem):
-    row = pl.multiple_of((where_ref[3] * Y + where_ref[4]) * SHARE, SHARE)
+    )(images, labels)
+
+
+def text_kernel(texts_ref, text_out, held, sem):
+    row = pl.multiple_of(lax.axis_index("lane") * SHARE, SHARE)
     copy = pltpu.make_async_copy(texts_ref.at[pl.ds(row, SHARE)], held, sem)
     copy.start()
     copy.wait()
     text_out[...] = held[...].astype(low)
 
 
-def own_text(where, texts):
+def own_text(texts):
     width = texts.shape[1]
     return pl.pallas_call(
         text_kernel,
         out_shape=jax.ShapeDtypeStruct((SHARE, width), low),
-        in_specs=[pl.BlockSpec(memory_space=pltpu.SMEM), HBM],
+        in_specs=[HBM],
         out_specs=VMEM,
         scratch_shapes=[pltpu.VMEM((SHARE, width), f32), pltpu.SemaphoreType.DMA],
         compiler_params=pltpu.CompilerParams(vmem_limit_bytes=52 * MIB),
         cost_estimate=pl.CostEstimate(flops=0, bytes_accessed=1 << 19, transcendentals=0),
-    )(where, texts)
-
-
-def arrange(where_ref, parts, images_ref, labels_ref):
+    )(texts)
+
+
+def arrange(parts, images_ref, labels_ref):
     labels = []
     for part in parts:
         digits = part[256:272, :256].astype(f32)
         labels.append(digits[0:1] * 128.0 + digits[1:2])
-    core = where_ref[2]
+    core = place()[2]
 
     @pl.when(core == 0)
     def _():
@@ -141,8 +141,8 @@
             labels_ref[:, k * 256 : (k + 1) * 256] = jnp.broadcast_to(row, (8, 256))
 
 
-def text_numbers(where_ref, group):
-    xl, z, c, xh, y = (where_ref[i] for i in range(5))
+def text_numbers(group):
+    xl, z, c, xh, y = place()
     sign = 1 - 2 * c
     numbers = [[], []]
     for d in group:
@@ -159,7 +159,7 @@
     return jnp.concatenate(numbers[0] + numbers[1], axis=0).astype(f32)
 
 
-def tile_kernel(group, kind, gives, where_ref, *refs):
+def tile_kernel(group, kind, gives, *refs):
     refs = list(refs)
     take = lambda count: [refs.pop(0) for _ in range(count)]
     if kind == "first":
@@ -169,7 +169,7 @@
     texts = take(2 * len(group))
     if kind == "first":
         images_ref, labels_ref = take(2)
-        arrange(where_ref, parts, images_ref, labels_ref)
+        arrange(parts, images_ref, labels_ref)
     image_outs = take(4 if kind == "last" else 1)
     term_refs = take(len(group) + gives)
     text_ref, weight_ref = refs
@@ -179,7 +179,7 @@
             piece = texts[2 * i + side]
             text_ref[at : at + piece.shape[0], :] = piece[...]
             at += piece.shape[0]
-    numbers = text_numbers(where_ref, group)
+    numbers = text_numbers(group)
     text = text_ref[...]
     for a in range(0, 1024, 256):
         cut = slice(a, a + 256)
@@ -204,7 +204,7 @@
         at += ref.shape[0]
 
 
-def tile(where, args, group, kind, sizes, give_sizes):
+def tile(args, group, kind, sizes, give_sizes):
     width = args[0].shape[1]
     n = 2 * sum(sizes)
     shape = jax.ShapeDtypeStruct
@@ -220,14 +220,14 @@
     return pl.pallas_call(
         functools.partial(tile_kernel, group, kind, len(give_sizes)),
         out_shape=tuple(outs),
-        in_specs=[pl.BlockSpec(memory_space=pltpu.SMEM)] + [VMEM] * len(args),
+        in_specs=[VMEM] * len(args),
         out_specs=(VMEM,) * len(outs),
         scratch_shapes=[pltpu.VMEM((n, width), low), pltpu.VMEM((n, 1024), low)],
         compiler_params=pltpu.CompilerParams(vmem_limit_bytes=28 * MIB),
         cost_estimate=pl.CostEstimate(
             flops=18 * 1024 * n * width, bytes_accessed=4 << 20, transcendentals=1024 * n
         ),
-    )(where, *args)
+    )(*args)
 
 
 def after(value, *others):
@@ -235,11 +235,10 @@
 
 
 def on_device(images, texts, labels):
-    where = jnp.stack(place()).astype(jnp.int32)
     label_rows = labels.reshape(4, 128)
-    text_own = own_text(where, texts)
+    text_own = own_text(texts)
     text_other = to_core(text_own)
-    image_near = prep(where, images, label_rows, False)
+    image_near = prep(images, label_rows, False)
     chunk = jnp.concatenate([text_own, text_other], axis=0)
     arrived_2 = to_z(chunk, -2)
     image_near = after(image_near, chunk)
@@ -247,19 +246,17 @@
     image_left = to_x(image_near, 1)
     arrived_1 = to_z(chunk, -1)
     swapped_1 = to_core(arrived_1)
-    image_far = prep(where, images, label_rows, True)
+    image_far = prep(images, label_rows, True)
     arrived_2 = after(arrived_2, swapped_1, image_far)
     arrived_3 = to_z(arrived_2, -1)
     arrived_4 = to_z(arrived_2[:SHARE], -2)
     swapped_2 = to_core(after(arrived_2, image_right, image_left))
 
     args = (image_near, after(image_right, arrived_2), image_far, image_left)
-    args += (text_own, text_other, arrived_1, swapped_1)
-    image_rows, label_row, held, own_keep, keep_1, own_give, give_1 = tile(
-        where, args, (0, 1), "first", (SHARE, 2 * SHARE), (SHARE, 2 * SHARE)
-    )
+    args += (arrived_1, swapped_1)
+    image_rows, label_row, held, keep_1, give_1 = tile(args, (1,), "first", (2 * SHARE,), (2 * SHARE,))
     args = (image_rows, label_row, held, arrived_2, swapped_2)
-    held, keep_2, give_2 = tile(where, args, (2,), "middle", (2 * SHARE,), (2 * SHARE,))
+    held, keep_2, give_2 = tile(args, (2,), "middle", (2 * SHARE,), (2 * SHARE,))
     arrived_3 = after(arrived_3, held)
     arrived_4 = after(arrived_4, held)
     swapped_4 = to_core(arrived_4)
@@ -268,10 +265,11 @@
 
     term_2 = keep_2 + to_core(give_2).astype(f32)
     held, term_1 = lax.optimization_barrier((held, term_1))
-    args = (image_rows, label_row, held, arrived_3, swapped_3, arrived_4, swapped_4)
-    sizes = (2 * SHARE, SHARE)
-    image_2, image_1, image_3, image_0, keep_3, keep_4, give_3, give_4 = tile(
-        where, args, (3, 4), "last", sizes, sizes
+    args = (image_rows, label_row, held)
+    args += (text_own, text_other, arrived_3, swapped_3, arrived_4, swapped_4)
+    sizes = (SHARE, 2 * SHARE, SHARE)
+    image_2, image_1, image_3, image_0, own_keep, keep_3, keep_4, own_give, give_3, give_4 = tile(
+        args, (0, 3, 4), "last", sizes, sizes
     )
     from_1 = to_z(term_1, 1)
     back_3, back_4 = to_core(give_3), to_core(give_4)

time: 77 us -> 73.4 us (0.953)
  starting transfers between devices: 40.2 us -> 44.6 us
  Pallas kernels: 16.9 us -> 12.7 us
  waiting for transfers between devices: 16.5 us -> 12.7 us
    ppermute x26, starting transfers between devices: 40.2 us -> 44.6 us  [send(): return lax.ppermute(value, AXES, pairs)]
    ppermute x26, waiting for transfers between devices: 16.5 us -> 12.7 us  [send(): return lax.ppermute(value, AXES, pairs)]
    pallas_call x3, Pallas kernels: 11.7 us -> 9.16 us  [tile(): pl.pallas_call(functools.partial(tile_kernel, group, kind, len(give_sizes...]
    pallas_call x2, Pallas kernels: 3.66 us -> 2.57 us  [prep(): pl.pallas_call(functools.partial(prep_kernel, far), out_shape=jax.ShapeDt...]
  transfers between devices with their start and end apart: 26 -> 26, of which waited for: 5 -> 6; matrix products, arithmetic and copies ran while one was open for 2% -> 2% of each run, Pallas kernels for 20% -> 16%
where the time goes in v4:
time: 73.4 us; the launch traced here: 73.2 us
  starting transfers between devices  44.6 us (61%)
  Pallas kernels  12.7 us (17%)
  waiting for transfers between devices  12.7 us (17%)
  other arithmetic  2.25 us (3%)
  between operations  0.82 us (1%)
    ppermute x26, starting transfers between devices, send(): return lax.ppermute(value, AXES, pairs)  44.6 us
    ppermute x26, waiting for transfers between devices, send(): return lax.ppermute(value, AXES, pairs)  12.7 us
    pallas_call x3, Pallas kernels, tile(): pl.pallas_call(functools.partial(tile_kernel, group, kind, len(give_sizes...  9.16 us
    pallas_call x2, Pallas kernels, prep(): pl.pallas_call(functools.partial(prep_kernel, far), out_shape=jax.ShapeDt...  2.57 us
  transfers between devices with their start and end apart: 26, of which 6 were waited for; matrix products, arithmetic and copies ran while one was open for 2% of the time, Pallas kernels for 16%

profile of v4, /device:TPU:1, one launch (start us, length us, event | category | flops | bytes accessed | tf_op | source)
XLA Modules:
  0.0 73.2 jit_solution(10995649277969171201)
XLA Ops:
  0.6 1.0 %shard_map.51.refs_3_ = bf16[64,1152]{1,0:T(8,128)(2,1)S(1)} custom-call(f32[512,1152]{1,0:T(8,128)} %texts_ref.1), custom_call_target="tpu_custom_call" | custom-call | bytes 524288 | tf_op jit(solution)/shard_map/pallas_call | solution.py:109
  1.6 3.3 %collective-permute-start = (bf16[64,1152]{1,0:T(8,128)(2,1)S(1)}, bf16[64,1152]{1,0:T(8,128)(2,1)S(1)}, u32[]{:S(2)}, u32[]{:S(2)}) collective-permute-start(bf16[64,1152]{1,0:T(8,128)(2,1)S(1)} %shard_map.51.refs_3_), channel_id=1, source_target_pairs={{0,8},{8,0},{16,24},{24,16},{32,40},{40,32},{48,56},{56,48},{64,72... | collective-permute-start | bytes 442376 | tf_op jit(solution)/shard_map/ppermute | solution.py:36
  5.0 1.3 %shard_map.50.refs_0_ = bf16[272,1152]{1,0:T(8,128)(2,1)S(1)} custom-call(f32[512,1152]{1,0:T(8,128)} %images_ref.3, s32[4,128]{1,0:T(4,128)S(1)} %bitcast.1), custom_call_target="tpu_custom_call" | custom-call | bytes 3145728 | tf_op jit(solution)/shard_map/pallas_call | solution.py:88
  6.3 0.8 %collective-permute-start.1 = (bf16[272,1152]{1,0:T(8,128)(2,1)S(1)}, bf16[272,1152]{1,0:T(8,128)(2,1)S(1)}, u32[]{:S(2)}, u32[]{:S(2)}) collective-permute-start(bf16[272,1152]{1,0:T(8,128)(2,1)S(1)} %shard_map.50.refs_0_), channel_id=1, source_target_pairs={{0,132},{8,140},{16,148},{24,156},{32,164},{40,172},{48,180},{56,1... | collective-permute-start | bytes 1880072 | tf_op jit(solution)/shard_map/ppermute | solution.py:36
  7.9 0.9 %collective-permute-start.3 = (bf16[128,1152]{1,0:T(8,128)(2,1)S(1)}, bf16[128,1152]{1,0:T(8,128)(2,1)S(1)}, u32[]{:S(2)}, u32[]{:S(2)}) collective-permute-start(bf16[128,1152]{1,0:T(8,128)(2,1)S(1)} %pad_maximum_fusion), channel_id=1, source_target_pairs={{0,112},{8,24},{16,0},{24,40},{32,16},{40,56},{48,32},{56,72},{64,... | collective-permute-start | bytes 884744 | tf_op jit(solution)/shard_map/ppermute | solution.py:36
  8.8 3.0 %collective-permute-start.2 = (bf16[128,1152]{1,0:T(8,128)(2,1)S(1)}, bf16[128,1152]{1,0:T(8,128)(2,1)S(1)}, u32[]{:S(2)}, u32[]{:S(2)}) collective-permute-start(bf16[128,1152]{1,0:T(8,128)(2,1)S(1)} %pad_maximum_fusion), channel_id=1, source_target_pairs={{0,96},{8,40},{16,112},{24,56},{32,0},{40,72},{48,16},{56,88},{64,... | collective-permute-start | bytes 884744 | tf_op jit(solution)/shard_map/ppermute | solution.py:36
  11.8 5.4 %collective-permute-done.3.refs_4_ = bf16[128,1152]{1,0:T(8,128)(2,1)S(1)} collective-permute-done((bf16[128,1152]{1,0:T(8,128)(2,1)S(1)}, bf16[128,1152]{1,0:T(8,128)(2,1)S(1)}, u32[]{:S(2)}, u32[]{:S(2)}) %collective-permute-start.3) | collective-permute-done | bytes 294944 | tf_op jit(solution)/shard_map/ppermute | solution.py:36
  17.1 2.8 %collective-permute-start.4 = (bf16[128,1152]{1,0:T(8,128)(2,1)S(1)}, bf16[128,1152]{1,0:T(8,128)(2,1)S(1)}, u32[]{:S(2)}, u32[]{:S(2)}) collective-permute-start(bf16[128,1152]{1,0:T(8,128)(2,1)S(1)} %collective-permute-done.3.refs_4_), channel_id=1, source_target_pairs={{0,8},{8,0},{16,24},{24,16},{32,40},{40,32},{48,56},{56,48},{64,72... | collective-permute-start | bytes 884744 | tf_op jit(solution)/shard_map/ppermute | solution.py:36
  19.9 1.3 %shard_map.52.refs_2_ = bf16[272,1152]{1,0:T(8,128)(2,1)S(1)} custom-call(f32[512,1152]{1,0:T(8,128)} %images_ref.3, s32[4,128]{1,0:T(4,128)S(1)} %bitcast.2), custom_call_target="tpu_custom_call" | custom-call | bytes 3145728 | tf_op jit(solution)/shard_map/pallas_call | solution.py:88
  21.7 2.7 %collective-permute-start.8 = (bf16[128,1152]{1,0:T(8,128)(2,1)S(1)}, bf16[128,1152]{1,0:T(8,128)(2,1)S(1)}, u32[]{:S(2)}, u32[]{:S(2)}) collective-permute-start(bf16[128,1152]{1,0:T(8,128)(2,1)S(1)} %collective-permute-done.2.refs_3_), channel_id=1, source_target_pairs={{0,112},{8,24},{16,0},{24,40},{32,16},{40,56},{48,32},{56,72},{64,... | collective-permute-start | bytes 884744 | tf_op jit(solution)/shard_map/ppermute | solution.py:36
  24.7 4.0 %collective-permute-start.6 = (bf16[128,1152]{1,0:T(8,128)(2,1)S(1)}, bf16[128,1152]{1,0:T(8,128)(2,1)S(1)}, u32[]{:S(2)}, u32[]{:S(2)}) collective-permute-start(bf16[128,1152]{1,0:T(8,128)(2,1)S(1)} %collective-permute-done.2.refs_3_), channel_id=1, source_target_pairs={{0,8},{8,0},{16,24},{24,16},{32,40},{40,32},{48,56},{56,48},{64,72... | collective-permute-start | bytes 884744 | tf_op jit(solution)/shard_map/ppermute | solution.py:36
  28.7 2.5 %shard_map.53 = (bf16[1024,1152]{1,0:T(8,128)(2,1)S(1)}, f32[8,1024]{1,0:T(8,128)S(1)}, f32[1024,1152]{1,0:T(8,128)S(1)}, f32[128,1152]{1,0:T(8,128)S(1)}, bf16[128,1152]{1,0:T(8,128)(2,1)S(1)}) custom-call(bf16[272,1152]{1,0:T(8,128)(2,1)S(1)} %shard_map.50.refs_0_, bf16[272,1152]{1,0:T(8,128)(2,1)S(1)} %collective-permute-done.1.refs_1_, ...), custom_call_target="tpu_custom_call" | custom-call | flops 5435817984 | bytes 4194304 | tf_op jit(solution)/shard_map/pallas_call | solution.py:220
  31.3 2.3 %shard_map.54 = (f32[1024,1152]{1,0:T(8,128)S(1)}, f32[128,1152]{1,0:T(8,128)S(1)}, bf16[128,1152]{1,0:T(8,128)(2,1)S(1)}) custom-call(bf16[1024,1152]{1,0:T(8,128)(2,1)S(1)} %get-tuple-element.36.refs_0_, f32[8,1024]{1,0:T(8,128)S(1)} %get-tuple-element.37.refs_1_, f32[1024,1152]{1,0:T(8,128)S(1)} %get-tuple-element.38.refs_2_, ...), custom_call_target="tpu_custom_call" | custom-call | flops 5435817984 | bytes 4194304 | tf_op jit(solution)/shard_map/pallas_call | solution.py:220
  34.6 2.4 %collective-permute-start.17 = (bf16[128,1152]{1,0:T(8,128)(2,1)S(1)}, bf16[128,1152]{1,0:T(8,128)(2,1)S(1)}, u32[]{:S(2)}, u32[]{:S(2)}) collective-permute-start(bf16[128,1152]{1,0:T(8,128)(2,1)S(1)} %add_convert_fusion.1), channel_id=1, source_target_pairs={{0,16},{8,120},{16,32},{24,8},{32,48},{40,24},{48,64},{56,40},{64,... | collective-permute-start | bytes 884744 | tf_op jit(solution)/shard_map/ppermute | solution.py:36
  36.9 4.3 %shard_map.55 = (bf16[256,1152]{1,0:T(8,128)(2,1)S(1)}, bf16[256,1152]{1,0:T(8,128)(2,1)S(1)}, bf16[256,1152]{1,0:T(8,128)(2,1)S(1)}, bf16[256,1152]{1,0:T(8,128...) custom-call(bf16[1024,1152]{1,0:T(8,128)(2,1)S(1)} %get-tuple-elemen, ...), custom_call_target="tpu_custom_call" | custom-call | flops 10871635968 | bytes 4194304 | tf_op jit(solution)/shard_map/pallas_call | solution.py:220
  42.0 2.9 %collective-permute-start.12 = (bf16[256,1152]{1,0:T(8,128)(2,1)S(1)}, bf16[256,1152]{1,0:T(8,128)(2,1)S(1)}, u32[]{:S(2)}, u32[]{:S(2)}) collective-permute-start(bf16[256,1152]{1,0:T(8,128)(2,1)S(1)} %get-tuple-element.47), channel_id=1, source_target_pairs={{0,4},{8,10},{16,20},{24,26},{32,36},{40,42},{48,52},{56,58},{64,6... | collective-permute-start | bytes 1769480 | tf_op jit(solution)/shard_map/ppermute | solution.py:36
  45.3 2.3 %collective-permute-start.14 = (bf16[256,1152]{1,0:T(8,128)(2,1)S(1)}, bf16[256,1152]{1,0:T(8,128)(2,1)S(1)}, u32[]{:S(2)}, u32[]{:S(2)}) collective-permute-start(bf16[256,1152]{1,0:T(8,128)(2,1)S(1)} %get-tuple-element.49), channel_id=1, source_target_pairs={{0,132},{8,11},{16,148},{24,27},{32,164},{40,43},{48,180},{56,59},... | collective-permute-start | bytes 1769480 | tf_op jit(solution)/shard_map/ppermute | solution.py:36
  47.6 3.1 %collective-permute-start.20 = (bf16[64,1152]{1,0:T(8,128)(2,1)S(1)}, bf16[64,1152]{1,0:T(8,128)(2,1)S(1)}, u32[]{:S(2)}, u32[]{:S(2)}) collective-permute-start(bf16[64,1152]{1,0:T(8,128)(2,1)S(1)} %add_convert_fusion.2), channel_id=1, source_target_pairs={{0,32},{8,104},{16,48},{24,120},{32,64},{40,8},{48,80},{56,24},{64... | collective-permute-start | bytes 442376 | tf_op jit(solution)/shard_map/ppermute | solution.py:36
  51.5 6.1 %collective-permute-done.18 = bf16[128,1152]{1,0:T(8,128)(2,1)S(1)} collective-permute-done((bf16[128,1152]{1,0:T(8,128)(2,1)S(1)}, bf16[128,1152]{1,0:T(8,128)(2,1)S(1)}, u32[]{:S(2)}, u32[]{:S(2)}) %collective-permute-start.18) | collective-permute-done | bytes 294944 | tf_op jit(solution)/shard_map/ppermute | solution.py:36
  57.8 2.5 %collective-permute-start.24 = (bf16[128,1152]{1,0:T(8,128)(2,1)S(1)}, bf16[128,1152]{1,0:T(8,128)(2,1)S(1)}, u32[]{:S(2)}, u32[]{:S(2)}) collective-permute-start(bf16[128,1152]{1,0:T(8,128)(2,1)S(1)} %pad_maximum_fusion.1), channel_id=1, source_target_pairs={{0,32},{8,104},{16,48},{24,120},{32,64},{40,8},{48,80},{56,24},{64... | collective-permute-start | bytes 884744 | tf_op jit(solution)/shard_map/ppermute | solution.py:36
  60.7 2.1 %collective-permute-start.21 = (bf16[64,1152]{1,0:T(8,128)(2,1)S(1)}, bf16[64,1152]{1,0:T(8,128)(2,1)S(1)}, u32[]{:S(2)}, u32[]{:S(2)}) collective-permute-start(bf16[64,1152]{1,0:T(8,128)(2,1)S(1)} %get-tuple-element.68), channel_id=1, source_target_pairs={{0,2},{8,12},{16,18},{24,28},{32,34},{40,44},{48,50},{56,60},{64,6... | collective-permute-start | bytes 442376 | tf_op jit(solution)/shard_map/ppermute | solution.py:36
  62.8 1.5 %collective-permute-start.22 = (bf16[64,1152]{1,0:T(8,128)(2,1)S(1)}, bf16[64,1152]{1,0:T(8,128)(2,1)S(1)}, u32[]{:S(2)}, u32[]{:S(2)}) collective-permute-start(bf16[64,1152]{1,0:T(8,128)(2,1)S(1)} %get-tuple-element.70), channel_id=1, source_target_pairs={{0,1},{8,136},{16,17},{24,152},{32,33},{40,168},{48,49},{56,184},{... | collective-permute-start | bytes 442376 | tf_op jit(solution)/shard_map/ppermute | solution.py:36
  64.3 1.2 %collective-permute-start.23 = (bf16[64,1152]{1,0:T(8,128)(2,1)S(1)}, bf16[64,1152]{1,0:T(8,128)(2,1)S(1)}, u32[]{:S(2)}, u32[]{:S(2)}) collective-permute-start(bf16[64,1152]{1,0:T(8,128)(2,1)S(1)} %get-tuple-element.69), channel_id=1, source_target_pairs={{0,3},{8,140},{16,19},{24,156},{32,35},{40,172},{48,51},{56,188},{... | collective-permute-start | bytes 442376 | tf_op jit(solution)/shard_map/ppermute | solution.py:36
  65.8 5.7 %collective-permute-start.25 = (bf16[64,1152]{1,0:T(8,128)(2,1)S(1)}, bf16[64,1152]{1,0:T(8,128)(2,1)S(1)}, u32[]{:S(2)}, u32[]{:S(2)}) collective-permute-start(bf16[64,1152]{1,0:T(8,128)(2,1)S(1)} %fusion), channel_id=1, source_target_pairs={{0,8},{8,0},{16,24},{24,16},{32,40},{40,32},{48,56},{56,48},{64,72... | collective-permute-start | bytes 442376 | tf_op jit(solution)/shard_map/ppermute | solution.py:36
  (51 shorter events, 7.0 us)
Async XLA Ops:
  1.6 4.6 %collective-permute-start = (bf16[64,1152]{1,0:T(8,128)(2,1)S(1)}, bf16[64,1152]{1,0:T(8,128)(2,1)S(1)}, u32[]{:S(2)}, u32[]{:S(2)}) collective-permute-start(bf16[64,1152]{1,0:T(8,128)(2,1)S(1)} %shard_map.51.refs_3_), channel_id=1, source_target_pairs={{0,8},{8,0},{16,24},{24,16},{32,40},{40,32},{48,56},{56,48},{64,72... | collective-permute-start | bytes 442376 | tf_op jit(solution)/shard_map/ppermute | solution.py:36
  6.3 18.4 %collective-permute-start.1 = (bf16[272,1152]{1,0:T(8,128)(2,1)S(1)}, bf16[272,1152]{1,0:T(8,128)(2,1)S(1)}, u32[]{:S(2)}, u32[]{:S(2)}) collective-permute-start(bf16[272,1152]{1,0:T(8,128)(2,1)S(1)} %shard_map.50.refs_0_), channel_id=1, source_target_pairs={{0,132},{8,140},{16,148},{24,156},{32,164},{40,172},{48,180},{56,1... | collective-permute-start | bytes 1880072 | tf_op jit(solution)/shard_map/ppermute | solution.py:36
  7.1 17.6 %collective-permute-start.5 = (bf16[272,1152]{1,0:T(8,128)(2,1)S(1)}, bf16[272,1152]{1,0:T(8,128)(2,1)S(1)}, u32[]{:S(2)}, u32[]{:S(2)}) collective-permute-start(bf16[272,1152]{1,0:T(8,128)(2,1)S(1)} %shard_map.50.refs_0_), channel_id=1, source_target_pairs={{0,128},{8,136},{16,144},{24,152},{32,160},{40,168},{48,176},{56,1... | collective-permute-start | bytes 1880072 | tf_op jit(solution)/shard_map/ppermute | solution.py:36
  7.9 9.3 %collective-permute-start.3 = (bf16[128,1152]{1,0:T(8,128)(2,1)S(1)}, bf16[128,1152]{1,0:T(8,128)(2,1)S(1)}, u32[]{:S(2)}, u32[]{:S(2)}) collective-permute-start(bf16[128,1152]{1,0:T(8,128)(2,1)S(1)} %pad_maximum_fusion), channel_id=1, source_target_pairs={{0,112},{8,24},{16,0},{24,40},{32,16},{40,56},{48,32},{56,72},{64,... | collective-permute-start | bytes 884744 | tf_op jit(solution)/shard_map/ppermute | solution.py:36
  8.8 12.9 %collective-permute-start.2 = (bf16[128,1152]{1,0:T(8,128)(2,1)S(1)}, bf16[128,1152]{1,0:T(8,128)(2,1)S(1)}, u32[]{:S(2)}, u32[]{:S(2)}) collective-permute-start(bf16[128,1152]{1,0:T(8,128)(2,1)S(1)} %pad_maximum_fusion), channel_id=1, source_target_pairs={{0,96},{8,40},{16,112},{24,56},{32,0},{40,72},{48,16},{56,88},{64,... | collective-permute-start | bytes 884744 | tf_op jit(solution)/shard_map/ppermute | solution.py:36
  17.1 4.6 %collective-permute-start.4 = (bf16[128,1152]{1,0:T(8,128)(2,1)S(1)}, bf16[128,1152]{1,0:T(8,128)(2,1)S(1)}, u32[]{:S(2)}, u32[]{:S(2)}) collective-permute-start(bf16[128,1152]{1,0:T(8,128)(2,1)S(1)} %collective-permute-done.3.refs_4_), channel_id=1, source_target_pairs={{0,8},{8,0},{16,24},{24,16},{32,40},{40,32},{48,56},{56,48},{64,72... | collective-permute-start | bytes 884744 | tf_op jit(solution)/shard_map/ppermute | solution.py:36
  21.7 12.7 %collective-permute-start.8 = (bf16[128,1152]{1,0:T(8,128)(2,1)S(1)}, bf16[128,1152]{1,0:T(8,128)(2,1)S(1)}, u32[]{:S(2)}, u32[]{:S(2)}) collective-permute-start(bf16[128,1152]{1,0:T(8,128)(2,1)S(1)} %collective-permute-done.2.refs_3_), channel_id=1, source_target_pairs={{0,112},{8,24},{16,0},{24,40},{32,16},{40,56},{48,32},{56,72},{64,... | collective-permute-start | bytes 884744 | tf_op jit(solution)/shard_map/ppermute | solution.py:36
  24.4 9.5 %collective-permute-start.10 = (bf16[64,1152]{1,0:T(8,128)(2,1)S(1)}, bf16[64,1152]{1,0:T(8,128)(2,1)S(1)}, u32[]{:S(2)}, u32[]{:S(2)}) collective-permute-start(bf16[64,1152]{1,0:T(8,128)(2,1)S(1)} %slice.36), channel_id=1, source_target_pairs={{0,96},{8,40},{16,112},{24,56},{32,0},{40,72},{48,16},{56,88},{64,... | collective-permute-start | bytes 442376 | tf_op jit(solution)/shard_map/ppermute | solution.py:36
  24.7 6.6 %collective-permute-start.6 = (bf16[128,1152]{1,0:T(8,128)(2,1)S(1)}, bf16[128,1152]{1,0:T(8,128)(2,1)S(1)}, u32[]{:S(2)}, u32[]{:S(2)}) collective-permute-start(bf16[128,1152]{1,0:T(8,128)(2,1)S(1)} %collective-permute-done.2.refs_3_), channel_id=1, source_target_pairs={{0,8},{8,0},{16,24},{24,16},{32,40},{40,32},{48,56},{56,48},{64,72... | collective-permute-start | bytes 884744 | tf_op jit(solution)/shard_map/ppermute | solution.py:36
  31.2 3.3 %collective-permute-start.7 = (bf16[128,1152]{1,0:T(8,128)(2,1)S(1)}, bf16[128,1152]{1,0:T(8,128)(2,1)S(1)}, u32[]{:S(2)}, u32[]{:S(2)}) collective-permute-start(bf16[128,1152]{1,0:T(8,128)(2,1)S(1)} %get-tuple-element.42), channel_id=1, source_target_pairs={{0,8},{8,0},{16,24},{24,16},{32,40},{40,32},{48,56},{56,48},{64,72... | collective-permute-start | bytes 884744 | tf_op jit(solution)/shard_map/ppermute | solution.py:36
  34.6 10.3 %collective-permute-start.17 = (bf16[128,1152]{1,0:T(8,128)(2,1)S(1)}, bf16[128,1152]{1,0:T(8,128)(2,1)S(1)}, u32[]{:S(2)}, u32[]{:S(2)}) collective-permute-start(bf16[128,1152]{1,0:T(8,128)(2,1)S(1)} %add_convert_fusion.1), channel_id=1, source_target_pairs={{0,16},{8,120},{16,32},{24,8},{32,48},{40,24},{48,64},{56,40},{64,... | collective-permute-start | bytes 884744 | tf_op jit(solution)/shard_map/ppermute | solution.py:36
  41.3 4.0 %collective-permute-start.19 = (bf16[64,1152]{1,0:T(8,128)(2,1)S(1)}, bf16[64,1152]{1,0:T(8,128)(2,1)S(1)}, u32[]{:S(2)}, u32[]{:S(2)}) collective-permute-start(bf16[64,1152]{1,0:T(8,128)(2,1)S(1)} %get-tuple-element.57), channel_id=1, source_target_pairs={{0,8},{8,0},{16,24},{24,16},{32,40},{40,32},{48,56},{56,48},{64,72... | collective-permute-start | bytes 442376 | tf_op jit(solution)/shard_map/ppermute | solution.py:36
  41.4 9.3 %collective-permute-start.15 = (bf16[128,1152]{1,0:T(8,128)(2,1)S(1)}, bf16[128,1152]{1,0:T(8,128)(2,1)S(1)}, u32[]{:S(2)}, u32[]{:S(2)}) collective-permute-start(bf16[128,1152]{1,0:T(8,128)(2,1)S(1)} %get-tuple-element.51), channel_id=1, source_target_pairs={{0,8},{8,0},{16,24},{24,16},{32,40},{40,32},{48,56},{56,48},{64,72... | collective-permute-start | bytes 884744 | tf_op jit(solution)/shard_map/ppermute | solution.py:36
  41.9 5.7 %collective-permute-start.16 = (bf16[128,1152]{1,0:T(8,128)(2,1)S(1)}, bf16[128,1152]{1,0:T(8,128)(2,1)S(1)}, u32[]{:S(2)}, u32[]{:S(2)}) collective-permute-start(bf16[128,1152]{1,0:T(8,128)(2,1)S(1)} %get-tuple-element.53), channel_id=1, source_target_pairs={{0,8},{8,0},{16,24},{24,16},{32,40},{40,32},{48,56},{56,48},{64,72... | collective-permute-start | bytes 884744 | tf_op jit(solution)/shard_map/ppermute | solution.py:36
  42.0 18.4 %collective-permute-start.12 = (bf16[256,1152]{1,0:T(8,128)(2,1)S(1)}, bf16[256,1152]{1,0:T(8,128)(2,1)S(1)}, u32[]{:S(2)}, u32[]{:S(2)}) collective-permute-start(bf16[256,1152]{1,0:T(8,128)(2,1)S(1)} %get-tuple-element.47), channel_id=1, source_target_pairs={{0,4},{8,10},{16,20},{24,26},{32,36},{40,42},{48,52},{56,58},{64,6... | collective-permute-start | bytes 1769480 | tf_op jit(solution)/shard_map/ppermute | solution.py:36
  44.9 15.4 %collective-permute-start.13 = (bf16[256,1152]{1,0:T(8,128)(2,1)S(1)}, bf16[256,1152]{1,0:T(8,128)(2,1)S(1)}, u32[]{:S(2)}, u32[]{:S(2)}) collective-permute-start(bf16[256,1152]{1,0:T(8,128)(2,1)S(1)} %get-tuple-element.48), channel_id=1, source_target_pairs={{0,128},{8,9},{16,144},{24,25},{32,160},{40,41},{48,176},{56,57},{... | collective-permute-start | bytes 1769480 | tf_op jit(solution)/shard_map/ppermute | solution.py:36
  45.3 15.0 %collective-permute-start.14 = (bf16[256,1152]{1,0:T(8,128)(2,1)S(1)}, bf16[256,1152]{1,0:T(8,128)(2,1)S(1)}, u32[]{:S(2)}, u32[]{:S(2)}) collective-permute-start(bf16[256,1152]{1,0:T(8,128)(2,1)S(1)} %get-tuple-element.49), channel_id=1, source_target_pairs={{0,132},{8,11},{16,148},{24,27},{32,164},{40,43},{48,180},{56,59},... | collective-permute-start | bytes 1769480 | tf_op jit(solution)/shard_map/ppermute | solution.py:36
  47.6 10.1 %collective-permute-start.20 = (bf16[64,1152]{1,0:T(8,128)(2,1)S(1)}, bf16[64,1152]{1,0:T(8,128)(2,1)S(1)}, u32[]{:S(2)}, u32[]{:S(2)}) collective-permute-start(bf16[64,1152]{1,0:T(8,128)(2,1)S(1)} %add_convert_fusion.2), channel_id=1, source_target_pairs={{0,32},{8,104},{16,48},{24,120},{32,64},{40,8},{48,80},{56,24},{64... | collective-permute-start | bytes 442376 | tf_op jit(solution)/shard_map/ppermute | solution.py:36
  50.8 6.9 %collective-permute-start.18 = (bf16[128,1152]{1,0:T(8,128)(2,1)S(1)}, bf16[128,1152]{1,0:T(8,128)(2,1)S(1)}, u32[]{:S(2)}, u32[]{:S(2)}) collective-permute-start(bf16[128,1152]{1,0:T(8,128)(2,1)S(1)} %add_convert_fusion), channel_id=1, source_target_pairs={{0,16},{8,120},{16,32},{24,8},{32,48},{40,24},{48,64},{56,40},{64,... | collective-permute-start | bytes 884744 | tf_op jit(solution)/shard_map/ppermute | solution.py:36
  57.8 7.9 %collective-permute-start.24 = (bf16[128,1152]{1,0:T(8,128)(2,1)S(1)}, bf16[128,1152]{1,0:T(8,128)(2,1)S(1)}, u32[]{:S(2)}, u32[]{:S(2)}) collective-permute-start(bf16[128,1152]{1,0:T(8,128)(2,1)S(1)} %pad_maximum_fusion.1), channel_id=1, source_target_pairs={{0,32},{8,104},{16,48},{24,120},{32,64},{40,8},{48,80},{56,24},{64... | collective-permute-start | bytes 884744 | tf_op jit(solution)/shard_map/ppermute | solution.py:36
  60.7 10.7 %collective-permute-start.21 = (bf16[64,1152]{1,0:T(8,128)(2,1)S(1)}, bf16[64,1152]{1,0:T(8,128)(2,1)S(1)}, u32[]{:S(2)}, u32[]{:S(2)}) collective-permute-start(bf16[64,1152]{1,0:T(8,128)(2,1)S(1)} %get-tuple-element.68), channel_id=1, source_target_pairs={{0,2},{8,12},{16,18},{24,28},{32,34},{40,44},{48,50},{56,60},{64,6... | collective-permute-start | bytes 442376 | tf_op jit(solution)/shard_map/ppermute | solution.py:36
  62.8 8.7 %collective-permute-start.22 = (bf16[64,1152]{1,0:T(8,128)(2,1)S(1)}, bf16[64,1152]{1,0:T(8,128)(2,1)S(1)}, u32[]{:S(2)}, u32[]{:S(2)}) collective-permute-start(bf16[64,1152]{1,0:T(8,128)(2,1)S(1)} %get-tuple-element.70), channel_id=1, source_target_pairs={{0,1},{8,136},{16,17},{24,152},{32,33},{40,168},{48,49},{56,184},{... | collective-permute-start | bytes 442376 | tf_op jit(solution)/shard_map/ppermute | solution.py:36
  64.3 7.1 %collective-permute-start.23 = (bf16[64,1152]{1,0:T(8,128)(2,1)S(1)}, bf16[64,1152]{1,0:T(8,128)(2,1)S(1)}, u32[]{:S(2)}, u32[]{:S(2)}) collective-permute-start(bf16[64,1152]{1,0:T(8,128)(2,1)S(1)} %get-tuple-element.69), channel_id=1, source_target_pairs={{0,3},{8,140},{16,19},{24,156},{32,35},{40,172},{48,51},{56,188},{... | collective-permute-start | bytes 442376 | tf_op jit(solution)/shard_map/ppermute | solution.py:36
  65.8 6.7 %collective-permute-start.25 = (bf16[64,1152]{1,0:T(8,128)(2,1)S(1)}, bf16[64,1152]{1,0:T(8,128)(2,1)S(1)}, u32[]{:S(2)}, u32[]{:S(2)}) collective-permute-start(bf16[64,1152]{1,0:T(8,128)(2,1)S(1)} %fusion), channel_id=1, source_target_pairs={{0,8},{8,0},{16,24},{24,16},{32,40},{40,32},{48,56},{56,48},{64,72... | collective-permute-start | bytes 442376 | tf_op jit(solution)/shard_map/ppermute | solution.py:36
  (3 other events, 9.9 us)

commit v5 on v4

--- a/solution.py
+++ b/solution.py
@@ -15,7 +15,7 @@
 low = jnp.bfloat16
 f32 = jnp.float32
 MIB = 1 << 20
-ORDER = (2, 1, 3, 0)
+ORDER = (1, 3, 2, 0)
 VMEM = pl.BlockSpec(memory_space=pltpu.VMEM)
 HBM = pl.BlockSpec(memory_space=pltpu.HBM)
 
@@ -268,7 +268,7 @@
     args = (image_rows, label_row, held)
     args += (text_own, text_other, arrived_3, swapped_3, arrived_4, swapped_4)
     sizes = (SHARE, 2 * SHARE, SHARE)
-    image_2, image_1, image_3, image_0, own_keep, keep_3, keep_4, own_give, give_3, give_4 = tile(
+    image_1, image_3, image_2, image_0, own_keep, keep_3, keep_4, own_give, give_3, give_4 = tile(
         args, (0, 3, 4), "last", sizes, sizes
     )
     from_1 = to_z(term_1, 1)
@@ -282,7 +282,7 @@
     parts = from_1.astype(f32) + to_z(term_2, 2).astype(f32)
 
     state = (image_0, image_1, image_2, image_3)
-    arrived = [first_stage(state[d], d) for d in (2, 1, 3)]
+    arrived = [first_stage(state[d], d) for d in (1, 3, 2)]
     arrived = list(lax.optimization_barrier((*arrived, term_2))[:3])
     image_sum = state[0].astype(f32)
     for value in arrived:

time: 73.4 us -> 72.6 us (0.989)
  starting transfers between devices: 44.6 us -> 43.4 us
    ppermute x26, starting transfers between devices: 44.6 us -> 43.4 us  [send(): return lax.ppermute(value, AXES, pairs)]
where the time goes in v5:
time: 72.6 us; the launch traced here: 72.5 us
  starting transfers between devices  43.4 us (60%)
  waiting for transfers between devices  13.2 us (18%)
  Pallas kernels  12.7 us (17%)
  other arithmetic  2.25 us (3%)
  between operations  0.81 us (1%)
    ppermute x26, starting transfers between devices, send(): return lax.ppermute(value, AXES, pairs)  43.4 us
    ppermute x26, waiting for transfers between devices, send(): return lax.ppermute(value, AXES, pairs)  13.2 us
    pallas_call x3, Pallas kernels, tile(): pl.pallas_call(functools.partial(tile_kernel, group, kind, len(give_sizes...  9.16 us
    pallas_call x2, Pallas kernels, prep(): pl.pallas_call(functools.partial(prep_kernel, far), out_shape=jax.ShapeDt...  2.57 us
  transfers between devices with their start and end apart: 26, of which 6 were waited for; matrix products, arithmetic and copies ran while one was open for 2% of the time, Pallas kernels for 16%

profile of v5, /device:TPU:1, one launch (start us, length us, event | category | flops | bytes accessed | tf_op | source)
XLA Modules:
  0.0 72.5 jit_solution(18365841716399380640)
XLA Ops:
  0.6 1.0 %shard_map.51.refs_3_ = bf16[64,1152]{1,0:T(8,128)(2,1)S(1)} custom-call(f32[512,1152]{1,0:T(8,128)} %texts_ref.1), custom_call_target="tpu_custom_call" | custom-call | bytes 524288 | tf_op jit(solution)/shard_map/pallas_call | solution.py:109
  1.6 3.3 %collective-permute-start = (bf16[64,1152]{1,0:T(8,128)(2,1)S(1)}, bf16[64,1152]{1,0:T(8,128)(2,1)S(1)}, u32[]{:S(2)}, u32[]{:S(2)}) collective-permute-start(bf16[64,1152]{1,0:T(8,128)(2,1)S(1)} %shard_map.51.refs_3_), channel_id=1, source_target_pairs={{0,8},{8,0},{16,24},{24,16},{32,40},{40,32},{48,56},{56,48},{64,72... | collective-permute-start | bytes 442376 | tf_op jit(solution)/shard_map/ppermute | solution.py:36
  5.0 1.3 %shard_map.50.refs_0_ = bf16[272,1152]{1,0:T(8,128)(2,1)S(1)} custom-call(f32[512,1152]{1,0:T(8,128)} %images_ref.3, s32[4,128]{1,0:T(4,128)S(1)} %bitcast.1), custom_call_target="tpu_custom_call" | custom-call | bytes 3145728 | tf_op jit(solution)/shard_map/pallas_call | solution.py:88
  7.9 0.9 %collective-permute-start.3 = (bf16[128,1152]{1,0:T(8,128)(2,1)S(1)}, bf16[128,1152]{1,0:T(8,128)(2,1)S(1)}, u32[]{:S(2)}, u32[]{:S(2)}) collective-permute-start(bf16[128,1152]{1,0:T(8,128)(2,1)S(1)} %pad_maximum_fusion), channel_id=1, source_target_pairs={{0,112},{8,24},{16,0},{24,40},{32,16},{40,56},{48,32},{56,72},{64,... | collective-permute-start | bytes 884744 | tf_op jit(solution)/shard_map/ppermute | solution.py:36
  8.8 3.0 %collective-permute-start.2 = (bf16[128,1152]{1,0:T(8,128)(2,1)S(1)}, bf16[128,1152]{1,0:T(8,128)(2,1)S(1)}, u32[]{:S(2)}, u32[]{:S(2)}) collective-permute-start(bf16[128,1152]{1,0:T(8,128)(2,1)S(1)} %pad_maximum_fusion), channel_id=1, source_target_pairs={{0,96},{8,40},{16,112},{24,56},{32,0},{40,72},{48,16},{56,88},{64,... | collective-permute-start | bytes 884744 | tf_op jit(solution)/shard_map/ppermute | solution.py:36
  11.8 5.4 %collective-permute-done.3.refs_4_ = bf16[128,1152]{1,0:T(8,128)(2,1)S(1)} collective-permute-done((bf16[128,1152]{1,0:T(8,128)(2,1)S(1)}, bf16[128,1152]{1,0:T(8,128)(2,1)S(1)}, u32[]{:S(2)}, u32[]{:S(2)}) %collective-permute-start.3) | collective-permute-done | bytes 294944 | tf_op jit(solution)/shard_map/ppermute | solution.py:36
  17.1 2.8 %collective-permute-start.4 = (bf16[128,1152]{1,0:T(8,128)(2,1)S(1)}, bf16[128,1152]{1,0:T(8,128)(2,1)S(1)}, u32[]{:S(2)}, u32[]{:S(2)}) collective-permute-start(bf16[128,1152]{1,0:T(8,128)(2,1)S(1)} %collective-permute-done.3.refs_4_), channel_id=1, source_target_pairs={{0,8},{8,0},{16,24},{24,16},{32,40},{40,32},{48,56},{56,48},{64,72... | collective-permute-start | bytes 884744 | tf_op jit(solution)/shard_map/ppermute | solution.py:36
  19.9 1.3 %shard_map.52.refs_2_ = bf16[272,1152]{1,0:T(8,128)(2,1)S(1)} custom-call(f32[512,1152]{1,0:T(8,128)} %images_ref.3, s32[4,128]{1,0:T(4,128)S(1)} %bitcast.2), custom_call_target="tpu_custom_call" | custom-call | bytes 3145728 | tf_op jit(solution)/shard_map/pallas_call | solution.py:88
  21.7 2.7 %collective-permute-start.8 = (bf16[128,1152]{1,0:T(8,128)(2,1)S(1)}, bf16[128,1152]{1,0:T(8,128)(2,1)S(1)}, u32[]{:S(2)}, u32[]{:S(2)}) collective-permute-start(bf16[128,1152]{1,0:T(8,128)(2,1)S(1)} %collective-permute-done.2.refs_3_), channel_id=1, source_target_pairs={{0,112},{8,24},{16,0},{24,40},{32,16},{40,56},{48,32},{56,72},{64,... | collective-permute-start | bytes 884744 | tf_op jit(solution)/shard_map/ppermute | solution.py:36
  24.7 4.0 %collective-permute-start.6 = (bf16[128,1152]{1,0:T(8,128)(2,1)S(1)}, bf16[128,1152]{1,0:T(8,128)(2,1)S(1)}, u32[]{:S(2)}, u32[]{:S(2)}) collective-permute-start(bf16[128,1152]{1,0:T(8,128)(2,1)S(1)} %collective-permute-done.2.refs_3_), channel_id=1, source_target_pairs={{0,8},{8,0},{16,24},{24,16},{32,40},{40,32},{48,56},{56,48},{64,72... | collective-permute-start | bytes 884744 | tf_op jit(solution)/shard_map/ppermute | solution.py:36
  28.7 2.5 %shard_map.53 = (bf16[1024,1152]{1,0:T(8,128)(2,1)S(1)}, f32[8,1024]{1,0:T(8,128)S(1)}, f32[1024,1152]{1,0:T(8,128)S(1)}, f32[128,1152]{1,0:T(8,128)S(1)}, bf16[128,1152]{1,0:T(8,128)(2,1)S(1)}) custom-call(bf16[272,1152]{1,0:T(8,128)(2,1)S(1)} %shard_map.50.refs_0_, bf16[272,1152]{1,0:T(8,128)(2,1)S(1)} %collective-permute-done.1.refs_1_, ...), custom_call_target="tpu_custom_call" | custom-call | flops 5435817984 | bytes 4194304 | tf_op jit(solution)/shard_map/pallas_call | solution.py:220
  31.3 2.3 %shard_map.54 = (f32[1024,1152]{1,0:T(8,128)S(1)}, f32[128,1152]{1,0:T(8,128)S(1)}, bf16[128,1152]{1,0:T(8,128)(2,1)S(1)}) custom-call(bf16[1024,1152]{1,0:T(8,128)(2,1)S(1)} %get-tuple-element.36.refs_0_, f32[8,1024]{1,0:T(8,128)S(1)} %get-tuple-element.37.refs_1_, f32[1024,1152]{1,0:T(8,128)S(1)} %get-tuple-element.38.refs_2_, ...), custom_call_target="tpu_custom_call" | custom-call | flops 5435817984 | bytes 4194304 | tf_op jit(solution)/shard_map/pallas_call | solution.py:220
  34.6 2.4 %collective-permute-start.17 = (bf16[128,1152]{1,0:T(8,128)(2,1)S(1)}, bf16[128,1152]{1,0:T(8,128)(2,1)S(1)}, u32[]{:S(2)}, u32[]{:S(2)}) collective-permute-start(bf16[128,1152]{1,0:T(8,128)(2,1)S(1)} %add_convert_fusion.1), channel_id=1, source_target_pairs={{0,16},{8,120},{16,32},{24,8},{32,48},{40,24},{48,64},{56,40},{64,... | collective-permute-start | bytes 884744 | tf_op jit(solution)/shard_map/ppermute | solution.py:36
  36.9 4.3 %shard_map.55 = (bf16[256,1152]{1,0:T(8,128)(2,1)S(1)}, bf16[256,1152]{1,0:T(8,128)(2,1)S(1)}, bf16[256,1152]{1,0:T(8,128)(2,1)S(1)}, bf16[256,1152]{1,0:T(8,128...) custom-call(bf16[1024,1152]{1,0:T(8,128)(2,1)S(1)} %get-tuple-elemen, ...), custom_call_target="tpu_custom_call" | custom-call | flops 10871635968 | bytes 4194304 | tf_op jit(solution)/shard_map/pallas_call | solution.py:220
  42.0 1.3 %collective-permute-start.12 = (bf16[256,1152]{1,0:T(8,128)(2,1)S(1)}, bf16[256,1152]{1,0:T(8,128)(2,1)S(1)}, u32[]{:S(2)}, u32[]{:S(2)}) collective-permute-start(bf16[256,1152]{1,0:T(8,128)(2,1)S(1)} %get-tuple-element.47), channel_id=1, source_target_pairs={{0,128},{8,9},{16,144},{24,25},{32,160},{40,41},{48,176},{56,57},{... | collective-permute-start | bytes 1769480 | tf_op jit(solution)/shard_map/ppermute | solution.py:36
  43.3 1.4 %collective-permute-start.13 = (bf16[256,1152]{1,0:T(8,128)(2,1)S(1)}, bf16[256,1152]{1,0:T(8,128)(2,1)S(1)}, u32[]{:S(2)}, u32[]{:S(2)}) collective-permute-start(bf16[256,1152]{1,0:T(8,128)(2,1)S(1)} %get-tuple-element.48), channel_id=1, source_target_pairs={{0,132},{8,11},{16,148},{24,27},{32,164},{40,43},{48,180},{56,59},... | collective-permute-start | bytes 1769480 | tf_op jit(solution)/shard_map/ppermute | solution.py:36
  44.7 1.6 %collective-permute-start.14 = (bf16[256,1152]{1,0:T(8,128)(2,1)S(1)}, bf16[256,1152]{1,0:T(8,128)(2,1)S(1)}, u32[]{:S(2)}, u32[]{:S(2)}) collective-permute-start(bf16[256,1152]{1,0:T(8,128)(2,1)S(1)} %get-tuple-element.49), channel_id=1, source_target_pairs={{0,4},{8,10},{16,20},{24,26},{32,36},{40,42},{48,52},{56,58},{64,6... | collective-permute-start | bytes 1769480 | tf_op jit(solution)/shard_map/ppermute | solution.py:36
  46.4 3.1 %collective-permute-start.20 = (bf16[64,1152]{1,0:T(8,128)(2,1)S(1)}, bf16[64,1152]{1,0:T(8,128)(2,1)S(1)}, u32[]{:S(2)}, u32[]{:S(2)}) collective-permute-start(bf16[64,1152]{1,0:T(8,128)(2,1)S(1)} %add_convert_fusion.2), channel_id=1, source_target_pairs={{0,32},{8,104},{16,48},{24,120},{32,64},{40,8},{48,80},{56,24},{64... | collective-permute-start | bytes 442376 | tf_op jit(solution)/shard_map/ppermute | solution.py:36
  50.3 6.1 %collective-permute-done.18 = bf16[128,1152]{1,0:T(8,128)(2,1)S(1)} collective-permute-done((bf16[128,1152]{1,0:T(8,128)(2,1)S(1)}, bf16[128,1152]{1,0:T(8,128)(2,1)S(1)}, u32[]{:S(2)}, u32[]{:S(2)}) %collective-permute-start.18) | collective-permute-done | bytes 294944 | tf_op jit(solution)/shard_map/ppermute | solution.py:36
  56.6 2.5 %collective-permute-start.24 = (bf16[128,1152]{1,0:T(8,128)(2,1)S(1)}, bf16[128,1152]{1,0:T(8,128)(2,1)S(1)}, u32[]{:S(2)}, u32[]{:S(2)}) collective-permute-start(bf16[128,1152]{1,0:T(8,128)(2,1)S(1)} %pad_maximum_fusion.1), channel_id=1, source_target_pairs={{0,32},{8,104},{16,48},{24,120},{32,64},{40,8},{48,80},{56,24},{64... | collective-permute-start | bytes 884744 | tf_op jit(solution)/shard_map/ppermute | solution.py:36
  60.1 1.8 %collective-permute-start.21 = (bf16[64,1152]{1,0:T(8,128)(2,1)S(1)}, bf16[64,1152]{1,0:T(8,128)(2,1)S(1)}, u32[]{:S(2)}, u32[]{:S(2)}) collective-permute-start(bf16[64,1152]{1,0:T(8,128)(2,1)S(1)} %get-tuple-element.68), channel_id=1, source_target_pairs={{0,2},{8,12},{16,18},{24,28},{32,34},{40,44},{48,50},{56,60},{64,6... | collective-permute-start | bytes 442376 | tf_op jit(solution)/shard_map/ppermute | solution.py:36
  61.9 1.5 %collective-permute-start.22 = (bf16[64,1152]{1,0:T(8,128)(2,1)S(1)}, bf16[64,1152]{1,0:T(8,128)(2,1)S(1)}, u32[]{:S(2)}, u32[]{:S(2)}) collective-permute-start(bf16[64,1152]{1,0:T(8,128)(2,1)S(1)} %get-tuple-element.70), channel_id=1, source_target_pairs={{0,1},{8,136},{16,17},{24,152},{32,33},{40,168},{48,49},{56,184},{... | collective-permute-start | bytes 442376 | tf_op jit(solution)/shard_map/ppermute | solution.py:36
  63.5 1.2 %collective-permute-start.23 = (bf16[64,1152]{1,0:T(8,128)(2,1)S(1)}, bf16[64,1152]{1,0:T(8,128)(2,1)S(1)}, u32[]{:S(2)}, u32[]{:S(2)}) collective-permute-start(bf16[64,1152]{1,0:T(8,128)(2,1)S(1)} %get-tuple-element.69), channel_id=1, source_target_pairs={{0,3},{8,140},{16,19},{24,156},{32,35},{40,172},{48,51},{56,188},{... | collective-permute-start | bytes 442376 | tf_op jit(solution)/shard_map/ppermute | solution.py:36
  64.7 6.0 %collective-permute-start.25 = (bf16[64,1152]{1,0:T(8,128)(2,1)S(1)}, bf16[64,1152]{1,0:T(8,128)(2,1)S(1)}, u32[]{:S(2)}, u32[]{:S(2)}) collective-permute-start(bf16[64,1152]{1,0:T(8,128)(2,1)S(1)} %fusion), channel_id=1, source_target_pairs={{0,8},{8,0},{16,24},{24,16},{32,40},{40,32},{48,56},{56,48},{64,72... | collective-permute-start | bytes 442376 | tf_op jit(solution)/shard_map/ppermute | solution.py:36
  (51 shorter events, 7.9 us)
Async XLA Ops:
  1.6 4.6 %collective-permute-start = (bf16[64,1152]{1,0:T(8,128)(2,1)S(1)}, bf16[64,1152]{1,0:T(8,128)(2,1)S(1)}, u32[]{:S(2)}, u32[]{:S(2)}) collective-permute-start(bf16[64,1152]{1,0:T(8,128)(2,1)S(1)} %shard_map.51.refs_3_), channel_id=1, source_target_pairs={{0,8},{8,0},{16,24},{24,16},{32,40},{40,32},{48,56},{56,48},{64,72... | collective-permute-start | bytes 442376 | tf_op jit(solution)/shard_map/ppermute | solution.py:36
  6.3 18.4 %collective-permute-start.1 = (bf16[272,1152]{1,0:T(8,128)(2,1)S(1)}, bf16[272,1152]{1,0:T(8,128)(2,1)S(1)}, u32[]{:S(2)}, u32[]{:S(2)}) collective-permute-start(bf16[272,1152]{1,0:T(8,128)(2,1)S(1)} %shard_map.50.refs_0_), channel_id=1, source_target_pairs={{0,132},{8,140},{16,148},{24,156},{32,164},{40,172},{48,180},{56,1... | collective-permute-start | bytes 1880072 | tf_op jit(solution)/shard_map/ppermute | solution.py:36
  7.1 17.6 %collective-permute-start.5 = (bf16[272,1152]{1,0:T(8,128)(2,1)S(1)}, bf16[272,1152]{1,0:T(8,128)(2,1)S(1)}, u32[]{:S(2)}, u32[]{:S(2)}) collective-permute-start(bf16[272,1152]{1,0:T(8,128)(2,1)S(1)} %shard_map.50.refs_0_), channel_id=1, source_target_pairs={{0,128},{8,136},{16,144},{24,152},{32,160},{40,168},{48,176},{56,1... | collective-permute-start | bytes 1880072 | tf_op jit(solution)/shard_map/ppermute | solution.py:36
  7.9 9.3 %collective-permute-start.3 = (bf16[128,1152]{1,0:T(8,128)(2,1)S(1)}, bf16[128,1152]{1,0:T(8,128)(2,1)S(1)}, u32[]{:S(2)}, u32[]{:S(2)}) collective-permute-start(bf16[128,1152]{1,0:T(8,128)(2,1)S(1)} %pad_maximum_fusion), channel_id=1, source_target_pairs={{0,112},{8,24},{16,0},{24,40},{32,16},{40,56},{48,32},{56,72},{64,... | collective-permute-start | bytes 884744 | tf_op jit(solution)/shard_map/ppermute | solution.py:36
  8.8 12.9 %collective-permute-start.2 = (bf16[128,1152]{1,0:T(8,128)(2,1)S(1)}, bf16[128,1152]{1,0:T(8,128)(2,1)S(1)}, u32[]{:S(2)}, u32[]{:S(2)}) collective-permute-start(bf16[128,1152]{1,0:T(8,128)(2,1)S(1)} %pad_maximum_fusion), channel_id=1, source_target_pairs={{0,96},{8,40},{16,112},{24,56},{32,0},{40,72},{48,16},{56,88},{64,... | collective-permute-start | bytes 884744 | tf_op jit(solution)/shard_map/ppermute | solution.py:36
  17.1 4.6 %collective-permute-start.4 = (bf16[128,1152]{1,0:T(8,128)(2,1)S(1)}, bf16[128,1152]{1,0:T(8,128)(2,1)S(1)}, u32[]{:S(2)}, u32[]{:S(2)}) collective-permute-start(bf16[128,1152]{1,0:T(8,128)(2,1)S(1)} %collective-permute-done.3.refs_4_), channel_id=1, source_target_pairs={{0,8},{8,0},{16,24},{24,16},{32,40},{40,32},{48,56},{56,48},{64,72... | collective-permute-start | bytes 884744 | tf_op jit(solution)/shard_map/ppermute | solution.py:36
  21.7 12.7 %collective-permute-start.8 = (bf16[128,1152]{1,0:T(8,128)(2,1)S(1)}, bf16[128,1152]{1,0:T(8,128)(2,1)S(1)}, u32[]{:S(2)}, u32[]{:S(2)}) collective-permute-start(bf16[128,1152]{1,0:T(8,128)(2,1)S(1)} %collective-permute-done.2.refs_3_), channel_id=1, source_target_pairs={{0,112},{8,24},{16,0},{24,40},{32,16},{40,56},{48,32},{56,72},{64,... | collective-permute-start | bytes 884744 | tf_op jit(solution)/shard_map/ppermute | solution.py:36
  24.4 9.5 %collective-permute-start.10 = (bf16[64,1152]{1,0:T(8,128)(2,1)S(1)}, bf16[64,1152]{1,0:T(8,128)(2,1)S(1)}, u32[]{:S(2)}, u32[]{:S(2)}) collective-permute-start(bf16[64,1152]{1,0:T(8,128)(2,1)S(1)} %slice.36), channel_id=1, source_target_pairs={{0,96},{8,40},{16,112},{24,56},{32,0},{40,72},{48,16},{56,88},{64,... | collective-permute-start | bytes 442376 | tf_op jit(solution)/shard_map/ppermute | solution.py:36
  24.7 6.6 %collective-permute-start.6 = (bf16[128,1152]{1,0:T(8,128)(2,1)S(1)}, bf16[128,1152]{1,0:T(8,128)(2,1)S(1)}, u32[]{:S(2)}, u32[]{:S(2)}) collective-permute-start(bf16[128,1152]{1,0:T(8,128)(2,1)S(1)} %collective-permute-done.2.refs_3_), channel_id=1, source_target_pairs={{0,8},{8,0},{16,24},{24,16},{32,40},{40,32},{48,56},{56,48},{64,72... | collective-permute-start | bytes 884744 | tf_op jit(solution)/shard_map/ppermute | solution.py:36
  31.2 3.3 %collective-permute-start.7 = (bf16[128,1152]{1,0:T(8,128)(2,1)S(1)}, bf16[128,1152]{1,0:T(8,128)(2,1)S(1)}, u32[]{:S(2)}, u32[]{:S(2)}) collective-permute-start(bf16[128,1152]{1,0:T(8,128)(2,1)S(1)} %get-tuple-element.42), channel_id=1, source_target_pairs={{0,8},{8,0},{16,24},{24,16},{32,40},{40,32},{48,56},{56,48},{64,72... | collective-permute-start | bytes 884744 | tf_op jit(solution)/shard_map/ppermute | solution.py:36
  34.6 8.7 %collective-permute-start.17 = (bf16[128,1152]{1,0:T(8,128)(2,1)S(1)}, bf16[128,1152]{1,0:T(8,128)(2,1)S(1)}, u32[]{:S(2)}, u32[]{:S(2)}) collective-permute-start(bf16[128,1152]{1,0:T(8,128)(2,1)S(1)} %add_convert_fusion.1), channel_id=1, source_target_pairs={{0,16},{8,120},{16,32},{24,8},{32,48},{40,24},{48,64},{56,40},{64,... | collective-permute-start | bytes 884744 | tf_op jit(solution)/shard_map/ppermute | solution.py:36
  41.3 3.4 %collective-permute-start.19 = (bf16[64,1152]{1,0:T(8,128)(2,1)S(1)}, bf16[64,1152]{1,0:T(8,128)(2,1)S(1)}, u32[]{:S(2)}, u32[]{:S(2)}) collective-permute-start(bf16[64,1152]{1,0:T(8,128)(2,1)S(1)} %get-tuple-element.57), channel_id=1, source_target_pairs={{0,8},{8,0},{16,24},{24,16},{32,40},{40,32},{48,56},{56,48},{64,72... | collective-permute-start | bytes 442376 | tf_op jit(solution)/shard_map/ppermute | solution.py:36
  41.4 8.1 %collective-permute-start.15 = (bf16[128,1152]{1,0:T(8,128)(2,1)S(1)}, bf16[128,1152]{1,0:T(8,128)(2,1)S(1)}, u32[]{:S(2)}, u32[]{:S(2)}) collective-permute-start(bf16[128,1152]{1,0:T(8,128)(2,1)S(1)} %get-tuple-element.51), channel_id=1, source_target_pairs={{0,8},{8,0},{16,24},{24,16},{32,40},{40,32},{48,56},{56,48},{64,72... | collective-permute-start | bytes 884744 | tf_op jit(solution)/shard_map/ppermute | solution.py:36
  41.9 4.5 %collective-permute-start.16 = (bf16[128,1152]{1,0:T(8,128)(2,1)S(1)}, bf16[128,1152]{1,0:T(8,128)(2,1)S(1)}, u32[]{:S(2)}, u32[]{:S(2)}) collective-permute-start(bf16[128,1152]{1,0:T(8,128)(2,1)S(1)} %get-tuple-element.53), channel_id=1, source_target_pairs={{0,8},{8,0},{16,24},{24,16},{32,40},{40,32},{48,56},{56,48},{64,72... | collective-permute-start | bytes 884744 | tf_op jit(solution)/shard_map/ppermute | solution.py:36
  42.0 17.1 %collective-permute-start.12 = (bf16[256,1152]{1,0:T(8,128)(2,1)S(1)}, bf16[256,1152]{1,0:T(8,128)(2,1)S(1)}, u32[]{:S(2)}, u32[]{:S(2)}) collective-permute-start(bf16[256,1152]{1,0:T(8,128)(2,1)S(1)} %get-tuple-element.47), channel_id=1, source_target_pairs={{0,128},{8,9},{16,144},{24,25},{32,160},{40,41},{48,176},{56,57},{... | collective-permute-start | bytes 1769480 | tf_op jit(solution)/shard_map/ppermute | solution.py:36
  43.3 15.8 %collective-permute-start.13 = (bf16[256,1152]{1,0:T(8,128)(2,1)S(1)}, bf16[256,1152]{1,0:T(8,128)(2,1)S(1)}, u32[]{:S(2)}, u32[]{:S(2)}) collective-permute-start(bf16[256,1152]{1,0:T(8,128)(2,1)S(1)} %get-tuple-element.48), channel_id=1, source_target_pairs={{0,132},{8,11},{16,148},{24,27},{32,164},{40,43},{48,180},{56,59},... | collective-permute-start | bytes 1769480 | tf_op jit(solution)/shard_map/ppermute | solution.py:36
  44.7 15.1 %collective-permute-start.14 = (bf16[256,1152]{1,0:T(8,128)(2,1)S(1)}, bf16[256,1152]{1,0:T(8,128)(2,1)S(1)}, u32[]{:S(2)}, u32[]{:S(2)}) collective-permute-start(bf16[256,1152]{1,0:T(8,128)(2,1)S(1)} %get-tuple-element.49), channel_id=1, source_target_pairs={{0,4},{8,10},{16,20},{24,26},{32,36},{40,42},{48,52},{56,58},{64,6... | collective-permute-start | bytes 1769480 | tf_op jit(solution)/shard_map/ppermute | solution.py:36
  46.4 10.1 %collective-permute-start.20 = (bf16[64,1152]{1,0:T(8,128)(2,1)S(1)}, bf16[64,1152]{1,0:T(8,128)(2,1)S(1)}, u32[]{:S(2)}, u32[]{:S(2)}) collective-permute-start(bf16[64,1152]{1,0:T(8,128)(2,1)S(1)} %add_convert_fusion.2), channel_id=1, source_target_pairs={{0,32},{8,104},{16,48},{24,120},{32,64},{40,8},{48,80},{56,24},{64... | collective-permute-start | bytes 442376 | tf_op jit(solution)/shard_map/ppermute | solution.py:36
  49.6 6.9 %collective-permute-start.18 = (bf16[128,1152]{1,0:T(8,128)(2,1)S(1)}, bf16[128,1152]{1,0:T(8,128)(2,1)S(1)}, u32[]{:S(2)}, u32[]{:S(2)}) collective-permute-start(bf16[128,1152]{1,0:T(8,128)(2,1)S(1)} %add_convert_fusion), channel_id=1, source_target_pairs={{0,16},{8,120},{16,32},{24,8},{32,48},{40,24},{48,64},{56,40},{64,... | collective-permute-start | bytes 884744 | tf_op jit(solution)/shard_map/ppermute | solution.py:36
  56.6 8.0 %collective-permute-start.24 = (bf16[128,1152]{1,0:T(8,128)(2,1)S(1)}, bf16[128,1152]{1,0:T(8,128)(2,1)S(1)}, u32[]{:S(2)}, u32[]{:S(2)}) collective-permute-start(bf16[128,1152]{1,0:T(8,128)(2,1)S(1)} %pad_maximum_fusion.1), channel_id=1, source_target_pairs={{0,32},{8,104},{16,48},{24,120},{32,64},{40,8},{48,80},{56,24},{64... | collective-permute-start | bytes 884744 | tf_op jit(solution)/shard_map/ppermute | solution.py:36
  60.1 10.6 %collective-permute-start.21 = (bf16[64,1152]{1,0:T(8,128)(2,1)S(1)}, bf16[64,1152]{1,0:T(8,128)(2,1)S(1)}, u32[]{:S(2)}, u32[]{:S(2)}) collective-permute-start(bf16[64,1152]{1,0:T(8,128)(2,1)S(1)} %get-tuple-element.68), channel_id=1, source_target_pairs={{0,2},{8,12},{16,18},{24,28},{32,34},{40,44},{48,50},{56,60},{64,6... | collective-permute-start | bytes 442376 | tf_op jit(solution)/shard_map/ppermute | solution.py:36
  61.9 8.8 %collective-permute-start.22 = (bf16[64,1152]{1,0:T(8,128)(2,1)S(1)}, bf16[64,1152]{1,0:T(8,128)(2,1)S(1)}, u32[]{:S(2)}, u32[]{:S(2)}) collective-permute-start(bf16[64,1152]{1,0:T(8,128)(2,1)S(1)} %get-tuple-element.70), channel_id=1, source_target_pairs={{0,1},{8,136},{16,17},{24,152},{32,33},{40,168},{48,49},{56,184},{... | collective-permute-start | bytes 442376 | tf_op jit(solution)/shard_map/ppermute | solution.py:36
  63.5 7.3 %collective-permute-start.23 = (bf16[64,1152]{1,0:T(8,128)(2,1)S(1)}, bf16[64,1152]{1,0:T(8,128)(2,1)S(1)}, u32[]{:S(2)}, u32[]{:S(2)}) collective-permute-start(bf16[64,1152]{1,0:T(8,128)(2,1)S(1)} %get-tuple-element.69), channel_id=1, source_target_pairs={{0,3},{8,140},{16,19},{24,156},{32,35},{40,172},{48,51},{56,188},{... | collective-permute-start | bytes 442376 | tf_op jit(solution)/shard_map/ppermute | solution.py:36
  64.7 7.0 %collective-permute-start.25 = (bf16[64,1152]{1,0:T(8,128)(2,1)S(1)}, bf16[64,1152]{1,0:T(8,128)(2,1)S(1)}, u32[]{:S(2)}, u32[]{:S(2)}) collective-permute-start(bf16[64,1152]{1,0:T(8,128)(2,1)S(1)} %fusion), channel_id=1, source_target_pairs={{0,8},{8,0},{16,24},{24,16},{32,40},{40,32},{48,56},{56,48},{64,72... | collective-permute-start | bytes 442376 | tf_op jit(solution)/shard_map/ppermute | solution.py:36
  (3 other events, 9.9 us)
